TPU v7x, 32 devices: a whole 2x2x4 slice. The times are simulated.
32 devices in a mesh: vol: 4 (over z), row: 4 (over y, core), col: 2 (over x).
Axes of the slice: x: 2, y: 2, z: 4, core: 2. Of those that a mesh axis runs over, the one named last changes fastest.
Arguments:
- vol_rhs: bfloat16 [64, 49152], P(None, ('vol', 'row', 'col')), may hold values from -6 to 6
- surf_rhs: bfloat16 [64, 4096], P(None, ('vol', 'row', 'col')), may hold values from -6 to 6
- vol_blocks: bfloat16 [384, 7, 128, 128], P(('vol', 'row', 'col')), may hold values from -0.1875 to 0.1875
- vol_cols: int32 [384, 7], P(('vol', 'row', 'col')), may hold values from 0 to 11, as said below
- coupling: bfloat16 [128, 128, 128], P(('vol', 'row', 'col')), may hold values from -0.5 to 0.5
- trace_map: int32 [128], P(('vol', 'row', 'col')), may hold values from 0 to 3
- bnd_count: int32 [32], P(('vol', 'row', 'col')), may hold values from 1 to 4
- surf_inverse: bfloat16 [32, 128, 128], P(('vol', 'row', 'col')), may hold values from -0.5 to 0.5
- near_blocks: bfloat16 [32, 2, 4, 128, 128], P(('vol', 'row'), 'col'), may hold values from -0.1875 to 0.1875
- near_cols: int32 [32, 2, 4], P(('vol', 'row'), 'col'), may hold values from 0 to 15
- far_u: bfloat16 [2, 32, 4096], P('col', None, ('vol', 'row')), may hold values from -1 to 1
- far_v: bfloat16 [16, 2, 32, 2048], P(('vol', 'row'), 'col'), may hold values from -0.125 to 0.125
Outputs:
- vol_field: float32 [64, 49152], P(None, ('vol', 'row', 'col'))
- surf_field: float32 [64, 4096], P(None, ('vol', 'row', 'col'))
Inputs may be any that keep to these rules, and one draw needn't show every extreme that they name: `vol_cols`: row b names 7 different blocks of its own subdomain, the first being b mod 12.
All inputs are finite; a program needn't handle non-finite values.
Results may differ from a plain program's by a relative error of at most 0.01.
Values may be sent and summed in bfloat16 or wider, within the bound.
No kernel may reach another device: no remote copies, remote signals or barrier semaphores. Data moves between devices by JAX's collectives and lax.ppermute only.
A program may use at most 64 MiB of HBM per device.

v0:
```python
import jax
import jax.numpy as jnp
from jax import lax
from jax.sharding import PartitionSpec as P

BS = 128
ITERS = 2


def volume_solve(field, blocks, columns):
    picked = jnp.take(field, columns, axis=1)
    return jnp.einsum("abnk,bnik->abi", picked, blocks, preferred_element_type=jnp.float32)


def surface_solve(field, blocks):
    return jnp.einsum("abk,bik->abi", field, blocks, preferred_element_type=jnp.float32)


def local(
    vol_rhs,
    surf_rhs,
    vol_blocks,
    vol_cols,
    coupling,
    trace_map,
    bnd_count,
    surf_inverse,
    near_blocks,
    near_cols,
    far_u,
    far_v,
):
    angles = vol_rhs.shape[0]
    vol_count = vol_blocks.shape[0]
    surf_count = surf_inverse.shape[0]
    slot_total = coupling.shape[0]
    piece_rows = surf_count * BS
    vol_size = lax.axis_size("vol")
    col_here = lax.axis_index("col")
    row_here = lax.axis_index("row")
    rhs_vol = vol_rhs.astype(jnp.float32).reshape(angles, vol_count, BS)
    rhs_surf = surf_rhs.astype(jnp.float32).reshape(angles, surf_count, BS)
    slot_alive = (jnp.arange(slot_total, dtype=jnp.int32) < bnd_count[0]).astype(jnp.float32)
    selector = (
        trace_map[:, None] == jnp.arange(vol_size * surf_count, dtype=jnp.int32)[None, :]
    ).astype(jnp.float32)
    near_local = near_blocks[:, 0]
    near_index = near_cols[:, 0]
    u_local = far_u[0]
    v_local = far_v[0, 0]
    padding = jnp.zeros((angles, vol_count - slot_total, BS), jnp.float32)
    volume = volume_solve(vol_rhs.reshape(angles, vol_count, BS), vol_blocks, vol_cols)
    surface = surface_solve(surf_rhs.reshape(angles, surf_count, BS), surf_inverse)
    for iteration in range(ITERS):
        x_half = volume.astype(jnp.bfloat16)
        s_half = surface.astype(jnp.bfloat16).reshape(angles, piece_rows)
        column_group = lax.all_gather(s_half, ("vol", "row"), axis=1, tiled=True)
        split_group = column_group.reshape(angles, vol_size, -1, piece_rows)
        group_surface = lax.dynamic_index_in_dim(split_group, row_here, 2, keepdims=False).reshape(
            angles, vol_size * piece_rows
        )
        picked = jnp.take(
            group_surface.reshape(angles, vol_size * surf_count, BS), trace_map, axis=1
        )
        current = (
            jnp.einsum("ajk,jik->aji", picked, coupling, preferred_element_type=jnp.float32)
            * slot_alive[None, :, None]
        )
        resid_vol = (rhs_vol - jnp.concatenate([current, padding], axis=1)).astype(jnp.bfloat16)
        contrib = (
            jnp.einsum(
                "aji,jik->jak", x_half[:, :slot_total], coupling, preferred_element_type=jnp.float32
            )
            * slot_alive[:, None, None]
        )
        traced = jnp.transpose(
            lax.psum_scatter(
                jnp.einsum("jm,jak->mak", selector, contrib), "vol", scatter_dimension=0, tiled=True
            ),
            (1, 0, 2),
        )
        column_blocks = column_group.reshape(angles, -1, BS)
        gathered = jnp.take(column_blocks, near_index, axis=1)
        near_term = jnp.einsum(
            "abnk,bnik->abi", gathered, near_local, preferred_element_type=jnp.float32
        )
        coeffs = jnp.einsum(
            "ak,qk->aq", column_group, v_local, preferred_element_type=jnp.float32
        ).astype(jnp.bfloat16)
        far_term = jnp.dot(coeffs, u_local, preferred_element_type=jnp.float32)
        row_partial = near_term.reshape(angles, -1) + far_term
        totals = lax.psum(row_partial, "col")
        integral = lax.dynamic_slice_in_dim(totals, col_here * piece_rows, piece_rows, 1)
        resid_surf = (rhs_surf - integral.reshape(angles, surf_count, BS) - traced).astype(
            jnp.bfloat16
        )
        volume = volume_solve(resid_vol, vol_blocks, vol_cols)
        surface = surface + surface_solve(resid_surf, surf_inverse)
    return (volume.reshape(angles, vol_count * BS), surface.reshape(angles, piece_rows))


def solution(mesh):
    in_specs = (
        P(None, ("vol", "row", "col")),
        P(None, ("vol", "row", "col")),
        P(("vol", "row", "col"), None, None, None),
        P(("vol", "row", "col"), None),
        P(("vol", "row", "col"), None, None),
        P(("vol", "row", "col")),
        P(("vol", "row", "col")),
        P(("vol", "row", "col"), None, None),
        P(("vol", "row"), "col", None, None, None),
        P(("vol", "row"), "col", None),
        P("col", None, ("vol", "row")),
        P(("vol", "row"), "col", None, None),
    )
    out_specs = (P(None, ("vol", "row", "col")), P(None, ("vol", "row", "col")))
    return jax.shard_map(local, mesh=mesh, in_specs=in_specs, out_specs=out_specs, check_vma=False)
```

profile of v0, /device:TPU:0, one launch (start us, length us, event | category | flops | bytes accessed | tf_op | source)
XLA Modules:
  0.0 128.1 jit_solution(11349936091575293454)
XLA Ops:
  8.0 0.0 copy-start
  8.0 0.0 copy-start.7
  8.0 0.0 all-reduce.5.cloned.1.call-start
  8.1 1.4 %compare_and_fusion.2 = pred[2,4]{1,0:T(4,128)(4,1)} fusion(s32[2,4]{1,0:T(2,128)} %bitcast.229), kind=kLoop, calls=%fused_computation.106 | loop fusion | flops 48 | bytes 40 | tf_op jit(solution)/shard_map/jit(_take)/and | solution.py:83
  9.5 0.7 compare_select_fusion.1
  10.1 0.1 reshape.188
  10.2 0.6 pad_clamp_fusion.2
  10.8 0.9 fusion.91
  11.7 23.8 %all-gather = bf16[64,1,2048]{2,0,1:T(8,128)(2,1)S(1)} all-gather(bf16[64,1,128]{2,0,1:T(8,128)(2,1)S(1)} %convert_bitcast_fusion.1), channel_id=2, replica_groups=mesh['vol'=4,'row'=4,'col'=2] {'vol','row'}, dimensions={2}, use_global_device_ids=true | all-gather | bytes 278528 | tf_op jit(solution)/shard_map/all_gather | solution.py:57
  35.6 0.1 copy.45
  35.6 1.3 %gather_fusion = bf16[8,64,128]{2,1,0:T(8,128)(2,1)} fusion(bf16[64,16,128]{2,0,1:T(8,128)(2,1)S(1)} %copy.45, s32[1024]{0:T(1024)} %pad_clamp_fusion.2), kind=kCustom, calls=%fused_computation.clone | custom fusion | bytes 262176 | tf_op jit(solution)/shard_map/jit(_take)/gather | solution.py:83
  37.0 1.2 convolution_bitcast_fusion.1
  38.2 1.9 %convolution_add_fusion.1 = f32[64,256]{1,0:T(8,128)} fusion(bf16[64,1,2048]{2,0,1:T(8,128)(2,1)S(1)} %all-gather, bf16[1,1,32,2048]{3,2,1,0:T(8,128)(2,1)} %param.29, f32[2,8,8,128]{3,2,1,0:T(8,128)S(1)} %convolution_bitcast_fusion.1, bf16[1,32,256]{2,1,0:T(8,128)(2,1)S(1)} %copy-done.7), kind=kOutput, calls=%fused_computation.35 | convolution fusion | flops 9455616 | bytes 540672 | tf_op jit(solution)/shard_map/dot_general | solution.py:90
  40.1 0.0 all-reduce.5.cloned.1.call-update
  40.1 0.0 reduce-scatter.3.cloned.1.call-start
  40.2 0.7 compare_and_fusion
  40.9 0.7 compare_select_fusion
  42.2 0.1 copy.43
  42.3 0.1 copy.48
  42.4 0.1 reshape.192
  42.5 1.0 copy_bitcast_fusion.1
  43.5 1.9 %gather_fusion.1 = bf16[84,64,128]{2,1,0:T(8,128)(2,1)} fusion(bf16[64,12,128]{2,0,1:T(8,128)(2,1)S(1)} %copy_bitcast_fusion.1, s32[1024]{0:T(1024)S(1)} %pad_clamp_fusion.1), kind=kCustom, calls=%fused_computation.1.clone | custom fusion | bytes 2752848 | tf_op jit(solution)/shard_map/jit(_take)/gather | solution.py:11
  45.4 1.7 %fusion.44 = bf16[4,64,128]{2,1,0:T(8,128)(2,1)S(1)} fusion(bf16[4,128,128]{2,1,0:T(8,128)(2,1)} %param.22, bf16[12,7,128,128]{3,2,1,0:T(8,128)(2,1)S(1)} %copy-done, bf16[12,7,64,128]{3,2,1,0:T(8,128)(2,1)} %bitcast.221, pred[12,7]{1,0:T(8,128)(4,1)S(1)} %copy.43, f32[4]{0:T(128)S(1)} %compare_convert_fusion), kind=kOutput, calls=%fused_computation.33 | convolution fusion | flops 185401344 | bytes 4325476 | tf_op jit(solution)/shard_map/aji,jik->jak/dot_general | solution.py:71
  47.1 0.2 fusion.71
  47.3 0.7 copy.51
  47.9 0.0 reduce-scatter.3.cloned.1.call-update
  48.0 0.0 all-reduce.7.cloned.1.call-start
  48.0 0.5 compare_and_fusion.1
  48.5 0.5 compare_select_fusion.2
  49.0 0.2 reshape.112
  49.2 0.1 constant_dynamic-slice_fusion
  49.4 0.6 pad_clamp_fusion
  50.0 0.6 gather_fusion.5
  50.6 1.8 %fusion.39 = f32[64,4,128]{2,0,1:T(8,128)} fusion(bf16[4,128,128]{2,1,0:T(8,128)(2,1)} %param.22, bf16[4,64,128]{2,1,0:T(8,128)(2,1)S(1)} %gather_fusion.5, f32[4]{0:T(128)S(1)} %compare_convert_fusion, pred[4]{0:T(512)(128)(4,1)} %compare_and_fusion.1), kind=kOutput, calls=%fused_computation.29 | convolution fusion | flops 8454144 | bytes 327700 | tf_op jit(solution)/shard_map/ajk,jik->aji/dot_general | solution.py:66
  52.4 5.9 %all-reduce.5.cloned.1.call-done = f32[64,256]{1,0:T(8,128)} async-done(((f32[64,256]{1,0:T(8,128)}), f32[64,256]{1,0:T(8,128)}) %all-reduce.5.cloned.1.call-update) | async-done | bytes 65552 | tf_op jit(solution)/shard_map/psum | solution.py:92
  58.3 6.1 %reduce-scatter.3.cloned.1.call-done = f32[1,64,128]{2,1,0:T(8,128)} async-done(((f32[4,64,128]{2,1,0:T(8,128)}), f32[1,64,128]{2,1,0:T(8,128)}) %reduce-scatter.3.cloned.1.call-update) | async-done | bytes 32784 | tf_op jit(solution)/shard_map/reduce_scatter | solution.py:77
  64.5 1.0 fusion.49
  65.4 19.3 %all-gather.1 = bf16[64,1,2048]{2,0,1:T(8,128)(2,1)S(1)} all-gather(bf16[64,1,128]{2,0,1:T(8,128)(2,1)S(1)} %convert_bitcast_fusion), channel_id=3, replica_groups=mesh['vol'=4,'row'=4,'col'=2] {'vol','row'}, dimensions={2}, use_global_device_ids=true | all-gather | bytes 278528 | tf_op jit(solution)/shard_map/all_gather | solution.py:57
  84.8 0.9 reshape.108
  85.7 0.0 copy-start.2
  85.7 0.8 copy.55
  86.5 2.3 %gather_fusion.4 = bf16[8,64,128]{2,1,0:T(8,128)(2,1)} fusion(bf16[64,16,128]{2,0,1:T(8,128)(2,1)} %copy.55, s32[1024]{0:T(1024)} %pad_clamp_fusion.2), kind=kCustom, calls=%fused_computation.3.clone | custom fusion | bytes 262176 | tf_op jit(solution)/shard_map/jit(_take)/gather | solution.py:83
  88.7 1.8 %convolution_bitcast_fusion = f32[2,8,8,128]{3,2,1,0:T(8,128)} fusion(bf16[2,1,4,128,128]{4,3,2,1,0:T(8,128)(2,1)S(1)} %copy-done.1, bf16[2,4,64,128]{3,2,1,0:T(8,128)(2,1)} %bitcast.224, pred[2,4]{1,0:T(4,128)(4,1)} %compare_and_fusion.2), kind=kOutput, calls=%fused_computation.36 | convolution fusion | flops 16842752 | bytes 458760 | tf_op jit(solution)/shard_map/abnk,bnik->abi/dot_general | solution.py:84
  90.5 1.9 %convolution_add_fusion = f32[64,256]{1,0:T(8,128)} fusion(bf16[64,1,2048]{2,0,1:T(8,128)(2,1)S(1)} %all-gather.1, bf16[1,1,32,2048]{3,2,1,0:T(8,128)(2,1)} %param.29, f32[2,8,8,128]{3,2,1,0:T(8,128)} %convolution_bitcast_fusion, bf16[1,32,256]{2,1,0:T(8,128)(2,1)S(1)} %copy-done.8), kind=kOutput, calls=%fused_computation.34 | convolution fusion | flops 9455616 | bytes 540672 | tf_op jit(solution)/shard_map/dot_general | solution.py:90
  92.5 1.1 constant_dynamic-slice_fusion.1
  93.6 0.6 gather_fusion.2
  94.1 0.0 all-reduce.7.cloned.1.call-update
  94.2 0.0 reduce-scatter.5.cloned.1.call-start
  94.2 1.1 fusion.40
  95.4 1.0 fusion.56
  96.4 0.0 copy-start.3
  96.4 1.9 %gather_fusion.6 = bf16[84,64,128]{2,1,0:T(8,128)(2,1)} fusion(bf16[64,12,128]{2,0,1:T(8,128)(2,1)S(1)} %get-tuple-element.4, s32[1024]{0:T(1024)S(1)} %pad_clamp_fusion.1), kind=kCustom, calls=%fused_computation.5.clone | custom fusion | bytes 2752848 | tf_op jit(solution)/shard_map/jit(_take)/gather | solution.py:11
  98.3 1.6 %fusion.41 = bf16[4,64,128]{2,1,0:T(8,128)(2,1)S(1)} fusion(bf16[4,128,128]{2,1,0:T(8,128)(2,1)S(1)} %copy-done.3, bf16[12,7,128,128]{3,2,1,0:T(8,128)(2,1)S(1)} %copy-done, bf16[12,7,64,128]{3,2,1,0:T(8,128)(2,1)} %bitcast.220, pred[12,7]{1,0:T(8,128)(4,1)S(1)} %copy-done.12, f32[4]{0:T(128)S(1)} %compare_convert_fusion), kind=kOutput, calls=%fused_computation.32 | convolution fusion | flops 185401344 | bytes 4325476 | tf_op jit(solution)/shard_map/aji,jik->jak/dot_general | solution.py:71
  99.9 0.2 fusion.69
  100.1 0.7 copy.61
  100.8 1.9 %gather_fusion.3 = bf16[84,64,128]{2,1,0:T(8,128)(2,1)} fusion(bf16[64,12,128]{2,0,1:T(8,128)(2,1)S(1)} %get-tuple-element.6, s32[1024]{0:T(1024)S(1)} %pad_clamp_fusion.1), kind=kCustom, calls=%fused_computation.4.clone | custom fusion | bytes 2752848 | tf_op jit(solution)/shard_map/jit(_take)/gather | solution.py:11
  102.7 0.0 reduce-scatter.5.cloned.1.call-update
  102.7 0.0 copy-start.5
  102.7 0.0 copy-start.6
  102.7 2.6 %fusion.15 = f32[12,8,8,128]{3,2,1,0:T(8,128)S(1)} fusion(bf16[12,7,128,128]{3,2,1,0:T(8,128)(2,1)S(1)} %copy-done, bf16[12,7,64,128]{3,2,1,0:T(8,128)(2,1)} %bitcast.219, pred[12,7]{1,0:T(8,128)(4,1)S(1)} %copy-done.12), kind=kOutput, calls=%fused_computation.20 | convolution fusion | flops 176848896 | bytes 4522068 | tf_op jit(solution)/shard_map/abnk,bnik->abi/dot_general | solution.py:12
  105.3 0.8 copy.89
  106.1 6.3 %all-reduce.7.cloned.1.call-done = f32[64,256]{1,0:T(8,128)} async-done(((f32[64,256]{1,0:T(8,128)}), f32[64,256]{1,0:T(8,128)}) %all-reduce.7.cloned.1.call-update) | async-done | bytes 65552 | tf_op jit(solution)/shard_map/psum | solution.py:92
  112.4 6.8 %reduce-scatter.5.cloned.1.call-done = f32[1,64,128]{2,1,0:T(8,128)} async-done(((f32[4,64,128]{2,1,0:T(8,128)}), f32[1,64,128]{2,1,0:T(8,128)}) %reduce-scatter.5.cloned.1.call-update) | async-done | bytes 32784 | tf_op jit(solution)/shard_map/reduce_scatter | solution.py:77
  119.2 1.5 %fusion.48 = f32[64,128]{1,0:T(8,128)} fusion(f32[128,64]{0,1:T(8,128)S(1)} %fusion.49, bf16[1,128,128]{2,1,0:T(8,128)(2,1)S(1)} %copy-done.5, bf16[64,128]{1,0:T(8,128)(2,1)S(1)} %copy-done.6, f32[1,64,128]{2,1,0:T(8,128)} %reduce-scatter.5.cloned.1.call-done, f32[64,256]{1,0:T(8,128)} %all-reduce.7.cloned.1.call-done, s32[]{:T(128)S(6)} %select_n.30), kind=kOutput, calls=%fused_computation.40 | convolution fusion | flops 2138112 | bytes 180228 | tf_op jit(solution)/shard_map/abk,bik->abi/dot_general | solution.py:16
  (28 shorter events, 0.2 us)
Async XLA Ops:
  8.0 37.4 %copy-start = (bf16[12,7,128,128]{3,2,1,0:T(8,128)(2,1)S(1)}, bf16[12,7,128,128]{3,2,1,0:T(8,128)(2,1)}, u32[]{:S(2)}) copy-start(bf16[12,7,128,128]{3,2,1,0:T(8,128)(2,1)} %param.20) | copy-start | bytes 8257540
  8.0 29.0 %copy-start.1 = (bf16[2,1,4,128,128]{4,3,2,1,0:T(8,128)(2,1)S(1)}, bf16[2,1,4,128,128]{4,3,2,1,0:T(8,128)(2,1)}, u32[]{:S(2)}) copy-start(bf16[2,1,4,128,128]{4,3,2,1,0:T(8,128)(2,1)} %param.26) | copy-start | bytes 786436
  8.0 30.1 %copy-start.7 = (bf16[1,32,256]{2,1,0:T(8,128)(2,1)S(1)}, bf16[1,32,256]{2,1,0:T(8,128)(2,1)}, u32[]{:S(2)}) copy-start(bf16[1,32,256]{2,1,0:T(8,128)(2,1)} %param.28) | copy-start | bytes 49156
  8.0 50.3 %all-reduce.5.cloned.1.call-start = ((), (), s32[]{:S(2)}) async-start(), calls=%async_computation.2 | async-start | bytes 131072 | tf_op jit(solution)/shard_map/psum | solution.py:92
  11.7 23.8 %copy-start.4 = (f32[128,64]{0,1:T(8,128)}, f32[128,64]{0,1:T(8,128)S(1)}, u32[]{:S(2)}) copy-start(f32[128,64]{0,1:T(8,128)S(1)} %fusion.91) | copy-start | bytes 98308
  40.1 24.4 %reduce-scatter.3.cloned.1.call-start = ((), (), s32[]{:S(2)}) async-start(), calls=%async_computation.3 | async-start | bytes 163840 | tf_op jit(solution)/shard_map/reduce_scatter | solution.py:77
  42.3 3.1 %copy-start.11 = (pred[12,7]{1,0:T(8,128)(4,1)}, pred[12,7]{1,0:T(8,128)(4,1)S(1)}, u32[]{:S(2)}) copy-start(pred[12,7]{1,0:T(8,128)(4,1)S(1)} %copy.43) | copy-start | bytes 256
  45.4 1.7 %copy-start.9 = (s32[4]{0:T(128)S(1)}, s32[4]{0:T(128)}, u32[]{:S(2)}) copy-start(s32[4]{0:T(128)} %param.23) | copy-start | bytes 52
  48.0 64.4 %all-reduce.7.cloned.1.call-start = ((), (), s32[]{:S(2)}) async-start(), calls=%async_computation.4 | async-start | bytes 131072 | tf_op jit(solution)/shard_map/psum | solution.py:92
  52.4 38.1 %copy-start.8 = (bf16[1,32,256]{2,1,0:T(8,128)(2,1)S(1)}, bf16[1,32,256]{2,1,0:T(8,128)(2,1)}, u32[]{:S(2)}) copy-start(bf16[1,32,256]{2,1,0:T(8,128)(2,1)} %param.28) | copy-start | bytes 49156
  85.6 8.6 %copy-start.10 = (pred[4]{0:T(512)(128)(4,1)S(1)}, pred[4]{0:T(512)(128)(4,1)}, u32[]{:S(2)}) copy-start(pred[4]{0:T(512)(128)(4,1)} %compare_and_fusion.1) | copy-start | bytes 16
  85.7 9.7 %copy-start.2 = (bf16[64,1536]{1,0:T(8,128)(2,1)S(1)}, bf16[64,1536]{1,0:T(8,128)(2,1)}, u32[]{:S(2)}) copy-start(bf16[64,1536]{1,0:T(8,128)(2,1)} %param.18) | copy-start | bytes 589828
  94.2 25.0 %reduce-scatter.5.cloned.1.call-start = ((), (), s32[]{:S(2)}) async-start(), calls=%async_computation.5 | async-start | bytes 163840 | tf_op jit(solution)/shard_map/reduce_scatter | solution.py:77
  96.4 1.9 %copy-start.3 = (bf16[4,128,128]{2,1,0:T(8,128)(2,1)S(1)}, bf16[4,128,128]{2,1,0:T(8,128)(2,1)}, u32[]{:S(2)}) copy-start(bf16[4,128,128]{2,1,0:T(8,128)(2,1)} %param.22) | copy-start | bytes 393220
  96.4 1.9 %copy-start.12 = (pred[12,7]{1,0:T(8,128)(4,1)S(1)}, pred[12,7]{1,0:T(8,128)(4,1)}, u32[]{:S(2)}) copy-start(pred[12,7]{1,0:T(8,128)(4,1)} %copy-done.11) | copy-start | bytes 256
  102.7 16.5 %copy-start.5 = (bf16[1,128,128]{2,1,0:T(8,128)(2,1)S(1)}, bf16[1,128,128]{2,1,0:T(8,128)(2,1)}, u32[]{:S(2)}) copy-start(bf16[1,128,128]{2,1,0:T(8,128)(2,1)} %param.25) | copy-start | bytes 98308
  102.7 16.5 %copy-start.6 = (bf16[64,128]{1,0:T(8,128)(2,1)S(1)}, bf16[64,128]{1,0:T(8,128)(2,1)}, u32[]{:S(2)}) copy-start(bf16[64,128]{1,0:T(8,128)(2,1)} %param.19) | copy-start | bytes 49156
Sparse Core Ops, SparseCore 0:
  40.2 18.0 all-reduce.4
  94.3 18.0 all-reduce.6
Sparse Core Ops, SparseCore 1:
  48.0 16.4 reduce-scatter.2
  102.8 16.3 reduce-scatter.4
where the time goes:
time: 129 us; the launch traced here: 128 us
  blocking collectives  43.1 us (33%)
  waiting for transfers between devices  25.2 us (20%)
  matrix products  19.3 us (15%)
  local copies, waits for them, and re-layouts  17.2 us (13%)
  between operations  16.4 us (13%)
  other arithmetic  6.73 us (5%)
    all_gather x2, blocking collectives, local(): column_group = lax.all_gather(s_half, ('vol', 'row'), axis=1, tiled=True)  43.1 us
    reduce_scatter x2, waiting for transfers between devices, local(): lax.psum_scatter(jnp.einsum('jm,jak->mak', selector, contrib), 'vol', sca...  12.9 us
    psum x2, waiting for transfers between devices, local(): totals = lax.psum(row_partial, 'col')  12.2 us
    gather x3, local copies, waits for them, and re-layouts, volume_solve(): picked = jnp.take(field, columns, axis=1)  5.72 us
    dot_general x2, matrix products, local(): far_term = jnp.dot(coeffs, u_local, preferred_element_type=jnp.float32)  3.86 us
    gather x2, local copies, waits for them, and re-layouts, local(): gathered = jnp.take(column_blocks, near_index, axis=1)  3.62 us
    dot_general x3, matrix products, surface_solve(): jnp.einsum('abk,bik->abi', field, blocks, preferred_element_type=jnp.floa...  3.38 us
    dot_general x2, matrix products, local(): jnp.einsum('aji,jik->jak', x_half[:, :slot_total], coupling, preferred_el...  3.32 us
  transfers between devices with their start and end apart: 4, of which 4 were waited for; matrix products, arithmetic and copies ran while one was open for 18% of the time, Pallas kernels for 0%

commit v1 on v0

v1 whole, which is shorter than its diff:
```python
import functools

import jax
import jax.numpy as jnp
from jax import lax
from jax.experimental import pallas as pl
from jax.experimental.pallas import tpu as pltpu
from jax.sharding import PartitionSpec as P

ITERS = 2
UNROLL = 16
F32 = jnp.float32
HALF = jnp.bfloat16


def by_rows(a, b):
    return lax.dot_general(a, b, (((1,), (1,)), ((), ())), preferred_element_type=F32)


def by_cols(a, b):
    return lax.dot_general(a, b, (((1,), (0,)), ((), ())), preferred_element_type=F32)


def block(start, size):
    return pl.ds(pl.multiple_of(start * size, size), size)


def slot_of(index, here, count):
    return lax.rem(index - here + count, count)


def block_row(read, blocks, columns, row):
    terms = blocks.shape[1]
    field = jnp.concatenate([read(columns[row, n]) for n in range(terms)], axis=1)
    inverse = jnp.concatenate([blocks[row, n] for n in range(terms)], axis=1)
    return by_rows(field, inverse)


def add_traces(total, boundary, coupling, trace_map, bnd_count, axis):
    count = total.shape[0]
    bs = coupling.shape[-1]
    subs = total.shape[2] // bs
    here = lax.axis_index(axis)
    for j in range(coupling.shape[0]):
        alive = (j < bnd_count[0]).astype(F32)
        contrib = by_cols(boundary(j), coupling[j]) * alive
        target = trace_map[j]
        slot = slot_of(target // subs, here, count)
        where = (slot, slice(None), block(lax.rem(target, subs), bs))
        total[where] = total[where] + contrib


def residual_blocks(resid, vol_rhs, group, coupling, trace_map, bnd_count, axis, count):
    bs = coupling.shape[-1]
    angles = vol_rhs.shape[0]
    subs = group.shape[1] // bs
    here = lax.axis_index(axis)
    for j in range(coupling.shape[0]):
        alive = (j < bnd_count[0]).astype(F32)
        target = trace_map[j]
        slot = slot_of(here, target // subs, count)
        picked = group[block(slot, angles), block(lax.rem(target, subs), bs)]
        current = by_rows(picked, coupling[j]) * alive
        rhs = vol_rhs[:, j * bs : (j + 1) * bs].astype(F32)
        resid[j] = (rhs - current).astype(HALF)


def send_out(payloads, half, total):
    angles = half.shape[0]
    for k, payload in enumerate(payloads):
        payload[0:angles, :] = half
        payload[angles : 2 * angles, :] = total[k + 1].astype(HALF)


def start_kernel(axis, refs):
    (surf_rhs, surf_inverse, vol_rhs, blocks, coupling, columns, trace_map, bnd_count) = refs[:8]
    surface, half_out, own_trace = refs[8:11]
    payloads, total = refs[11:-1], refs[-1]
    bs = coupling.shape[-1]
    for b in range(surf_inverse.shape[0]):
        cols = slice(b * bs, (b + 1) * bs)
        surface[:, cols] = by_rows(surf_rhs[:, cols], surf_inverse[b])
    half = surface[...].astype(HALF)
    half_out[...] = half
    total[...] = jnp.zeros_like(total)

    def read(col):
        return vol_rhs[:, block(col, bs)]

    def boundary(j):
        return block_row(read, blocks, columns, j).astype(HALF)

    add_traces(total, boundary, coupling, trace_map, bnd_count, axis)
    own_trace[...] = total[0]
    send_out(payloads, half, total)


def boundary_kernel(axis, refs):
    (group, vol_rhs, blocks, coupling, columns, trace_map, bnd_count, total, field) = refs
    bs = coupling.shape[-1]
    slots = coupling.shape[0]
    count = total.shape[0]
    for b in range(slots, vol_rhs.shape[1] // bs):
        field[b] = vol_rhs[:, b * bs : (b + 1) * bs]
    residual_blocks(field, vol_rhs, group, coupling, trace_map, bnd_count, axis, count)
    total[...] = jnp.zeros_like(total)

    def boundary(j):
        return block_row(lambda col: field[col], blocks, columns, j).astype(HALF)

    add_traces(total, boundary, coupling, trace_map, bnd_count, axis)


def volume_kernel(axis, count, refs):
    (group, vol_rhs, blocks, coupling, columns, trace_map, bnd_count, volume, field) = refs
    bs = coupling.shape[-1]
    for b in range(coupling.shape[0], vol_rhs.shape[1] // bs):
        field[b] = vol_rhs[:, b * bs : (b + 1) * bs]
    residual_blocks(field, vol_rhs, group, coupling, trace_map, bnd_count, axis, count)
    for b in range(blocks.shape[0]):
        volume[:, b * bs : (b + 1) * bs] = block_row(lambda col: field[col], blocks, columns, b)


def dense_kernel(vol_size, row_size, col_size, refs):
    near_blocks, near_cols, far_u, far_v, dense, work = refs
    bs = near_blocks.shape[-1]
    rows = near_blocks.shape[0]
    subs = rows // col_size
    vol, row, col = (lax.axis_index(name) for name in ("vol", "row", "col"))

    def place(number):
        piece = number // subs
        row_slot = slot_of(row, lax.rem(piece, row_size), row_size)
        vol_slot = slot_of(vol, piece // row_size, vol_size)
        return (row_slot * vol_size + vol_slot) * subs + lax.rem(number, subs)

    total = vol_size * row_size * subs
    for k in range(col_size):
        piece = lax.rem(col + k, col_size)
        for sub in range(subs):
            b = piece * subs + sub
            u = far_u[0, :, block(b, bs)]

            def far(number, _):
                v = far_v[0, 0, :, block(number, bs)]
                work[block(place(number), bs), :] = lax.dot_general(
                    v, u, (((0,), (0,)), ((), ())), preferred_element_type=F32
                )
                return _

            lax.fori_loop(0, total, far, 0, unroll=min(total, UNROLL))
            for n in range(near_blocks.shape[2]):
                where = (block(place(near_cols[b, 0, n]), bs), slice(None))
                work[where] = work[where] + near_blocks[b, 0, n].astype(F32).T
            at = (k * subs + sub) * bs
            dense[:, at : at + bs] = work[...].astype(HALF)


def integral_kernel(row_size, vol_size, refs):
    groups, dense, outs = refs[:row_size], refs[row_size], refs[row_size + 1 :]
    angles, width = groups[0].shape[0] // vol_size, groups[0].shape[1]
    field = jnp.concatenate(
        [g[k * angles : (k + 1) * angles, :] for g in groups for k in range(vol_size)], axis=1
    )
    part = by_cols(field, dense[...])
    for k, out in enumerate(outs):
        out[...] = part[:, k * width : (k + 1) * width].astype(out.dtype)


def update_surface(surface, surf_rhs, surf_inverse, integral, traces, sums, received, out):
    bs = surf_inverse.shape[-1]
    angles = surf_rhs.shape[0]
    taken = integral[...] + traces
    for s in sums:
        taken = taken + s[...].astype(F32)
    for r in received:
        taken = taken + r[angles : 2 * angles, :].astype(F32)
    resid = (surf_rhs[...].astype(F32) - taken).astype(HALF)
    for b in range(surf_inverse.shape[0]):
        cols = slice(b * bs, (b + 1) * bs)
        out[:, cols] = surface[:, cols] + by_rows(resid[:, cols], surf_inverse[b])


def step_kernel(sums, received, refs):
    surface, surf_rhs, surf_inverse, integral, own_trace, total = refs[:6]
    sums, refs = refs[6 : 6 + sums], refs[6 + sums :]
    received, refs = refs[:received], refs[received:]
    out, half_out, next_trace = refs[:3]
    payloads = refs[3:]
    update_surface(
        surface, surf_rhs, surf_inverse, integral, own_trace[...], sums, received, out
    )
    half = out[...].astype(HALF)
    half_out[...] = half
    next_trace[...] = total[0]
    send_out(payloads, half, total)


def last_kernel(sums, received, refs):
    surface, surf_rhs, surf_inverse, integral, own_trace = refs[:5]
    out = refs[-1]
    sums, received = refs[5 : 5 + sums], refs[5 + sums : 5 + sums + received]
    update_surface(
        surface, surf_rhs, surf_inverse, integral, own_trace[...], sums, received, out
    )


VMEM = pl.BlockSpec(memory_space=pltpu.VMEM)
SMEM = pl.BlockSpec(memory_space=pltpu.SMEM)


def call(body, name, in_specs, outs, flops, moved, scratch=()):
    def kernel(*refs):
        body(refs)

    return pl.pallas_call(
        kernel,
        name=name,
        out_shape=outs,
        in_specs=in_specs,
        out_specs=[VMEM] * len(outs),
        scratch_shapes=list(scratch),
        cost_estimate=pl.CostEstimate(flops=flops, bytes_accessed=moved, transcendentals=0),
        compiler_params=pltpu.CompilerParams(vmem_limit_bytes=48 << 20),
    )


def shifted(value, axis, shift):
    size = lax.axis_size(axis)
    return lax.ppermute(value, axis, [(i, (i + shift) % size) for i in range(size)])


def local(
    vol_rhs,
    surf_rhs,
    vol_blocks,
    vol_cols,
    coupling,
    trace_map,
    bnd_count,
    surf_inverse,
    near_blocks,
    near_cols,
    far_u,
    far_v,
):
    angles, width = surf_rhs.shape
    vol_count, terms, bs, _ = vol_blocks.shape
    slots = coupling.shape[0]
    nv, nr, nc = (lax.axis_size(a) for a in ("vol", "row", "col"))
    piece = (angles, width)
    product = 2 * angles * bs * bs

    def shape(dims, dtype):
        return jax.ShapeDtypeStruct(dims, dtype)

    boundary_blocks = vol_blocks[:slots]
    tables = (vol_cols, trace_map, bnd_count)
    payload_shapes = [shape((2 * angles, width), HALF)] * (nv - 1)
    totals = pltpu.VMEM((nv,) + piece, F32)
    field = pltpu.VMEM((vol_count, angles, bs), HALF)

    surface, half, own_trace, *payloads = call(
        functools.partial(start_kernel, "vol"),
        "start",
        [VMEM] * 3 + [VMEM] * 2 + [SMEM] * 3,
        [shape(piece, F32), shape(piece, HALF), shape(piece, F32)] + payload_shapes,
        product * slots * (terms + 1),
        2 * bs * bs * slots * (terms + 1),
        [totals],
    )(surf_rhs, surf_inverse, vol_rhs, boundary_blocks, coupling, *tables)

    (dense,) = call(
        functools.partial(dense_kernel, nv, nr, nc),
        "dense",
        [VMEM, SMEM, VMEM, VMEM],
        [shape((nv * nr * width, nc * width), HALF)],
        product * nv * nr * nc,
        4 * nv * nr * nc * bs * bs,
        [pltpu.VMEM((nv * nr * width, bs), F32)],
    )(near_blocks, near_cols, far_u, far_v)

    for iteration in range(ITERS):
        received = [shifted(payloads[k - 1], "vol", k) for k in range(1, nv)]
        group = jnp.concatenate([half] + [r[:angles] for r in received], axis=0)
        groups = [group] + [shifted(group, "row", k) for k in range(1, nr)]
        last = iteration == ITERS - 1
        if last:
            (volume,) = call(
                functools.partial(volume_kernel, "vol", nv),
                "volume",
                [VMEM] * 4 + [SMEM] * 3,
                [shape((angles, vol_count * bs), F32)],
                product * vol_count * terms,
                2 * bs * bs * vol_count * terms,
                [field],
            )(group, vol_rhs, vol_blocks, coupling, *tables)
        else:
            (total,) = call(
                functools.partial(boundary_kernel, "vol"),
                "boundary",
                [VMEM] * 2 + [VMEM] * 2 + [SMEM] * 3,
                [shape((nv,) + piece, F32)],
                product * slots * (terms + 2),
                2 * bs * bs * slots * (terms + 1),
                [field],
            )(group, vol_rhs, boundary_blocks, coupling, *tables)
        integral, *parts = call(
            functools.partial(integral_kernel, nr, nv),
            "integral",
            [VMEM] * (nr + 1),
            [shape(piece, F32)] + [shape(piece, HALF)] * (nc - 1),
            product * nv * nr * nc,
            2 * nv * nr * nc * width * width,
        )(*groups, dense)
        sums = [shifted(parts[k - 1], "col", k) for k in range(1, nc)]
        if last:
            (surface,) = call(
                functools.partial(last_kernel, nc - 1, nv - 1),
                "last",
                [VMEM] * (5 + nc - 1 + nv - 1),
                [shape(piece, F32)],
                product,
                1 << 17,
            )(surface, surf_rhs, surf_inverse, integral, own_trace, *sums, *received)
        else:
            surface, half, own_trace, *payloads = call(
                functools.partial(step_kernel, nc - 1, nv - 1),
                "step",
                [VMEM] * (6 + nc - 1 + nv - 1),
                [shape(piece, F32), shape(piece, HALF), shape(piece, F32)] + payload_shapes,
                product,
                1 << 17,
            )(surface, surf_rhs, surf_inverse, integral, own_trace, total, *sums, *received)
    return volume, surface


def solution(mesh):
    everywhere = ("vol", "row", "col")
    in_specs = (
        P(None, everywhere),
        P(None, everywhere),
        P(everywhere, None, None, None),
        P(everywhere, None),
        P(everywhere, None, None),
        P(everywhere),
        P(everywhere),
        P(everywhere, None, None),
        P(("vol", "row"), "col", None, None, None),
        P(("vol", "row"), "col", None),
        P("col", None, ("vol", "row")),
        P(("vol", "row"), "col", None, None),
    )
    out_specs = (P(None, everywhere), P(None, everywhere))
    return jax.shard_map(local, mesh=mesh, in_specs=in_specs, out_specs=out_specs, check_vma=False)
```

time: 129 us -> 47.6 us (0.37)
  blocking collectives: 43.1 us -> 0 us
  matrix products: 19.3 us -> 0 us
  starting transfers between devices: 0.17 us -> 16.9 us
  between operations: 16.4 us -> 1.5 us
  waiting for transfers between devices: 25.2 us -> 13.6 us
  local copies, waits for them, and re-layouts: 17.2 us -> 6.07 us
  Pallas kernels: 0 us -> 9.09 us
  other arithmetic: 6.73 us -> 0.01 us
    all_gather x2 -> x0, blocking collectives: 43.1 us -> none  [local(): column_group = lax.all_gather(s_half, ('vol', 'row'), axis=1, tiled=True)]
    dot_general x14 -> x0, matrix products: 19.3 us -> none  [the longest x2 3.86 us: local(): far_term = jnp.dot(coeffs, u_local, preferred_element_type=jnp.float32)]
    ppermute x0 -> x14, starting transfers between devices: none -> 16.9 us  [shifted(): lax.ppermute(value, axis, [(i, (i + shift) % size) for i in range(size)])]
    ppermute x0 -> x14, waiting for transfers between devices: none -> 13.6 us  [shifted(): lax.ppermute(value, axis, [(i, (i + shift) % size) for i in range(size)])]
    reduce_scatter x2 -> x0, waiting for transfers between devices: 12.9 us -> none  [local(): lax.psum_scatter(jnp.einsum('jm,jak->mak', selector, contrib), 'vol', sca...]
    psum x2 -> x0, waiting for transfers between devices: 12.2 us -> none  [local(): totals = lax.psum(row_partial, 'col')]
    gather x7 -> x0, local copies, waits for them, and re-layouts: 10.5 us -> none  [the longest x3 5.72 us: volume_solve(): picked = jnp.take(field, columns, axis=1)]
    pallas_call x0 -> x8, Pallas kernels: none -> 9.09 us  [the longest x1 2.77 us: local(): call(functools.partial(volume_kernel, 'vol', nv), 'volume', [VMEM] * 4 +...]
  transfers between devices with their start and end apart: 4 -> 14, of which waited for: 4 -> 11; matrix products, arithmetic and copies ran while one was open for 18% -> 0% of each run, Pallas kernels for 0% -> 13%
where the time goes in v1:
time: 47.6 us; the launch traced here: 47.2 us
  starting transfers between devices  16.9 us (36%)
  waiting for transfers between devices  13.6 us (29%)
  Pallas kernels  9.09 us (19%)
  local copies, waits for them, and re-layouts  6.07 us (13%)
  between operations  1.5 us (3%)
    ppermute x14, starting transfers between devices, shifted(): lax.ppermute(value, axis, [(i, (i + shift) % size) for i in range(size)])  16.9 us
    ppermute x14, waiting for transfers between devices, shifted(): lax.ppermute(value, axis, [(i, (i + shift) % size) for i in range(size)])  13.6 us
    unnamed x29, local copies, waits for them, and re-layouts  4.77 us
    pallas_call x1, Pallas kernels, local(): call(functools.partial(volume_kernel, 'vol', nv), 'volume', [VMEM] * 4 +...  2.77 us
    pallas_call x1, Pallas kernels, local(): call(functools.partial(boundary_kernel, 'vol'), 'boundary', [VMEM] * 2 +...  1.88 us
    pallas_call x1, Pallas kernels, local(): call(functools.partial(start_kernel, 'vol'), 'start', [VMEM] * 3 + [VMEM]...  1.65 us
    slice x1, local copies, waits for them, and re-layouts, local(): boundary_blocks = vol_blocks[:slots]  1.29 us
    pallas_call x1, Pallas kernels, local(): call(functools.partial(dense_kernel, nv, nr, nc), 'dense', [VMEM, SMEM, V...  1.26 us
  transfers between devices with their start and end apart: 14, of which 11 were waited for; matrix products, arithmetic and copies ran while one was open for 0% of the time, Pallas kernels for 13%

profile of v1, /device:TPU:0, one launch (start us, length us, event | category | flops | bytes accessed | tf_op | source)
XLA Modules:
  0.0 47.2 jit_solution(4263595938850262190)
XLA Ops:
  0.6 0.0 copy-start.9
  0.6 0.0 copy-start.10
  0.7 0.0 copy-start.13
  0.7 0.0 copy-start.7
  1.4 0.8 %copy.14.refs_5_.refs_4_ = s32[12,7]{1,0:T(8,128)S(1)} copy(s32[12,7]{0,1:T(8,128)} %param.15) | data formatting | bytes 672 | tf_op args[3]
  2.2 0.0 copy-start.2
  2.2 0.0 copy-start.4
  2.2 1.3 %slice.21.refs_3_.refs_2_ = bf16[4,7,128,128]{3,2,1,0:T(8,128)(2,1)S(1)} slice(bf16[12,7,128,128]{3,2,1,0:T(8,128)(2,1)} %refs_2_.8), slice={[0:4], [0:7], [0:128], [0:128]} | slice | bytes 1835008 | tf_op jit(solution)/shard_map/slice | solution.py:257
  3.5 0.0 copy-start.1
  3.5 0.9 %copy-done.1 = bf16[64,1536]{1,0:T(8,128)(2,1)S(1)} copy-done((bf16[64,1536]{1,0:T(8,128)(2,1)S(1)}, bf16[64,1536]{1,0:T(8,128)(2,1)}, u32[]{:S(2)}) %copy-start.1) | copy-done | bytes 196632
  4.4 0.0 copy-start.3
  4.4 0.9 %copy-done.3 = bf16[4,128,128]{2,1,0:T(8,128)(2,1)S(1)} copy-done((bf16[4,128,128]{2,1,0:T(8,128)(2,1)S(1)}, bf16[4,128,128]{2,1,0:T(8,128)(2,1)}, u32[]{:S(2)}) %copy-start.3) | copy-done | bytes 131096
  5.3 0.0 copy-start.5
  5.3 0.8 %copy-done.5 = bf16[1,128,128]{2,1,0:T(8,128)(2,1)S(1)} copy-done((bf16[1,128,128]{2,1,0:T(8,128)(2,1)S(1)}, bf16[1,128,128]{2,1,0:T(8,128)(2,1)}, u32[]{:S(2)}) %copy-start.5) | copy-done | bytes 32792
  6.0 0.0 copy-start.8
  6.0 0.7 %copy-done.8 = bf16[64,128]{1,0:T(8,128)(2,1)S(1)} copy-done((bf16[64,128]{1,0:T(8,128)(2,1)S(1)}, bf16[64,128]{1,0:T(8,128)(2,1)}, u32[]{:S(2)}) %copy-start.8) | copy-done | bytes 16408
  6.8 0.7 %copy-done.11 = s32[4]{0:T(128)S(1)} copy-done((s32[4]{0:T(128)S(1)}, s32[4]{0:T(128)}, u32[]{:S(2)}) %copy-start.11) | copy-done | bytes 40
  7.4 1.7 %start.1 = (f32[64,128]{1,0:T(8,128)S(1)}, bf16[64,128]{1,0:T(8,128)(2,1)S(1)}, f32[64,128]{1,0:T(8,128)S(1)}, bf16[128,128]{1,0:T(8,128)(2,1)S(1)}, bf16[128,12...) custom-call(bf16[64,128]{1,0:T(8,128)(2,1)S(1)} %copy-done.8, bf16[1,128,128]{2,1,0:T(8,128)(2,1)S(1)} %copy-done.5, ...), custom_call_target="tpu_custom_call" | custom-call | flops 67108864 | bytes 1048576 | tf_op jit(solution)/shard_map/start/pallas_call | solution.py:263
  9.1 3.1 %collective-permute-start = (bf16[128,128]{1,0:T(8,128)(2,1)S(1)}, bf16[128,128]{1,0:T(8,128)(2,1)S(1)}, u32[]{:S(2)}, u32[]{:S(2)}) collective-permute-start(bf16[128,128]{1,0:T(8,128)(2,1)S(1)} %get-tuple-element.20), channel_id=1, source_target_pairs={{0,8},{8,16},{16,24},{24,0},{1,9},{9,17},{17,25},{25,1},{2,10},{10... | collective-permute-start | bytes 98312 | tf_op jit(solution)/shard_map/ppermute | solution.py:230
  12.2 2.6 %collective-permute-start.1 = (bf16[128,128]{1,0:T(8,128)(2,1)S(1)}, bf16[128,128]{1,0:T(8,128)(2,1)S(1)}, u32[]{:S(2)}, u32[]{:S(2)}) collective-permute-start(bf16[128,128]{1,0:T(8,128)(2,1)S(1)} %get-tuple-element.21), channel_id=1, source_target_pairs={{0,16},{8,24},{16,0},{24,8},{1,17},{9,25},{17,1},{25,9},{2,18},{10... | collective-permute-start | bytes 98312 | tf_op jit(solution)/shard_map/ppermute | solution.py:230
  14.8 1.3 %collective-permute-start.2 = (bf16[128,128]{1,0:T(8,128)(2,1)S(1)}, bf16[128,128]{1,0:T(8,128)(2,1)S(1)}, u32[]{:S(2)}, u32[]{:S(2)}) collective-permute-start(bf16[128,128]{1,0:T(8,128)(2,1)S(1)} %get-tuple-element.22), channel_id=1, source_target_pairs={{0,24},{8,0},{16,8},{24,16},{1,25},{9,1},{17,9},{25,17},{2,26},{10... | collective-permute-start | bytes 98312 | tf_op jit(solution)/shard_map/ppermute | solution.py:230
  16.1 0.0 collective-permute-done.refs_7_
  16.1 1.2 %collective-permute-done.1.refs_8_ = bf16[128,128]{1,0:T(8,128)(2,1)S(1)} collective-permute-done((bf16[128,128]{1,0:T(8,128)(2,1)S(1)}, bf16[128,128]{1,0:T(8,128)(2,1)S(1)}, u32[]{:S(2)}, u32[]{:S(2)}) %collective-permute-start.1) | collective-permute-done | bytes 32800 | tf_op jit(solution)/shard_map/ppermute | solution.py:230
  17.3 1.3 %collective-permute-done.2.refs_9_ = bf16[128,128]{1,0:T(8,128)(2,1)S(1)} collective-permute-done((bf16[128,128]{1,0:T(8,128)(2,1)S(1)}, bf16[128,128]{1,0:T(8,128)(2,1)S(1)}, u32[]{:S(2)}, u32[]{:S(2)}) %collective-permute-start.2) | collective-permute-done | bytes 32800 | tf_op jit(solution)/shard_map/ppermute | solution.py:230
  18.7 0.0 copy-start
  18.7 0.0 copy-start.12
  18.7 0.1 collective-permute-start.5
  18.8 1.6 %collective-permute-start.4 = (bf16[256,128]{1,0:T(8,128)(2,1)S(1)}, bf16[256,128]{1,0:T(8,128)(2,1)S(1)}, u32[]{:S(2)}, u32[]{:S(2)}) collective-permute-start(bf16[256,128]{1,0:T(8,128)(2,1)S(1)} %pad_maximum_fusion.refs_0_), channel_id=1, source_target_pairs={{0,4},{2,6},{4,0},{6,2},{1,5},{3,7},{5,1},{7,3},{8,12},{10,14},{12... | collective-permute-start | bytes 196616 | tf_op jit(solution)/shard_map/ppermute | solution.py:230
  20.4 0.2 collective-permute-start.3
  20.5 0.0 copy-done.9
  20.5 0.0 copy-done.10
  20.5 0.0 copy-done.13
  20.5 0.0 copy-done.7
  20.5 1.3 %dense.1.refs_4_ = bf16[2048,256]{1,0:T(8,128)(2,1)S(1)} custom-call(bf16[2,1,4,128,128]{4,3,2,1,0:T(8,128)(2,1)S(1)} %copy-done.7, s32[2,1,4]{2,1,0:T(1,128)S(1)} %copy-done.13, bf16[1,32,256]{2,1,0:T(8,128)(2,1)S(1)} %copy-done.10, bf16[1,1,32,2048]{3,2,1,0:T(8,128)(2,1)S(1)} %copy-done.9), custom_call_target="tpu_custom_call" | custom-call | flops 67108864 | bytes 2097152 | tf_op jit(solution)/shard_map/dense/pallas_call | solution.py:273
  21.8 0.0 collective-permute-done.5.refs_3_
  21.8 2.6 %collective-permute-done.4.refs_2_ = bf16[256,128]{1,0:T(8,128)(2,1)S(1)} collective-permute-done((bf16[256,128]{1,0:T(8,128)(2,1)S(1)}, bf16[256,128]{1,0:T(8,128)(2,1)S(1)}, u32[]{:S(2)}, u32[]{:S(2)}) %collective-permute-start.4) | collective-permute-done | bytes 65568 | tf_op jit(solution)/shard_map/ppermute | solution.py:230
  24.4 0.2 collective-permute-done.3.refs_1_
  24.6 0.3 integral.2
  24.9 1.6 %collective-permute-start.6 = (bf16[64,128]{1,0:T(8,128)(2,1)S(1)}, bf16[64,128]{1,0:T(8,128)(2,1)S(1)}, u32[]{:S(2)}, u32[]{:S(2)}) collective-permute-start(bf16[64,128]{1,0:T(8,128)(2,1)S(1)} %get-tuple-element.25), channel_id=1, source_target_pairs={{0,1},{1,0},{2,3},{3,2},{4,5},{5,4},{6,7},{7,6},{8,9},{9,8},{10,11... | collective-permute-start | bytes 49160 | tf_op jit(solution)/shard_map/ppermute | solution.py:230
  26.5 0.0 copy-done.2
  26.5 0.0 copy-done.4
  26.5 1.9 %boundary.1.refs_5_ = f32[4,64,128]{2,1,0:T(8,128)S(1)} custom-call(bf16[256,128]{1,0:T(8,128)(2,1)S(1)} %pad_maximum_fusion.refs_0_, bf16[64,1536]{1,0:T(8,128)(2,1)S(1)} %copy-done.2, bf16[4,7,128,128]{3,2,1,0:T(8,128)(2,1)S(1)} %slice.21.refs_3_.refs_2_, bf16[4,128,128]{2,1,0:T(8,128)(2,1)S(1)} %copy-done.4, s32[12,7]{1,0:T(8,128)S(1)} %copy.14.refs_5_.refs_4_, ...), custom_call_target="tpu_custom_call" | custom-call | flops 75497472 | bytes 1048576 | tf_op jit(solution)/shard_map/boundary/pallas_call | solution.py:299
  28.4 0.4 collective-permute-done.6.refs_6_
  28.7 0.0 copy-done.6
  28.7 0.2 step.1
  28.9 0.2 collective-permute-start.7
  29.1 3.5 %collective-permute-start.8 = (bf16[128,128]{1,0:T(8,128)(2,1)S(1)}, bf16[128,128]{1,0:T(8,128)(2,1)S(1)}, u32[]{:S(2)}, u32[]{:S(2)}) collective-permute-start(bf16[128,128]{1,0:T(8,128)(2,1)S(1)} %get-tuple-element.28), channel_id=1, source_target_pairs={{0,16},{8,24},{16,0},{24,8},{1,17},{9,25},{17,1},{25,9},{2,18},{10... | collective-permute-start | bytes 98312 | tf_op jit(solution)/shard_map/ppermute | solution.py:230
  32.6 0.1 collective-permute-start.9
  32.7 2.0 %collective-permute-done.7.refs_6_ = bf16[128,128]{1,0:T(8,128)(2,1)S(1)} collective-permute-done((bf16[128,128]{1,0:T(8,128)(2,1)S(1)}, bf16[128,128]{1,0:T(8,128)(2,1)S(1)}, u32[]{:S(2)}, u32[]{:S(2)}) %collective-permute-start.7) | collective-permute-done | bytes 32800 | tf_op jit(solution)/shard_map/ppermute | solution.py:230
  34.7 0.5 %collective-permute-done.8.refs_7_ = bf16[128,128]{1,0:T(8,128)(2,1)S(1)} collective-permute-done((bf16[128,128]{1,0:T(8,128)(2,1)S(1)}, bf16[128,128]{1,0:T(8,128)(2,1)S(1)}, u32[]{:S(2)}, u32[]{:S(2)}) %collective-permute-start.8) | collective-permute-done | bytes 32800 | tf_op jit(solution)/shard_map/ppermute | solution.py:230
  35.2 1.3 %collective-permute-done.9.refs_8_ = bf16[128,128]{1,0:T(8,128)(2,1)S(1)} collective-permute-done((bf16[128,128]{1,0:T(8,128)(2,1)S(1)}, bf16[128,128]{1,0:T(8,128)(2,1)S(1)}, u32[]{:S(2)}, u32[]{:S(2)}) %collective-permute-start.9) | collective-permute-done | bytes 32800 | tf_op jit(solution)/shard_map/ppermute | solution.py:230
  36.5 0.1 collective-permute-start.12
  36.6 0.9 %collective-permute-start.11 = (bf16[256,128]{1,0:T(8,128)(2,1)S(1)}, bf16[256,128]{1,0:T(8,128)(2,1)S(1)}, u32[]{:S(2)}, u32[]{:S(2)}) collective-permute-start(bf16[256,128]{1,0:T(8,128)(2,1)S(1)} %pad_maximum_fusion.1.refs_0_), channel_id=1, source_target_pairs={{0,4},{2,6},{4,0},{6,2},{1,5},{3,7},{5,1},{7,3},{8,12},{10,14},{12... | collective-permute-start | bytes 196616 | tf_op jit(solution)/shard_map/ppermute | solution.py:230
  37.5 0.2 collective-permute-start.10
  37.7 1.0 %collective-permute-done.12.refs_3_ = bf16[256,128]{1,0:T(8,128)(2,1)S(1)} collective-permute-done((bf16[256,128]{1,0:T(8,128)(2,1)S(1)}, bf16[256,128]{1,0:T(8,128)(2,1)S(1)}, u32[]{:S(2)}, u32[]{:S(2)}) %collective-permute-start.12) | collective-permute-done | bytes 65568 | tf_op jit(solution)/shard_map/ppermute | solution.py:230
  38.7 2.8 %collective-permute-done.11.refs_2_ = bf16[256,128]{1,0:T(8,128)(2,1)S(1)} collective-permute-done((bf16[256,128]{1,0:T(8,128)(2,1)S(1)}, bf16[256,128]{1,0:T(8,128)(2,1)S(1)}, u32[]{:S(2)}, u32[]{:S(2)}) %collective-permute-start.11) | collective-permute-done | bytes 65568 | tf_op jit(solution)/shard_map/ppermute | solution.py:230
  41.6 0.3 collective-permute-done.10.refs_1_
  41.8 0.3 integral.3
  42.1 1.6 %collective-permute-start.13 = (bf16[64,128]{1,0:T(8,128)(2,1)S(1)}, bf16[64,128]{1,0:T(8,128)(2,1)S(1)}, u32[]{:S(2)}, u32[]{:S(2)}) collective-permute-start(bf16[64,128]{1,0:T(8,128)(2,1)S(1)} %get-tuple-element.33), channel_id=1, source_target_pairs={{0,1},{1,0},{2,3},{3,2},{4,5},{5,4},{6,7},{7,6},{8,9},{9,8},{10,11... | collective-permute-start | bytes 49160 | tf_op jit(solution)/shard_map/ppermute | solution.py:230
  43.7 0.0 copy-done
  43.7 0.0 copy-done.12
  43.7 2.8 %volume.1 = f32[64,1536]{1,0:T(8,128)} custom-call(bf16[256,128]{1,0:T(8,128)(2,1)S(1)} %pad_maximum_fusion.1.refs_0_, bf16[64,1536]{1,0:T(8,128)(2,1)S(1)} %copy-done.2, bf16[12,7,128,128]{3,2,1,0:T(8,128)(2,1)S(1)} %copy-done, bf16[4,128,128]{2,1,0:T(8,128)(2,1)S(1)} %copy-done.4, s32[12,7]{1,0:T(8,128)S(1)} %copy.14.refs_5_.refs_4_, s32[4]{0:T(128)S(1)} %copy-done.12, ...), custom_call_target="tpu_custom_call" | custom-call | flops 176160768 | bytes 2752512 | tf_op jit(solution)/shard_map/volume/pallas_call | solution.py:289
  46.5 0.0 collective-permute-done.13.refs_5_
  46.5 0.8 %last.1 = f32[64,128]{1,0:T(8,128)} custom-call(f32[64,128]{1,0:T(8,128)S(1)} %get-tuple-element.30.refs_0_, bf16[64,128]{1,0:T(8,128)(2,1)S(1)} %copy-done.8, bf16[1,128,128]{2,1,0:T(8,128)(2,1)S(1)} %copy-done.6, f32[64,128]{1,0:T(8,128)S(1)} %get-tuple-element.31.refs_3_, f32[64,128]{1,0:T(8,128)S(1)} %get-tuple-element.32.refs_4_, ...), custom_call_target="tpu_custom_call" | custom-call | flops 2097152 | bytes 131072 | tf_op jit(solution)/shard_map/last/pallas_call | solution.py:318
  (10 shorter events, 0.0 us)
Async XLA Ops:
  0.6 19.9 %copy-start.9 = (bf16[1,1,32,2048]{3,2,1,0:T(8,128)(2,1)S(1)}, bf16[1,1,32,2048]{3,2,1,0:T(8,128)(2,1)}, u32[]{:S(2)}) copy-start(bf16[1,1,32,2048]{3,2,1,0:T(8,128)(2,1)} %refs_3_.3) | copy-start | bytes 393220
  0.6 19.9 %copy-start.10 = (bf16[1,32,256]{2,1,0:T(8,128)(2,1)S(1)}, bf16[1,32,256]{2,1,0:T(8,128)(2,1)}, u32[]{:S(2)}) copy-start(bf16[1,32,256]{2,1,0:T(8,128)(2,1)} %refs_2_.6) | copy-start | bytes 49156
  0.7 19.9 %copy-start.13 = (s32[2,1,4]{2,1,0:T(1,128)S(1)}, s32[2,1,4]{2,1,0:T(1,128)}, u32[]{:S(2)}) copy-start(s32[2,1,4]{2,1,0:T(1,128)} %refs_1_.7) | copy-start | bytes 100
  0.7 19.9 %copy-start.7 = (bf16[2,1,4,128,128]{4,3,2,1,0:T(8,128)(2,1)S(1)}, bf16[2,1,4,128,128]{4,3,2,1,0:T(8,128)(2,1)}, u32[]{:S(2)}) copy-start(bf16[2,1,4,128,128]{4,3,2,1,0:T(8,128)(2,1)} %refs_0_.3) | copy-start | bytes 786436
  2.2 24.3 %copy-start.2 = (bf16[64,1536]{1,0:T(8,128)(2,1)S(1)}, bf16[64,1536]{1,0:T(8,128)(2,1)}, u32[]{:S(2)}) copy-start(bf16[64,1536]{1,0:T(8,128)(2,1)} %refs_1_.10) | copy-start | bytes 589828
  2.2 24.3 %copy-start.4 = (bf16[4,128,128]{2,1,0:T(8,128)(2,1)S(1)}, bf16[4,128,128]{2,1,0:T(8,128)(2,1)}, u32[]{:S(2)}) copy-start(bf16[4,128,128]{2,1,0:T(8,128)(2,1)} %refs_3_.5) | copy-start | bytes 393220
  3.5 0.9 %copy-start.1 = (bf16[64,1536]{1,0:T(8,128)(2,1)S(1)}, bf16[64,1536]{1,0:T(8,128)(2,1)}, u32[]{:S(2)}) copy-start(bf16[64,1536]{1,0:T(8,128)(2,1)} %refs_1_.10) | copy-start | bytes 589828
  4.4 0.9 %copy-start.3 = (bf16[4,128,128]{2,1,0:T(8,128)(2,1)S(1)}, bf16[4,128,128]{2,1,0:T(8,128)(2,1)}, u32[]{:S(2)}) copy-start(bf16[4,128,128]{2,1,0:T(8,128)(2,1)} %refs_3_.5) | copy-start | bytes 393220
  5.3 0.8 %copy-start.5 = (bf16[1,128,128]{2,1,0:T(8,128)(2,1)S(1)}, bf16[1,128,128]{2,1,0:T(8,128)(2,1)}, u32[]{:S(2)}) copy-start(bf16[1,128,128]{2,1,0:T(8,128)(2,1)} %refs_2_.9) | copy-start | bytes 98308
  6.0 0.7 %copy-start.8 = (bf16[64,128]{1,0:T(8,128)(2,1)S(1)}, bf16[64,128]{1,0:T(8,128)(2,1)}, u32[]{:S(2)}) copy-start(bf16[64,128]{1,0:T(8,128)(2,1)} %refs_1_.11) | copy-start | bytes 49156
  6.8 0.7 %copy-start.11 = (s32[4]{0:T(128)S(1)}, s32[4]{0:T(128)}, u32[]{:S(2)}) copy-start(s32[4]{0:T(128)} %refs_5_.4) | copy-start | bytes 52
  7.4 21.3 %copy-start.6 = (bf16[1,128,128]{2,1,0:T(8,128)(2,1)S(1)}, bf16[1,128,128]{2,1,0:T(8,128)(2,1)}, u32[]{:S(2)}) copy-start(bf16[1,128,128]{2,1,0:T(8,128)(2,1)} %refs_2_.9) | copy-start | bytes 98308
  9.1 7.0 %collective-permute-start = (bf16[128,128]{1,0:T(8,128)(2,1)S(1)}, bf16[128,128]{1,0:T(8,128)(2,1)S(1)}, u32[]{:S(2)}, u32[]{:S(2)}) collective-permute-start(bf16[128,128]{1,0:T(8,128)(2,1)S(1)} %get-tuple-element.20), channel_id=1, source_target_pairs={{0,8},{8,16},{16,24},{24,0},{1,9},{9,17},{17,25},{25,1},{2,10},{10... | collective-permute-start | bytes 98312 | tf_op jit(solution)/shard_map/ppermute | solution.py:230
  12.2 5.2 %collective-permute-start.1 = (bf16[128,128]{1,0:T(8,128)(2,1)S(1)}, bf16[128,128]{1,0:T(8,128)(2,1)S(1)}, u32[]{:S(2)}, u32[]{:S(2)}) collective-permute-start(bf16[128,128]{1,0:T(8,128)(2,1)S(1)} %get-tuple-element.21), channel_id=1, source_target_pairs={{0,16},{8,24},{16,0},{24,8},{1,17},{9,25},{17,1},{25,9},{2,18},{10... | collective-permute-start | bytes 98312 | tf_op jit(solution)/shard_map/ppermute | solution.py:230
  14.8 3.9 %collective-permute-start.2 = (bf16[128,128]{1,0:T(8,128)(2,1)S(1)}, bf16[128,128]{1,0:T(8,128)(2,1)S(1)}, u32[]{:S(2)}, u32[]{:S(2)}) collective-permute-start(bf16[128,128]{1,0:T(8,128)(2,1)S(1)} %get-tuple-element.22), channel_id=1, source_target_pairs={{0,24},{8,0},{16,8},{24,16},{1,25},{9,1},{17,9},{25,17},{2,26},{10... | collective-permute-start | bytes 98312 | tf_op jit(solution)/shard_map/ppermute | solution.py:230
  18.7 25.0 %copy-start = (bf16[12,7,128,128]{3,2,1,0:T(8,128)(2,1)S(1)}, bf16[12,7,128,128]{3,2,1,0:T(8,128)(2,1)}, u32[]{:S(2)}) copy-start(bf16[12,7,128,128]{3,2,1,0:T(8,128)(2,1)} %refs_2_.8) | copy-start | bytes 8257540
  18.7 25.0 %copy-start.12 = (s32[4]{0:T(128)S(1)}, s32[4]{0:T(128)}, u32[]{:S(2)}) copy-start(s32[4]{0:T(128)} %refs_5_.4) | copy-start | bytes 52
  18.7 3.1 %collective-permute-start.5 = (bf16[256,128]{1,0:T(8,128)(2,1)S(1)}, bf16[256,128]{1,0:T(8,128)(2,1)S(1)}, u32[]{:S(2)}, u32[]{:S(2)}) collective-permute-start(bf16[256,128]{1,0:T(8,128)(2,1)S(1)} %pad_maximum_fusion.refs_0_), channel_id=1, source_target_pairs={{0,6},{2,0},{4,2},{6,4},{1,7},{3,1},{5,3},{7,5},{8,14},{10,8},{12,... | collective-permute-start | bytes 196616 | tf_op jit(solution)/shard_map/ppermute | solution.py:230
  18.8 5.7 %collective-permute-start.4 = (bf16[256,128]{1,0:T(8,128)(2,1)S(1)}, bf16[256,128]{1,0:T(8,128)(2,1)S(1)}, u32[]{:S(2)}, u32[]{:S(2)}) collective-permute-start(bf16[256,128]{1,0:T(8,128)(2,1)S(1)} %pad_maximum_fusion.refs_0_), channel_id=1, source_target_pairs={{0,4},{2,6},{4,0},{6,2},{1,5},{3,7},{5,1},{7,3},{8,12},{10,14},{12... | collective-permute-start | bytes 196616 | tf_op jit(solution)/shard_map/ppermute | solution.py:230
  20.4 4.3 %collective-permute-start.3 = (bf16[256,128]{1,0:T(8,128)(2,1)S(1)}, bf16[256,128]{1,0:T(8,128)(2,1)S(1)}, u32[]{:S(2)}, u32[]{:S(2)}) collective-permute-start(bf16[256,128]{1,0:T(8,128)(2,1)S(1)} %pad_maximum_fusion.refs_0_), channel_id=1, source_target_pairs={{0,2},{2,4},{4,6},{6,0},{1,3},{3,5},{5,7},{7,1},{8,10},{10,12},{12... | collective-permute-start | bytes 196616 | tf_op jit(solution)/shard_map/ppermute | solution.py:230
  24.9 3.8 %collective-permute-start.6 = (bf16[64,128]{1,0:T(8,128)(2,1)S(1)}, bf16[64,128]{1,0:T(8,128)(2,1)S(1)}, u32[]{:S(2)}, u32[]{:S(2)}) collective-permute-start(bf16[64,128]{1,0:T(8,128)(2,1)S(1)} %get-tuple-element.25), channel_id=1, source_target_pairs={{0,1},{1,0},{2,3},{3,2},{4,5},{5,4},{6,7},{7,6},{8,9},{9,8},{10,11... | collective-permute-start | bytes 49160 | tf_op jit(solution)/shard_map/ppermute | solution.py:230
  28.9 5.8 %collective-permute-start.7 = (bf16[128,128]{1,0:T(8,128)(2,1)S(1)}, bf16[128,128]{1,0:T(8,128)(2,1)S(1)}, u32[]{:S(2)}, u32[]{:S(2)}) collective-permute-start(bf16[128,128]{1,0:T(8,128)(2,1)S(1)} %get-tuple-element.27), channel_id=1, source_target_pairs={{0,8},{8,16},{16,24},{24,0},{1,9},{9,17},{17,25},{25,1},{2,10},{10... | collective-permute-start | bytes 98312 | tf_op jit(solution)/shard_map/ppermute | solution.py:230
  29.1 6.1 %collective-permute-start.8 = (bf16[128,128]{1,0:T(8,128)(2,1)S(1)}, bf16[128,128]{1,0:T(8,128)(2,1)S(1)}, u32[]{:S(2)}, u32[]{:S(2)}) collective-permute-start(bf16[128,128]{1,0:T(8,128)(2,1)S(1)} %get-tuple-element.28), channel_id=1, source_target_pairs={{0,16},{8,24},{16,0},{24,8},{1,17},{9,25},{17,1},{25,9},{2,18},{10... | collective-permute-start | bytes 98312 | tf_op jit(solution)/shard_map/ppermute | solution.py:230
  32.6 3.9 %collective-permute-start.9 = (bf16[128,128]{1,0:T(8,128)(2,1)S(1)}, bf16[128,128]{1,0:T(8,128)(2,1)S(1)}, u32[]{:S(2)}, u32[]{:S(2)}) collective-permute-start(bf16[128,128]{1,0:T(8,128)(2,1)S(1)} %get-tuple-element.29), channel_id=1, source_target_pairs={{0,24},{8,0},{16,8},{24,16},{1,25},{9,1},{17,9},{25,17},{2,26},{10... | collective-permute-start | bytes 98312 | tf_op jit(solution)/shard_map/ppermute | solution.py:230
  36.5 2.2 %collective-permute-start.12 = (bf16[256,128]{1,0:T(8,128)(2,1)S(1)}, bf16[256,128]{1,0:T(8,128)(2,1)S(1)}, u32[]{:S(2)}, u32[]{:S(2)}) collective-permute-start(bf16[256,128]{1,0:T(8,128)(2,1)S(1)} %pad_maximum_fusion.1.refs_0_), channel_id=1, source_target_pairs={{0,6},{2,0},{4,2},{6,4},{1,7},{3,1},{5,3},{7,5},{8,14},{10,8},{12,... | collective-permute-start | bytes 196616 | tf_op jit(solution)/shard_map/ppermute | solution.py:230
  36.6 5.0 %collective-permute-start.11 = (bf16[256,128]{1,0:T(8,128)(2,1)S(1)}, bf16[256,128]{1,0:T(8,128)(2,1)S(1)}, u32[]{:S(2)}, u32[]{:S(2)}) collective-permute-start(bf16[256,128]{1,0:T(8,128)(2,1)S(1)} %pad_maximum_fusion.1.refs_0_), channel_id=1, source_target_pairs={{0,4},{2,6},{4,0},{6,2},{1,5},{3,7},{5,1},{7,3},{8,12},{10,14},{12... | collective-permute-start | bytes 196616 | tf_op jit(solution)/shard_map/ppermute | solution.py:230
  37.5 4.3 %collective-permute-start.10 = (bf16[256,128]{1,0:T(8,128)(2,1)S(1)}, bf16[256,128]{1,0:T(8,128)(2,1)S(1)}, u32[]{:S(2)}, u32[]{:S(2)}) collective-permute-start(bf16[256,128]{1,0:T(8,128)(2,1)S(1)} %pad_maximum_fusion.1.refs_0_), channel_id=1, source_target_pairs={{0,2},{2,4},{4,6},{6,0},{1,3},{3,5},{5,7},{7,1},{8,10},{10,12},{12... | collective-permute-start | bytes 196616 | tf_op jit(solution)/shard_map/ppermute | solution.py:230
  42.1 4.3 %collective-permute-start.13 = (bf16[64,128]{1,0:T(8,128)(2,1)S(1)}, bf16[64,128]{1,0:T(8,128)(2,1)S(1)}, u32[]{:S(2)}, u32[]{:S(2)}) collective-permute-start(bf16[64,128]{1,0:T(8,128)(2,1)S(1)} %get-tuple-element.33), channel_id=1, source_target_pairs={{0,1},{1,0},{2,3},{3,2},{4,5},{5,4},{6,7},{7,6},{8,9},{9,8},{10,11... | collective-permute-start | bytes 49160 | tf_op jit(solution)/shard_map/ppermute | solution.py:230

commit v2 on v1

--- a/solution.py
+++ b/solution.py
@@ -31,7 +31,7 @@
 
 def block_row(read, blocks, columns, row):
     terms = blocks.shape[1]
-    field = jnp.concatenate([read(columns[row, n]) for n in range(terms)], axis=1)
+    field = jnp.concatenate([read(columns[n, row]) for n in range(terms)], axis=1)
     inverse = jnp.concatenate([blocks[row, n] for n in range(terms)], axis=1)
     return by_rows(field, inverse)
 
@@ -72,27 +72,47 @@
         payload[angles : 2 * angles, :] = total[k + 1].astype(HALF)
 
 
-def start_kernel(axis, refs):
-    (surf_rhs, surf_inverse, vol_rhs, blocks, coupling, columns, trace_map, bnd_count) = refs[:8]
-    surface, half_out, own_trace = refs[8:11]
-    payloads, total = refs[11:-1], refs[-1]
+def start_kernel(axis, outs, kept, refs):
+    bnd_count, operands, refs = refs[0], refs[1 : 8 + kept], refs[8 + kept :]
+    surface, half_out, own_trace, *payloads = refs[:outs]
+    copied, refs = refs[outs : outs + kept + 2], refs[outs + kept + 2 :]
+    surf_rhs, surf_inverse, vol_rhs, blocks, coupling, columns, trace_map, total, sems = refs
+    slots = coupling.shape[0]
     bs = coupling.shape[-1]
+    count = iter(range(sems.shape[0]))
+
+    def copy(source, to):
+        started = pltpu.make_async_copy(source, to, sems.at[next(count)])
+        started.start()
+        return started
+
+    tables = [copy(operands[5 + i], t) for i, t in enumerate((columns, trace_map))]
+    first = [copy(operands[0], surf_rhs), copy(operands[1], surf_inverse)]
+    tables.append(copy(operands[2], vol_rhs))
+    rows = [copy(operands[3].at[j], blocks.at[j]) for j in range(slots)]
+    last = copy(operands[4], coupling)
+    later = [copy(operands[5 + i], t) for i, t in enumerate(copied)]
+    total[...] = jnp.zeros_like(total)
+    for c in first:
+        c.wait()
     for b in range(surf_inverse.shape[0]):
         cols = slice(b * bs, (b + 1) * bs)
         surface[:, cols] = by_rows(surf_rhs[:, cols], surf_inverse[b])
     half = surface[...].astype(HALF)
     half_out[...] = half
-    total[...] = jnp.zeros_like(total)
-
-    def read(col):
-        return vol_rhs[:, block(col, bs)]
-
-    def boundary(j):
-        return block_row(read, blocks, columns, j).astype(HALF)
-
-    add_traces(total, boundary, coupling, trace_map, bnd_count, axis)
+    for c in tables:
+        c.wait()
+    solved = []
+    for j in range(slots):
+        rows[j].wait()
+        read = lambda col: vol_rhs[:, block(col, bs)]
+        solved.append(block_row(read, blocks, columns, j).astype(HALF))
+    last.wait()
+    add_traces(total, lambda j: solved[j], coupling, trace_map, bnd_count, axis)
     own_trace[...] = total[0]
     send_out(payloads, half, total)
+    for c in later:
+        c.wait()
 
 
 def boundary_kernel(axis, refs):
@@ -111,13 +131,22 @@
     add_traces(total, boundary, coupling, trace_map, bnd_count, axis)
 
 
-def volume_kernel(axis, count, refs):
-    (group, vol_rhs, blocks, coupling, columns, trace_map, bnd_count, volume, field) = refs
+def early_kernel(axis, count, refs):
+    (group, vol_rhs, blocks, coupling, columns, trace_map, bnd_count, early, field) = refs
     bs = coupling.shape[-1]
     for b in range(coupling.shape[0], vol_rhs.shape[1] // bs):
         field[b] = vol_rhs[:, b * bs : (b + 1) * bs]
     residual_blocks(field, vol_rhs, group, coupling, trace_map, bnd_count, axis, count)
-    for b in range(blocks.shape[0]):
+    for b in range(early.shape[1] // bs):
+        early[:, b * bs : (b + 1) * bs] = block_row(lambda col: field[col], blocks, columns, b)
+
+
+def late_kernel(refs):
+    early, field, blocks, columns, volume = refs
+    bs = field.shape[-1]
+    first = early.shape[1] // bs
+    volume[:, : first * bs] = early[...]
+    for b in range(first, blocks.shape[0]):
         volume[:, b * bs : (b + 1) * bs] = block_row(lambda col: field[col], blocks, columns, b)
 
 
@@ -157,7 +186,7 @@
 
 
 def integral_kernel(row_size, vol_size, refs):
-    groups, dense, outs = refs[:row_size], refs[row_size], refs[row_size + 1 :]
+    groups, dense, outs = refs[:row_size], refs[row_size], refs[row_size + 2 :]
     angles, width = groups[0].shape[0] // vol_size, groups[0].shape[1]
     field = jnp.concatenate(
         [g[k * angles : (k + 1) * angles, :] for g in groups for k in range(vol_size)], axis=1
@@ -209,6 +238,10 @@
 SMEM = pl.BlockSpec(memory_space=pltpu.SMEM)
 
 
+ANY = pl.BlockSpec(memory_space=pl.ANY)
+HBM = pl.BlockSpec(memory_space=pltpu.HBM)
+
+
 def call(body, name, in_specs, outs, flops, moved, scratch=()):
     def kernel(*refs):
         body(refs)
@@ -223,6 +256,10 @@
         cost_estimate=pl.CostEstimate(flops=flops, bytes_accessed=moved, transcendentals=0),
         compiler_params=pltpu.CompilerParams(vmem_limit_bytes=48 << 20),
     )
+
+
+def in_hbm(operand):
+    return pltpu.with_memory_space_constraint(operand, pltpu.HBM)
 
 
 def shifted(value, axis, shift):
@@ -254,21 +291,34 @@
     def shape(dims, dtype):
         return jax.ShapeDtypeStruct(dims, dtype)
 
-    boundary_blocks = vol_blocks[:slots]
-    tables = (vol_cols, trace_map, bnd_count)
+    tables = (vol_cols.T, trace_map)
     payload_shapes = [shape((2 * angles, width), HALF)] * (nv - 1)
+    start_shapes = [shape(piece, F32), shape(piece, HALF), shape(piece, F32)] + payload_shapes
     totals = pltpu.VMEM((nv,) + piece, F32)
     field = pltpu.VMEM((vol_count, angles, bs), HALF)
 
-    surface, half, own_trace, *payloads = call(
-        functools.partial(start_kernel, "vol"),
+    kept = (near_blocks, near_cols, far_u, far_v)
+    started = call(
+        functools.partial(start_kernel, "vol", len(start_shapes), len(kept)),
         "start",
-        [VMEM] * 3 + [VMEM] * 2 + [SMEM] * 3,
-        [shape(piece, F32), shape(piece, HALF), shape(piece, F32)] + payload_shapes,
+        [SMEM] + [HBM] * (7 + len(kept)),
+        start_shapes + [pltpu.VMEM(a.shape, a.dtype) for a in tables + kept],
         product * slots * (terms + 1),
         2 * bs * bs * slots * (terms + 1),
-        [totals],
-    )(surf_rhs, surf_inverse, vol_rhs, boundary_blocks, coupling, *tables)
+        [
+            pltpu.VMEM(piece, HALF),
+            pltpu.VMEM(surf_inverse.shape, HALF),
+            pltpu.VMEM(vol_rhs.shape, HALF),
+            pltpu.VMEM((slots, terms, bs, bs), HALF),
+            pltpu.VMEM(coupling.shape, HALF),
+            *(pltpu.SMEM(t.shape, jnp.int32) for t in tables),
+            totals,
+            pltpu.SemaphoreType.DMA((8 + slots + len(kept),)),
+        ],
+    )(bnd_count, *map(in_hbm, (surf_rhs, surf_inverse, vol_rhs, vol_blocks, coupling) + tables + kept))
+    surface, half, own_trace, *payloads = started[: len(start_shapes)]
+    kept = started[len(start_shapes) :]
+    tables, kept = (*kept[:2], bnd_count), kept[2:]
 
     (dense,) = call(
         functools.partial(dense_kernel, nv, nr, nc),
@@ -278,43 +328,55 @@
         product * nv * nr * nc,
         4 * nv * nr * nc * bs * bs,
         [pltpu.VMEM((nv * nr * width, bs), F32)],
-    )(near_blocks, near_cols, far_u, far_v)
+    )(*kept)
 
     for iteration in range(ITERS):
         received = [shifted(payloads[k - 1], "vol", k) for k in range(1, nv)]
         group = jnp.concatenate([half] + [r[:angles] for r in received], axis=0)
+        if iteration == 0:
+            group, dense = lax.optimization_barrier((group, dense))
         groups = [group] + [shifted(group, "row", k) for k in range(1, nr)]
         last = iteration == ITERS - 1
         if last:
-            (volume,) = call(
-                functools.partial(volume_kernel, "vol", nv),
-                "volume",
+            split = vol_count // 2
+            early, residual = call(
+                functools.partial(early_kernel, "vol", nv),
+                "early_volume",
                 [VMEM] * 4 + [SMEM] * 3,
-                [shape((angles, vol_count * bs), F32)],
-                product * vol_count * terms,
-                2 * bs * bs * vol_count * terms,
-                [field],
+                [shape((angles, split * bs), F32), shape((vol_count, angles, bs), HALF)],
+                product * split * terms,
+                2 * bs * bs * split * terms,
             )(group, vol_rhs, vol_blocks, coupling, *tables)
+            beside = early
         else:
             (total,) = call(
                 functools.partial(boundary_kernel, "vol"),
                 "boundary",
-                [VMEM] * 2 + [VMEM] * 2 + [SMEM] * 3,
+                [VMEM] * 4 + [SMEM] * 3,
                 [shape((nv,) + piece, F32)],
                 product * slots * (terms + 2),
                 2 * bs * bs * slots * (terms + 1),
                 [field],
-            )(group, vol_rhs, boundary_blocks, coupling, *tables)
+            )(group, vol_rhs, vol_blocks, coupling, *tables)
+            beside = total
         integral, *parts = call(
             functools.partial(integral_kernel, nr, nv),
             "integral",
-            [VMEM] * (nr + 1),
+            [VMEM] * (nr + 1) + [ANY],
             [shape(piece, F32)] + [shape(piece, HALF)] * (nc - 1),
             product * nv * nr * nc,
             2 * nv * nr * nc * width * width,
-        )(*groups, dense)
+        )(*groups, dense, beside)
         sums = [shifted(parts[k - 1], "col", k) for k in range(1, nc)]
         if last:
+            (volume,) = call(
+                late_kernel,
+                "late_volume",
+                [VMEM] * 3 + [SMEM],
+                [shape((angles, vol_count * bs), F32)],
+                product * (vol_count - split) * terms,
+                2 * bs * bs * (vol_count - split) * terms,
+            )(early, residual, vol_blocks, tables[0])
             (surface,) = call(
                 functools.partial(last_kernel, nc - 1, nv - 1),
                 "last",

time: 47.6 us -> 41.7 us (0.88)
  local copies, waits for them, and re-layouts: 6.07 us -> 0.04 us
  Pallas kernels: 9.09 us -> 10.5 us
  waiting for transfers between devices: 13.6 us -> 12.5 us
    unnamed x29 -> x10, local copies, waits for them, and re-layouts: 4.77 us -> 0.03 us
    pallas_call x3 -> x4, Pallas kernels: 6.3 us -> 7.74 us  [the longest x1 2.51 us: local(): call(functools.partial(start_kernel, 'vol', len(start_shapes), len(kept))...]
    slice x1 -> x0, local copies, waits for them, and re-layouts: 1.29 us -> none  [local(): boundary_blocks = vol_blocks[:slots]]
    ppermute x14, waiting for transfers between devices: 13.6 us -> 12.5 us  [shifted(): lax.ppermute(value, axis, [(i, (i + shift) % size) for i in range(size)])]
  transfers between devices with their start and end apart: 14 -> 14, of which waited for: 11 -> 10; matrix products, arithmetic and copies ran while one was open for 0% -> 0% of each run, Pallas kernels for 13% -> 16%
where the time goes in v2:
time: 41.7 us; the launch traced here: 41.6 us
  starting transfers between devices  16.9 us (41%)
  waiting for transfers between devices  12.5 us (30%)
  Pallas kernels  10.5 us (25%)
  between operations  1.6 us (4%)
    ppermute x14, starting transfers between devices, shifted(): lax.ppermute(value, axis, [(i, (i + shift) % size) for i in range(size)])  16.9 us
    ppermute x14, waiting for transfers between devices, shifted(): lax.ppermute(value, axis, [(i, (i + shift) % size) for i in range(size)])  12.5 us
    pallas_call x1, Pallas kernels, local(): call(functools.partial(start_kernel, 'vol', len(start_shapes), len(kept))...  2.51 us
    pallas_call x1, Pallas kernels, local(): call(late_kernel, 'late_volume', [VMEM] * 3 + [SMEM], [shape((angles, vol...  1.99 us
    pallas_call x1, Pallas kernels, local(): call(functools.partial(boundary_kernel, 'vol'), 'boundary', [VMEM] * 4 +...  1.82 us
    pallas_call x1, Pallas kernels, local(): call(functools.partial(early_kernel, 'vol', nv), 'early_volume', [VMEM] *...  1.42 us
    pallas_call x1, Pallas kernels, local(): call(functools.partial(dense_kernel, nv, nr, nc), 'dense', [VMEM, SMEM, V...  1.26 us
  transfers between devices with their start and end apart: 14, of which 10 were waited for; matrix products, arithmetic and copies ran while one was open for 0% of the time, Pallas kernels for 16%

profile of v2, /device:TPU:0, one launch (start us, length us, event | category | flops | bytes accessed | tf_op | source)
XLA Modules:
  0.0 41.6 jit_solution(11102964151380648960)
XLA Ops:
  0.6 0.0 copy-start
  0.6 0.0 copy-start.2
  0.7 0.0 copy-start.1
  1.5 2.5 %start.1 = (f32[64,128]{1,0:T(8,128)S(1)}, bf16[64,128]{1,0:T(8,128)(2,1)S(1)}, f32[64,128]{1,0:T(8,128)S(1)}, bf16[128,128]{1,0:T(8,128)(2,1)S(1)}, bf16[128,12...) custom-call(s32[1]{0:T(128)S(6)} %copy.14.refs_0_.refs_6_, ...), custom_call_target="tpu_custom_call" | custom-call | flops 67108864 | bytes 1048576 | tf_op jit(solution)/shard_map/start/pallas_call | solution.py:301
  4.0 3.1 %collective-permute-start = (bf16[128,128]{1,0:T(8,128)(2,1)S(1)}, bf16[128,128]{1,0:T(8,128)(2,1)S(1)}, u32[]{:S(2)}, u32[]{:S(2)}) collective-permute-start(bf16[128,128]{1,0:T(8,128)(2,1)S(1)} %get-tuple-element.30), channel_id=1, source_target_pairs={{0,8},{8,16},{16,24},{24,0},{1,9},{9,17},{17,25},{25,1},{2,10},{10... | collective-permute-start | bytes 98312 | tf_op jit(solution)/shard_map/ppermute | solution.py:267
  7.0 2.6 %collective-permute-start.1 = (bf16[128,128]{1,0:T(8,128)(2,1)S(1)}, bf16[128,128]{1,0:T(8,128)(2,1)S(1)}, u32[]{:S(2)}, u32[]{:S(2)}) collective-permute-start(bf16[128,128]{1,0:T(8,128)(2,1)S(1)} %get-tuple-element.31), channel_id=1, source_target_pairs={{0,16},{8,24},{16,0},{24,8},{1,17},{9,25},{17,1},{25,9},{2,18},{10... | collective-permute-start | bytes 98312 | tf_op jit(solution)/shard_map/ppermute | solution.py:267
  9.6 1.4 %collective-permute-start.2 = (bf16[128,128]{1,0:T(8,128)(2,1)S(1)}, bf16[128,128]{1,0:T(8,128)(2,1)S(1)}, u32[]{:S(2)}, u32[]{:S(2)}) collective-permute-start(bf16[128,128]{1,0:T(8,128)(2,1)S(1)} %get-tuple-element.32), channel_id=1, source_target_pairs={{0,24},{8,0},{16,8},{24,16},{1,25},{9,1},{17,9},{25,17},{2,26},{10... | collective-permute-start | bytes 98312 | tf_op jit(solution)/shard_map/ppermute | solution.py:267
  11.0 1.3 %dense.1.refs_4_ = bf16[2048,256]{1,0:T(8,128)(2,1)S(1)} custom-call(bf16[2,1,4,128,128]{4,3,2,1,0:T(8,128)(2,1)S(1)} %get-tuple-element.33.refs_0_, s32[2,1,4]{2,1,0:T(1,128)S(1)} %get-tuple-element.34.refs_1_, bf16[1,32,256]{2,1,0:T(8,128)(2,1)S(1)} %get-tuple-element.35.refs_2_, bf16[1,1,32,2048]{3,2,1,0:T(8,128)(2,1)S(1)} %get-tuple-element.36.refs_3_), custom_call_target="tpu_custom_call" | custom-call | flops 67108864 | bytes 2097152 | tf_op jit(solution)/shard_map/dense/pallas_call | solution.py:323
  12.3 0.0 copy-start.3
  12.3 0.0 copy-start.4
  12.3 0.0 collective-permute-done.refs_7_
  12.3 0.0 collective-permute-done.1.refs_8_
  12.3 1.2 %collective-permute-done.2.refs_9_ = bf16[128,128]{1,0:T(8,128)(2,1)S(1)} collective-permute-done((bf16[128,128]{1,0:T(8,128)(2,1)S(1)}, bf16[128,128]{1,0:T(8,128)(2,1)S(1)}, u32[]{:S(2)}, u32[]{:S(2)}) %collective-permute-start.2) | collective-permute-done | bytes 32800 | tf_op jit(solution)/shard_map/ppermute | solution.py:267
  13.6 0.1 collective-permute-start.5
  13.6 1.6 %collective-permute-start.4 = (bf16[256,128]{1,0:T(8,128)(2,1)S(1)}, bf16[256,128]{1,0:T(8,128)(2,1)S(1)}, u32[]{:S(2)}, u32[]{:S(2)}) collective-permute-start(bf16[256,128]{1,0:T(8,128)(2,1)S(1)} %pad_maximum_fusion.refs_0_), channel_id=1, source_target_pairs={{0,4},{2,6},{4,0},{6,2},{1,5},{3,7},{5,1},{7,3},{8,12},{10,14},{12... | collective-permute-start | bytes 196616 | tf_op jit(solution)/shard_map/ppermute | solution.py:267
  15.2 0.2 collective-permute-start.3
  15.4 0.0 copy-done
  15.4 0.0 copy-done.2
  15.4 0.0 copy-done.1
  15.4 1.8 %boundary.1.refs_5_ = f32[4,64,128]{2,1,0:T(8,128)S(1)} custom-call(bf16[256,128]{1,0:T(8,128)(2,1)S(1)} %pad_maximum_fusion.refs_0_, bf16[64,1536]{1,0:T(8,128)(2,1)S(1)} %copy-done.1, bf16[12,7,128,128]{3,2,1,0:T(8,128)(2,1)S(1)} %copy-done, bf16[4,128,128]{2,1,0:T(8,128)(2,1)S(1)} %copy-done.2, s32[7,12]{1,0:T(8,128)S(1)} %get-tuple-element.39.refs_4_.refs_3_, ...), custom_call_target="tpu_custom_call" | custom-call | flops 75497472 | bytes 1048576 | tf_op jit(solution)/shard_map/boundary/pallas_call | solution.py:352
  17.2 0.0 collective-permute-done.5.refs_3_
  17.2 2.1 %collective-permute-done.4.refs_2_ = bf16[256,128]{1,0:T(8,128)(2,1)S(1)} collective-permute-done((bf16[256,128]{1,0:T(8,128)(2,1)S(1)}, bf16[256,128]{1,0:T(8,128)(2,1)S(1)}, u32[]{:S(2)}, u32[]{:S(2)}) %collective-permute-start.4) | collective-permute-done | bytes 65568 | tf_op jit(solution)/shard_map/ppermute | solution.py:267
  19.3 0.2 collective-permute-done.3.refs_1_
  19.5 0.3 integral.2
  19.8 1.6 %collective-permute-start.6 = (bf16[64,128]{1,0:T(8,128)(2,1)S(1)}, bf16[64,128]{1,0:T(8,128)(2,1)S(1)}, u32[]{:S(2)}, u32[]{:S(2)}) collective-permute-start(bf16[64,128]{1,0:T(8,128)(2,1)S(1)} %get-tuple-element.43), channel_id=1, source_target_pairs={{0,1},{1,0},{2,3},{3,2},{4,5},{5,4},{6,7},{7,6},{8,9},{9,8},{10,11... | collective-permute-start | bytes 49160 | tf_op jit(solution)/shard_map/ppermute | solution.py:267
  21.3 2.2 %collective-permute-done.6.refs_6_ = bf16[64,128]{1,0:T(8,128)(2,1)S(1)} collective-permute-done((bf16[64,128]{1,0:T(8,128)(2,1)S(1)}, bf16[64,128]{1,0:T(8,128)(2,1)S(1)}, u32[]{:S(2)}, u32[]{:S(2)}) %collective-permute-start.6) | collective-permute-done | bytes 16416 | tf_op jit(solution)/shard_map/ppermute | solution.py:267
  23.6 0.0 copy-done.3
  23.6 0.0 copy-done.4
  23.6 0.2 step.1
  23.8 0.2 collective-permute-start.7
  24.0 3.5 %collective-permute-start.8 = (bf16[128,128]{1,0:T(8,128)(2,1)S(1)}, bf16[128,128]{1,0:T(8,128)(2,1)S(1)}, u32[]{:S(2)}, u32[]{:S(2)}) collective-permute-start(bf16[128,128]{1,0:T(8,128)(2,1)S(1)} %get-tuple-element.46), channel_id=1, source_target_pairs={{0,16},{8,24},{16,0},{24,8},{1,17},{9,25},{17,1},{25,9},{2,18},{10... | collective-permute-start | bytes 98312 | tf_op jit(solution)/shard_map/ppermute | solution.py:267
  27.5 0.1 collective-permute-start.9
  27.6 2.0 %collective-permute-done.7.refs_6_ = bf16[128,128]{1,0:T(8,128)(2,1)S(1)} collective-permute-done((bf16[128,128]{1,0:T(8,128)(2,1)S(1)}, bf16[128,128]{1,0:T(8,128)(2,1)S(1)}, u32[]{:S(2)}, u32[]{:S(2)}) %collective-permute-start.7) | collective-permute-done | bytes 32800 | tf_op jit(solution)/shard_map/ppermute | solution.py:267
  29.6 0.5 %collective-permute-done.8.refs_7_ = bf16[128,128]{1,0:T(8,128)(2,1)S(1)} collective-permute-done((bf16[128,128]{1,0:T(8,128)(2,1)S(1)}, bf16[128,128]{1,0:T(8,128)(2,1)S(1)}, u32[]{:S(2)}, u32[]{:S(2)}) %collective-permute-start.8) | collective-permute-done | bytes 32800 | tf_op jit(solution)/shard_map/ppermute | solution.py:267
  30.1 1.3 %collective-permute-done.9.refs_8_ = bf16[128,128]{1,0:T(8,128)(2,1)S(1)} collective-permute-done((bf16[128,128]{1,0:T(8,128)(2,1)S(1)}, bf16[128,128]{1,0:T(8,128)(2,1)S(1)}, u32[]{:S(2)}, u32[]{:S(2)}) %collective-permute-start.9) | collective-permute-done | bytes 32800 | tf_op jit(solution)/shard_map/ppermute | solution.py:267
  31.4 0.1 collective-permute-start.12
  31.5 0.9 %collective-permute-start.11 = (bf16[256,128]{1,0:T(8,128)(2,1)S(1)}, bf16[256,128]{1,0:T(8,128)(2,1)S(1)}, u32[]{:S(2)}, u32[]{:S(2)}) collective-permute-start(bf16[256,128]{1,0:T(8,128)(2,1)S(1)} %pad_maximum_fusion.1.refs_0_), channel_id=1, source_target_pairs={{0,4},{2,6},{4,0},{6,2},{1,5},{3,7},{5,1},{7,3},{8,12},{10,14},{12... | collective-permute-start | bytes 196616 | tf_op jit(solution)/shard_map/ppermute | solution.py:267
  32.4 0.2 collective-permute-start.10
  32.6 1.4 %early_volume.1 = (f32[64,768]{1,0:T(8,128)S(1)}, bf16[12,64,128]{2,1,0:T(8,128)(2,1)S(1)}) custom-call(bf16[256,128]{1,0:T(8,128)(2,1)S(1)} %pad_maximum_fusion.1.refs_0_, bf16[64,1536]{1,0:T(8,128)(2,1)S(1)} %copy-done.1, bf16[12,7,128,128]{3,2,1,0:T(8,128)(2,1)S(1)} %copy-done, bf16[4,128,128]{2,1,0:T(8,128)(2,1)S(1)} %copy-done.2, ...), custom_call_target="tpu_custom_call" | custom-call | flops 88080384 | bytes 1376256 | tf_op jit(solution)/shard_map/early_volume/pallas_call | solution.py:342
  34.0 0.0 collective-permute-done.12.refs_3_
  34.0 2.4 %collective-permute-done.11.refs_2_ = bf16[256,128]{1,0:T(8,128)(2,1)S(1)} collective-permute-done((bf16[256,128]{1,0:T(8,128)(2,1)S(1)}, bf16[256,128]{1,0:T(8,128)(2,1)S(1)}, u32[]{:S(2)}, u32[]{:S(2)}) %collective-permute-start.11) | collective-permute-done | bytes 65568 | tf_op jit(solution)/shard_map/ppermute | solution.py:267
  36.4 0.3 collective-permute-done.10.refs_1_
  36.7 0.3 integral.3
  37.0 1.6 %collective-permute-start.13 = (bf16[64,128]{1,0:T(8,128)(2,1)S(1)}, bf16[64,128]{1,0:T(8,128)(2,1)S(1)}, u32[]{:S(2)}, u32[]{:S(2)}) collective-permute-start(bf16[64,128]{1,0:T(8,128)(2,1)S(1)} %get-tuple-element.53), channel_id=1, source_target_pairs={{0,1},{1,0},{2,3},{3,2},{4,5},{5,4},{6,7},{7,6},{8,9},{9,8},{10,11... | collective-permute-start | bytes 49160 | tf_op jit(solution)/shard_map/ppermute | solution.py:267
  38.5 2.0 %late_volume.1 = f32[64,1536]{1,0:T(8,128)} custom-call(f32[64,768]{1,0:T(8,128)S(1)} %get-tuple-element.48.refs_0_.refs_5_, bf16[12,64,128]{2,1,0:T(8,128)(2,1)S(1)} %get-tuple-element.49.refs_1_, bf16[12,7,128,128]{3,2,1,0:T(8,128)(2,1)S(1)} %copy-done, s32[7,12]{1,0:T(8,128)S(1)} %get-tuple-element.39.refs_4_.refs_3_), custom_call_target="tpu_custom_call" | custom-call | flops 88080384 | bytes 1376256 | tf_op jit(solution)/shard_map/late_volume/pallas_call | solution.py:372
  40.5 0.3 collective-permute-done.13.refs_5_
  40.8 0.8 %last.1 = f32[64,128]{1,0:T(8,128)} custom-call(f32[64,128]{1,0:T(8,128)S(1)} %get-tuple-element.50.refs_0_, bf16[64,128]{1,0:T(8,128)(2,1)S(1)} %copy-done.4, bf16[1,128,128]{2,1,0:T(8,128)(2,1)S(1)} %copy-done.3, f32[64,128]{1,0:T(8,128)S(1)} %get-tuple-element.51.refs_3_, f32[64,128]{1,0:T(8,128)S(1)} %get-tuple-element.52.refs_4_, ...), custom_call_target="tpu_custom_call" | custom-call | flops 2097152 | bytes 131072 | tf_op jit(solution)/shard_map/last/pallas_call | solution.py:380
  (8 shorter events, 0.0 us)
Async XLA Ops:
  0.6 14.8 %copy-start = (bf16[12,7,128,128]{3,2,1,0:T(8,128)(2,1)S(1)}, bf16[12,7,128,128]{3,2,1,0:T(8,128)(2,1)}, u32[]{:S(2)}) copy-start(bf16[12,7,128,128]{3,2,1,0:T(8,128)(2,1)} %refs_2_.10) | copy-start | bytes 8257540
  0.6 14.7 %copy-start.2 = (bf16[4,128,128]{2,1,0:T(8,128)(2,1)S(1)}, bf16[4,128,128]{2,1,0:T(8,128)(2,1)}, u32[]{:S(2)}) copy-start(bf16[4,128,128]{2,1,0:T(8,128)(2,1)} %refs_3_.5) | copy-start | bytes 393220
  0.7 14.7 %copy-start.1 = (bf16[64,1536]{1,0:T(8,128)(2,1)S(1)}, bf16[64,1536]{1,0:T(8,128)(2,1)}, u32[]{:S(2)}) copy-start(bf16[64,1536]{1,0:T(8,128)(2,1)} %refs_1_.8) | copy-start | bytes 589828
  4.0 8.3 %collective-permute-start = (bf16[128,128]{1,0:T(8,128)(2,1)S(1)}, bf16[128,128]{1,0:T(8,128)(2,1)S(1)}, u32[]{:S(2)}, u32[]{:S(2)}) collective-permute-start(bf16[128,128]{1,0:T(8,128)(2,1)S(1)} %get-tuple-element.30), channel_id=1, source_target_pairs={{0,8},{8,16},{16,24},{24,0},{1,9},{9,17},{17,25},{25,1},{2,10},{10... | collective-permute-start | bytes 98312 | tf_op jit(solution)/shard_map/ppermute | solution.py:267
  7.0 5.3 %collective-permute-start.1 = (bf16[128,128]{1,0:T(8,128)(2,1)S(1)}, bf16[128,128]{1,0:T(8,128)(2,1)S(1)}, u32[]{:S(2)}, u32[]{:S(2)}) collective-permute-start(bf16[128,128]{1,0:T(8,128)(2,1)S(1)} %get-tuple-element.31), channel_id=1, source_target_pairs={{0,16},{8,24},{16,0},{24,8},{1,17},{9,25},{17,1},{25,9},{2,18},{10... | collective-permute-start | bytes 98312 | tf_op jit(solution)/shard_map/ppermute | solution.py:267
  9.6 3.9 %collective-permute-start.2 = (bf16[128,128]{1,0:T(8,128)(2,1)S(1)}, bf16[128,128]{1,0:T(8,128)(2,1)S(1)}, u32[]{:S(2)}, u32[]{:S(2)}) collective-permute-start(bf16[128,128]{1,0:T(8,128)(2,1)S(1)} %get-tuple-element.32), channel_id=1, source_target_pairs={{0,24},{8,0},{16,8},{24,16},{1,25},{9,1},{17,9},{25,17},{2,26},{10... | collective-permute-start | bytes 98312 | tf_op jit(solution)/shard_map/ppermute | solution.py:267
  12.3 11.3 %copy-start.3 = (bf16[1,128,128]{2,1,0:T(8,128)(2,1)S(1)}, bf16[1,128,128]{2,1,0:T(8,128)(2,1)}, u32[]{:S(2)}) copy-start(bf16[1,128,128]{2,1,0:T(8,128)(2,1)} %refs_2_.11) | copy-start | bytes 98308
  12.3 11.3 %copy-start.4 = (bf16[64,128]{1,0:T(8,128)(2,1)S(1)}, bf16[64,128]{1,0:T(8,128)(2,1)}, u32[]{:S(2)}) copy-start(bf16[64,128]{1,0:T(8,128)(2,1)} %refs_1_.9) | copy-start | bytes 49156
  13.6 3.7 %collective-permute-start.5 = (bf16[256,128]{1,0:T(8,128)(2,1)S(1)}, bf16[256,128]{1,0:T(8,128)(2,1)S(1)}, u32[]{:S(2)}, u32[]{:S(2)}) collective-permute-start(bf16[256,128]{1,0:T(8,128)(2,1)S(1)} %pad_maximum_fusion.refs_0_), channel_id=1, source_target_pairs={{0,6},{2,0},{4,2},{6,4},{1,7},{3,1},{5,3},{7,5},{8,14},{10,8},{12,... | collective-permute-start | bytes 196616 | tf_op jit(solution)/shard_map/ppermute | solution.py:267
  13.6 5.7 %collective-permute-start.4 = (bf16[256,128]{1,0:T(8,128)(2,1)S(1)}, bf16[256,128]{1,0:T(8,128)(2,1)S(1)}, u32[]{:S(2)}, u32[]{:S(2)}) collective-permute-start(bf16[256,128]{1,0:T(8,128)(2,1)S(1)} %pad_maximum_fusion.refs_0_), channel_id=1, source_target_pairs={{0,4},{2,6},{4,0},{6,2},{1,5},{3,7},{5,1},{7,3},{8,12},{10,14},{12... | collective-permute-start | bytes 196616 | tf_op jit(solution)/shard_map/ppermute | solution.py:267
  15.2 4.3 %collective-permute-start.3 = (bf16[256,128]{1,0:T(8,128)(2,1)S(1)}, bf16[256,128]{1,0:T(8,128)(2,1)S(1)}, u32[]{:S(2)}, u32[]{:S(2)}) collective-permute-start(bf16[256,128]{1,0:T(8,128)(2,1)S(1)} %pad_maximum_fusion.refs_0_), channel_id=1, source_target_pairs={{0,2},{2,4},{4,6},{6,0},{1,3},{3,5},{5,7},{7,1},{8,10},{10,12},{12... | collective-permute-start | bytes 196616 | tf_op jit(solution)/shard_map/ppermute | solution.py:267
  19.8 3.8 %collective-permute-start.6 = (bf16[64,128]{1,0:T(8,128)(2,1)S(1)}, bf16[64,128]{1,0:T(8,128)(2,1)S(1)}, u32[]{:S(2)}, u32[]{:S(2)}) collective-permute-start(bf16[64,128]{1,0:T(8,128)(2,1)S(1)} %get-tuple-element.43), channel_id=1, source_target_pairs={{0,1},{1,0},{2,3},{3,2},{4,5},{5,4},{6,7},{7,6},{8,9},{9,8},{10,11... | collective-permute-start | bytes 49160 | tf_op jit(solution)/shard_map/ppermute | solution.py:267
  23.8 5.8 %collective-permute-start.7 = (bf16[128,128]{1,0:T(8,128)(2,1)S(1)}, bf16[128,128]{1,0:T(8,128)(2,1)S(1)}, u32[]{:S(2)}, u32[]{:S(2)}) collective-permute-start(bf16[128,128]{1,0:T(8,128)(2,1)S(1)} %get-tuple-element.45), channel_id=1, source_target_pairs={{0,8},{8,16},{16,24},{24,0},{1,9},{9,17},{17,25},{25,1},{2,10},{10... | collective-permute-start | bytes 98312 | tf_op jit(solution)/shard_map/ppermute | solution.py:267
  24.0 6.1 %collective-permute-start.8 = (bf16[128,128]{1,0:T(8,128)(2,1)S(1)}, bf16[128,128]{1,0:T(8,128)(2,1)S(1)}, u32[]{:S(2)}, u32[]{:S(2)}) collective-permute-start(bf16[128,128]{1,0:T(8,128)(2,1)S(1)} %get-tuple-element.46), channel_id=1, source_target_pairs={{0,16},{8,24},{16,0},{24,8},{1,17},{9,25},{17,1},{25,9},{2,18},{10... | collective-permute-start | bytes 98312 | tf_op jit(solution)/shard_map/ppermute | solution.py:267
  27.5 3.9 %collective-permute-start.9 = (bf16[128,128]{1,0:T(8,128)(2,1)S(1)}, bf16[128,128]{1,0:T(8,128)(2,1)S(1)}, u32[]{:S(2)}, u32[]{:S(2)}) collective-permute-start(bf16[128,128]{1,0:T(8,128)(2,1)S(1)} %get-tuple-element.47), channel_id=1, source_target_pairs={{0,24},{8,0},{16,8},{24,16},{1,25},{9,1},{17,9},{25,17},{2,26},{10... | collective-permute-start | bytes 98312 | tf_op jit(solution)/shard_map/ppermute | solution.py:267
  31.4 2.6 %collective-permute-start.12 = (bf16[256,128]{1,0:T(8,128)(2,1)S(1)}, bf16[256,128]{1,0:T(8,128)(2,1)S(1)}, u32[]{:S(2)}, u32[]{:S(2)}) collective-permute-start(bf16[256,128]{1,0:T(8,128)(2,1)S(1)} %pad_maximum_fusion.1.refs_0_), channel_id=1, source_target_pairs={{0,6},{2,0},{4,2},{6,4},{1,7},{3,1},{5,3},{7,5},{8,14},{10,8},{12,... | collective-permute-start | bytes 196616 | tf_op jit(solution)/shard_map/ppermute | solution.py:267
  31.5 5.0 %collective-permute-start.11 = (bf16[256,128]{1,0:T(8,128)(2,1)S(1)}, bf16[256,128]{1,0:T(8,128)(2,1)S(1)}, u32[]{:S(2)}, u32[]{:S(2)}) collective-permute-start(bf16[256,128]{1,0:T(8,128)(2,1)S(1)} %pad_maximum_fusion.1.refs_0_), channel_id=1, source_target_pairs={{0,4},{2,6},{4,0},{6,2},{1,5},{3,7},{5,1},{7,3},{8,12},{10,14},{12... | collective-permute-start | bytes 196616 | tf_op jit(solution)/shard_map/ppermute | solution.py:267
  32.4 4.3 %collective-permute-start.10 = (bf16[256,128]{1,0:T(8,128)(2,1)S(1)}, bf16[256,128]{1,0:T(8,128)(2,1)S(1)}, u32[]{:S(2)}, u32[]{:S(2)}) collective-permute-start(bf16[256,128]{1,0:T(8,128)(2,1)S(1)} %pad_maximum_fusion.1.refs_0_), channel_id=1, source_target_pairs={{0,2},{2,4},{4,6},{6,0},{1,3},{3,5},{5,7},{7,1},{8,10},{10,12},{12... | collective-permute-start | bytes 196616 | tf_op jit(solution)/shard_map/ppermute | solution.py:267
  37.0 3.8 %collective-permute-start.13 = (bf16[64,128]{1,0:T(8,128)(2,1)S(1)}, bf16[64,128]{1,0:T(8,128)(2,1)S(1)}, u32[]{:S(2)}, u32[]{:S(2)}) collective-permute-start(bf16[64,128]{1,0:T(8,128)(2,1)S(1)} %get-tuple-element.53), channel_id=1, source_target_pairs={{0,1},{1,0},{2,3},{3,2},{4,5},{5,4},{6,7},{7,6},{8,9},{9,8},{10,11... | collective-permute-start | bytes 49160 | tf_op jit(solution)/shard_map/ppermute | solution.py:267

commit v3 on v2

v3 whole, which is shorter than its diff:
```python
import functools

import jax
import jax.numpy as jnp
from jax import lax
from jax.experimental import pallas as pl
from jax.experimental.pallas import tpu as pltpu
from jax.sharding import PartitionSpec as P

UNROLL = 16
INTEGRAL_COST = 10**9
STEP_COST = 10**9
F32 = jnp.float32
HALF = jnp.bfloat16


def by_rows(a, b):
    return lax.dot_general(a, b, (((1,), (1,)), ((), ())), preferred_element_type=F32)


def by_cols(a, b):
    return lax.dot_general(a, b, (((1,), (0,)), ((), ())), preferred_element_type=F32)


def block(start, size):
    return pl.ds(pl.multiple_of(start * size, size), size)


def slot_of(index, here, count):
    return lax.rem(index - here + count, count)


def pair_size(rows):
    return 2 if rows % 2 == 0 else 1


def block_row(read, blocks, columns, row):
    terms = blocks.shape[1]
    field = jnp.concatenate([read(columns[n, row]) for n in range(terms)], axis=1)
    inverse = jnp.concatenate([blocks[row, n] for n in range(terms)], axis=1)
    return by_rows(field, inverse)


def add_traces(total, boundary, coupling, trace_map, bnd_count, axis):
    count = total.shape[0]
    bs = coupling.shape[-1]
    subs = total.shape[2] // bs
    here = lax.axis_index(axis)
    for j in range(coupling.shape[0]):
        alive = (j < bnd_count[0]).astype(F32)
        contrib = by_cols(boundary(j), coupling[j]) * alive
        target = trace_map[j]
        slot = slot_of(target // subs, here, count)
        where = (slot, slice(None), block(lax.rem(target, subs), bs))
        total[where] = total[where] + contrib


def residual_blocks(resid, vol_rhs, group, coupling, trace_map, bnd_count, axis, count, stride):
    bs = coupling.shape[-1]
    angles = vol_rhs.shape[0]
    subs = group.shape[1] // bs
    here = lax.axis_index(axis)
    for j in range(coupling.shape[0]):
        alive = (j < bnd_count[0]).astype(F32)
        target = trace_map[j]
        slot = slot_of(here, target // subs, count)
        picked = group[block(slot * stride, angles), block(lax.rem(target, subs), bs)]
        current = by_rows(picked, coupling[j]) * alive
        rhs = vol_rhs[:, j * bs : (j + 1) * bs].astype(F32)
        resid[j] = (rhs - current).astype(HALF)


def send_out(payloads, half, total):
    rows = half.shape[0]
    for k, payload in enumerate(payloads):
        payload[0:rows, :] = half
        payload[rows:, :] = total[k + 1].astype(HALF)


def start_kernel(axis, outs, kept, refs):
    bnd_count, operands, refs = refs[0], refs[1 : 8 + kept], refs[8 + kept :]
    half_out, own_trace, *payloads = refs[:outs]
    copied, refs = refs[outs : outs + kept + 2], refs[outs + kept + 2 :]
    surf_rhs, surf_inverse, vol_rhs, blocks, coupling, columns, trace_map, total, sems = refs
    slots = coupling.shape[0]
    bs = coupling.shape[-1]
    count = iter(range(sems.shape[0]))

    def copy(source, to):
        started = pltpu.make_async_copy(source, to, sems.at[next(count)])
        started.start()
        return started

    tables = [copy(operands[5 + i], t) for i, t in enumerate((columns, trace_map))]
    first = [copy(operands[0], surf_rhs), copy(operands[1], surf_inverse)]
    tables.append(copy(operands[2], vol_rhs))
    rows = [copy(operands[3].at[j], blocks.at[j]) for j in range(slots)]
    last = copy(operands[4], coupling)
    later = [copy(operands[5 + i], t) for i, t in enumerate(copied)]
    total[...] = jnp.zeros_like(total)
    for c in first:
        c.wait()
    for b in range(surf_inverse.shape[0]):
        cols = slice(b * bs, (b + 1) * bs)
        half_out[:, cols] = by_rows(surf_rhs[:, cols], surf_inverse[b]).astype(HALF)
    for c in tables:
        c.wait()
    solved = []
    for j in range(slots):
        rows[j].wait()
        read = lambda col: vol_rhs[:, block(col, bs)]
        solved.append(block_row(read, blocks, columns, j).astype(HALF))
    last.wait()
    add_traces(total, lambda j: solved[j], coupling, trace_map, bnd_count, axis)
    own_trace[...] = total[0]
    send_out(payloads, half_out[...], total)
    for c in later:
        c.wait()


def boundary_kernel(axis, refs):
    (group, vol_rhs, blocks, coupling, columns, trace_map, bnd_count, total, field) = refs
    bs = coupling.shape[-1]
    slots = coupling.shape[0]
    count = total.shape[0]
    for b in range(slots, vol_rhs.shape[1] // bs):
        field[b] = vol_rhs[:, b * bs : (b + 1) * bs]
    residual_blocks(field, vol_rhs, group, coupling, trace_map, bnd_count, axis, count, 1)
    total[...] = jnp.zeros_like(total)

    def boundary(j):
        return block_row(lambda col: field[col], blocks, columns, j).astype(HALF)

    add_traces(total, boundary, coupling, trace_map, bnd_count, axis)


def early_kernel(axis, count, stride, refs):
    (group, vol_rhs, blocks, coupling, columns, trace_map, bnd_count, early, field) = refs
    bs = coupling.shape[-1]
    for b in range(coupling.shape[0], vol_rhs.shape[1] // bs):
        field[b] = vol_rhs[:, b * bs : (b + 1) * bs]
    residual_blocks(field, vol_rhs, group, coupling, trace_map, bnd_count, axis, count, stride)
    for b in range(early.shape[1] // bs):
        early[:, b * bs : (b + 1) * bs] = block_row(lambda col: field[col], blocks, columns, b)


def late_kernel(refs):
    early, field, blocks, columns, volume = refs
    bs = field.shape[-1]
    first = early.shape[1] // bs
    volume[:, : first * bs] = early[...]
    for b in range(first, blocks.shape[0]):
        volume[:, b * bs : (b + 1) * bs] = block_row(lambda col: field[col], blocks, columns, b)


def dense_kernel(vol_size, row_size, col_size, refs):
    near_blocks, near_cols, far_u, far_v, surf_rhs, surf_inverse, dense, *messages, work = refs
    bs = near_blocks.shape[-1]
    rows = near_blocks.shape[0]
    subs = rows // col_size
    pair = pair_size(row_size)
    chips = row_size // pair
    vol, row, col = (lax.axis_index(name) for name in ("vol", "row", "col"))

    def place(number):
        piece = number // subs
        from_row = lax.rem(piece, row_size)
        chip_slot = slot_of(row // pair, from_row // pair, chips)
        pair_slot = slot_of(lax.rem(row, pair), lax.rem(from_row, pair), pair)
        vol_slot = slot_of(vol, piece // row_size, vol_size)
        slot = (chip_slot * pair + pair_slot) * vol_size + vol_slot
        return slot * subs + lax.rem(number, subs)

    total = vol_size * row_size * subs
    part = total * bs // chips
    for k in range(col_size):
        piece = lax.rem(col + k, col_size)
        for sub in range(subs):
            b = piece * subs + sub
            u = far_u[0, :, block(b, bs)]

            def far(number, _):
                v = far_v[0, 0, :, block(number, bs)]
                work[block(place(number), bs), :] = lax.dot_general(
                    v, u, (((0,), (0,)), ((), ())), preferred_element_type=F32
                )
                return _

            lax.fori_loop(0, total, far, 0, unroll=min(total, UNROLL))
            for n in range(near_blocks.shape[2]):
                where = (block(place(near_cols[b, 0, n]), bs), slice(None))
                work[where] = work[where] + near_blocks[b, 0, n].astype(F32).T
            at = (k * subs + sub) * bs
            dense[:, at : at + bs] = work[...].astype(HALF)
            for a in range(chips):
                if a or k:
                    message = messages[a * col_size + k - 1]
                    message[0:part, sub * bs : (sub + 1) * bs] = work[
                        a * part : (a + 1) * part, :
                    ].astype(HALF)
    angles = surf_rhs.shape[0]
    for k in range(1, col_size):
        message = messages[k - 1]
        message[part : part + angles, :] = surf_rhs[...]
        for sub in range(subs):
            at = part + angles + sub * bs
            message[at : at + bs, sub * bs : (sub + 1) * bs] = surf_inverse[sub]


def add_received(total, received):
    for r in received:
        total = total + r[-total.shape[0] :, :].astype(F32)
    return total


def integral_kernel(row_size, vol_size, col_size, refs):
    groups, refs = refs[:row_size], refs[row_size:]
    dense, own_trace, *received, _, parts, message = refs
    angles, width = own_trace.shape
    field = jnp.concatenate(
        [g[k * angles : (k + 1) * angles, :] for g in groups for k in range(vol_size)], axis=1
    )
    part = by_cols(field, dense[...])
    for k in range(col_size):
        rows = slice(k * angles, (k + 1) * angles)
        term = part[:, k * width : (k + 1) * width]
        if k == 0:
            term = term + add_received(own_trace[...], received)
        parts[rows, :] = term
        message[rows, :] = term.astype(HALF)


def step_kernel(col_size, refs):
    parts, surf_rhs, surf_inverse, total, *refs = refs
    neighbours, refs = refs[: col_size - 1], refs[col_size - 1 :]
    messages, refs = refs[: col_size - 1], refs[col_size - 1 :]
    surface, half, next_trace, *payloads = refs
    angles = surf_rhs.shape[0]
    bs = surf_inverse.shape[-1]
    subs = surf_inverse.shape[0]
    for j in range(col_size):
        taken = parts[j * angles : (j + 1) * angles, :]
        for shift, message in enumerate(messages, 1):
            k = (j + shift) % col_size
            taken = taken + message[k * angles : (k + 1) * angles, :].astype(F32)
        source = None if j == 0 else neighbours[col_size - j - 1]
        first = 0 if j == 0 else source.shape[0] - angles - subs * bs
        for sub in range(subs):
            cols = slice(sub * bs, (sub + 1) * bs)
            if j == 0:
                rhs, inverse = surf_rhs[:, cols], surf_inverse[sub]
            else:
                at = first + angles + sub * bs
                rhs, inverse = source[first : first + angles, cols], source[at : at + bs, cols]
            resid = (rhs.astype(F32) - taken[:, cols]).astype(HALF)
            value = by_rows(rhs, inverse) + by_rows(resid, inverse)
            if j == 0:
                surface[:, cols] = value
            half[j * angles : (j + 1) * angles, cols] = value.astype(HALF)
    next_trace[...] = total[0]
    send_out(payloads, half[...], total)


def last_integral_kernel(pair, vol_size, col_size, chips, refs):
    groups, refs = refs[:pair], refs[pair:]
    dense, refs = refs[0], refs[1:]
    blocks, outs = refs[: chips * col_size - 1], refs[chips * col_size - 1 :][-chips:]
    angles, width = outs[0].shape
    part = dense.shape[0] // chips
    total = jnp.zeros((angles, chips * width), F32)
    for b in range(col_size):
        place = (col_size - b) % col_size
        field = []
        for g in groups:
            for k in range(vol_size):
                at = (k * col_size + place) * angles
                field.append(g[at : at + angles, :])
        matrix = []
        for a in range(chips):
            own = a == 0 and b == 0
            source = dense if own else blocks[a * col_size + b - 1]
            matrix.append(source[0:part, 0:width])
        total = total + by_cols(
            jnp.concatenate(field, axis=1), jnp.concatenate(matrix, axis=1)
        )
    for a, out in enumerate(outs):
        out[...] = total[:, a * width : (a + 1) * width].astype(out.dtype)


def last_kernel(sums, refs):
    surface, surf_rhs, surf_inverse, integral, own_trace, *refs = refs
    sums, received, out = refs[:sums], refs[sums:-1], refs[-1]
    bs = surf_inverse.shape[-1]
    taken = add_received(integral[...] + own_trace[...], received)
    for s in sums:
        taken = taken + s[...].astype(F32)
    resid = (surf_rhs[...].astype(F32) - taken).astype(HALF)
    for b in range(surf_inverse.shape[0]):
        cols = slice(b * bs, (b + 1) * bs)
        out[:, cols] = surface[:, cols] + by_rows(resid[:, cols], surf_inverse[b])


VMEM = pl.BlockSpec(memory_space=pltpu.VMEM)
SMEM = pl.BlockSpec(memory_space=pltpu.SMEM)


ANY = pl.BlockSpec(memory_space=pl.ANY)
HBM = pl.BlockSpec(memory_space=pltpu.HBM)


def call(body, name, in_specs, outs, flops, moved, scratch=()):
    def kernel(*refs):
        body(refs)

    return pl.pallas_call(
        kernel,
        name=name,
        out_shape=outs,
        in_specs=in_specs,
        out_specs=[VMEM] * len(outs),
        scratch_shapes=list(scratch),
        cost_estimate=pl.CostEstimate(flops=flops, bytes_accessed=moved, transcendentals=0),
        compiler_params=pltpu.CompilerParams(vmem_limit_bytes=48 << 20),
    )


def in_hbm(operand):
    return pltpu.with_memory_space_constraint(operand, pltpu.HBM)


def shifted(value, axis, shift):
    size = lax.axis_size(axis)
    return lax.ppermute(value, axis, [(i, (i + shift) % size) for i in range(size)])


def shifted_in_plane(value, chip, core=0, col=0):
    rows, cols = lax.axis_size("row"), lax.axis_size("col")
    pair = pair_size(rows)
    chips = rows // pair
    pairs = []
    for r in range(rows):
        to = (r // pair + chip) % chips * pair + (r % pair + core) % pair
        pairs += [(r * cols + c, to * cols + (c + col) % cols) for c in range(cols)]
    return lax.ppermute(value, ("row", "col"), pairs)


def local(
    vol_rhs,
    surf_rhs,
    vol_blocks,
    vol_cols,
    coupling,
    trace_map,
    bnd_count,
    surf_inverse,
    near_blocks,
    near_cols,
    far_u,
    far_v,
):
    angles, width = surf_rhs.shape
    vol_count, terms, bs, _ = vol_blocks.shape
    slots = coupling.shape[0]
    nv, nr, nc = (lax.axis_size(a) for a in ("vol", "row", "col"))
    piece = (angles, width)
    product = 2 * angles * bs * bs

    def shape(dims, dtype):
        return jax.ShapeDtypeStruct(dims, dtype)

    tables = (vol_cols.T, trace_map)
    payload_shapes = [shape((2 * angles, width), HALF)] * (nv - 1)
    start_shapes = [shape(piece, HALF), shape(piece, F32)] + payload_shapes
    totals = pltpu.VMEM((nv,) + piece, F32)
    field = pltpu.VMEM((vol_count, angles, bs), HALF)

    kept = (near_blocks, near_cols, far_u, far_v, surf_rhs, surf_inverse)
    started = call(
        functools.partial(start_kernel, "vol", len(start_shapes), len(kept)),
        "start",
        [SMEM] + [HBM] * (7 + len(kept)),
        start_shapes + [pltpu.VMEM(a.shape, a.dtype) for a in tables + kept],
        product * slots * (terms + 1),
        2 * bs * bs * slots * (terms + 1),
        [
            pltpu.VMEM(piece, HALF),
            pltpu.VMEM(surf_inverse.shape, HALF),
            pltpu.VMEM(vol_rhs.shape, HALF),
            pltpu.VMEM((slots, terms, bs, bs), HALF),
            pltpu.VMEM(coupling.shape, HALF),
            *(pltpu.SMEM(t.shape, jnp.int32) for t in tables),
            totals,
            pltpu.SemaphoreType.DMA((8 + slots + len(kept),)),
        ],
    )(bnd_count, *map(in_hbm, (surf_rhs, surf_inverse, vol_rhs, vol_blocks, coupling) + tables + kept))
    half, own_trace, *payloads = started[: len(start_shapes)]
    kept = started[len(start_shapes) :]
    tables, kept = (*kept[:2], bnd_count), kept[2:]

    pair = pair_size(nr)
    chips = nr // pair
    part = nv * pair * width
    sizes = [
        part + (angles + surf_inverse.shape[0] * bs if a == 0 else 0)
        for a in range(chips)
        for b in range(nc)
    ]
    dense, *messages = call(
        functools.partial(dense_kernel, nv, nr, nc),
        "dense",
        [VMEM, SMEM] + [VMEM] * 4,
        [shape((nv * nr * width, nc * width), HALF)]
        + [shape((size, width), HALF) for size in sizes[1:]],
        product * nv * nr * nc,
        4 * nv * nr * nc * bs * bs,
        [pltpu.VMEM((nv * nr * width, bs), F32)],
    )(*kept)

    received = [shifted(payloads[k - 1], "vol", k) for k in range(1, nv)]
    blocks = [
        shifted_in_plane(messages[i - 1], chip=-(i // nc), col=i % nc) for i in range(1, nc)
    ]
    group = jnp.concatenate([half] + [r[:angles] for r in received], axis=0)
    group, dense = lax.optimization_barrier((group, dense))
    groups = [group] + [
        shifted_in_plane(group, chip=i // pair, core=i % pair) for i in range(1, nr)
    ]
    (total,) = call(
        functools.partial(boundary_kernel, "vol"),
        "boundary",
        [VMEM] * 4 + [SMEM] * 3,
        [shape((nv,) + piece, F32)],
        product * slots * (terms + 2),
        2 * bs * bs * slots * (terms + 1),
        [field],
    )(group, vol_rhs, vol_blocks, coupling, *tables)
    ahead = [
        shifted_in_plane(messages[i - 1], chip=-(i // nc), col=0) for i in range(nc, nc * chips, nc)
    ]
    parts, message = call(
        functools.partial(integral_kernel, nr, nv, nc),
        "integral",
        [VMEM] * (nr + nv + 1) + [ANY],
        [shape((nc * angles, width), F32), shape((nc * angles, width), HALF)],
        INTEGRAL_COST,
        2 * nv * nr * nc * width * width,
    )(*groups, dense, own_trace, *received, total)
    sums = [shifted(message, "col", k) for k in range(1, nc)]
    parts, *later = lax.optimization_barrier(
        (parts, *(messages[i - 1] for i in range(nc, nc * chips) if i % nc))
    )
    later = iter(later)
    after = {
        i: shifted_in_plane(next(later), chip=-(i // nc), col=i % nc)
        for i in range(nc, nc * chips)
        if i % nc
    }
    surface, half, own_trace, *payloads = call(
        functools.partial(step_kernel, nc),
        "step",
        [VMEM] * (4 + 2 * (nc - 1)),
        [shape(piece, F32), shape((nc * angles, width), HALF), shape(piece, F32)]
        + [shape(((nc + 1) * angles, width), HALF)] * (nv - 1),
        STEP_COST,
        nc << 17,
    )(parts, surf_rhs, surf_inverse, total, *blocks, *sums)

    received = [shifted(payloads[k - 1], "vol", k) for k in range(1, nv)]
    received, ahead = lax.optimization_barrier((received, ahead))
    group = jnp.concatenate([half] + [r[: nc * angles] for r in received], axis=0)
    group, after = lax.optimization_barrier((group, after))
    blocks += [
        after[i] if i % nc else ahead[i // nc - 1] for i in range(nc, nc * chips)
    ]
    groups = [group] + [shifted_in_plane(group, chip=0, core=k) for k in range(1, pair)]
    split = vol_count // 2
    early, residual = call(
        functools.partial(early_kernel, "vol", nv, nc),
        "early_volume",
        [VMEM] * 4 + [SMEM] * 3,
        [shape((angles, split * bs), F32), shape((vol_count, angles, bs), HALF)],
        product * split * terms,
        2 * bs * bs * split * terms,
    )(group, vol_rhs, vol_blocks, coupling, *tables)
    integral, *parts = call(
        functools.partial(last_integral_kernel, pair, nv, nc, chips),
        "last_integral",
        [VMEM] * (pair + chips * nc) + [ANY],
        [shape(piece, F32)] + [shape(piece, HALF)] * (chips - 1),
        product * nv * nr * nc,
        2 * nv * nr * nc * width * width,
    )(*groups, dense, *blocks, early)
    sums = [shifted_in_plane(parts[a - 1], chip=a) for a in range(1, chips)]
    (volume,) = call(
        late_kernel,
        "late_volume",
        [VMEM] * 3 + [SMEM],
        [shape((angles, vol_count * bs), F32)],
        product * (vol_count - split) * terms,
        2 * bs * bs * (vol_count - split) * terms,
    )(early, residual, vol_blocks, tables[0])
    (surface,) = call(
        functools.partial(last_kernel, chips - 1),
        "last",
        [VMEM] * (5 + chips - 1 + nv - 1),
        [shape(piece, F32)],
        product,
        1 << 17,
    )(surface, surf_rhs, surf_inverse, integral, own_trace, *sums, *received)
    return volume, surface


def solution(mesh):
    everywhere = ("vol", "row", "col")
    in_specs = (
        P(None, everywhere),
        P(None, everywhere),
        P(everywhere, None, None, None),
        P(everywhere, None),
        P(everywhere, None, None),
        P(everywhere),
        P(everywhere),
        P(everywhere, None, None),
        P(("vol", "row"), "col", None, None, None),
        P(("vol", "row"), "col", None),
        P("col", None, ("vol", "row")),
        P(("vol", "row"), "col", None, None),
    )
    out_specs = (P(None, everywhere), P(None, everywhere))
    return jax.shard_map(local, mesh=mesh, in_specs=in_specs, out_specs=out_specs, check_vma=False)
```

time: 41.7 us -> 38.8 us (0.930)
  waiting for transfers between devices: 12.5 us -> 7.25 us
  starting transfers between devices: 16.9 us -> 18.9 us
    ppermute x14 -> x7, waiting for transfers between devices: 12.5 us -> 3.07 us  [shifted(): lax.ppermute(value, axis, [(i, (i + shift) % size) for i in range(size)])]
    ppermute x0 -> x8, starting transfers between devices: none -> 6.89 us  [shifted_in_plane(): return lax.ppermute(value, ('row', 'col'), pairs)]
    ppermute x14 -> x7, starting transfers between devices: 16.9 us -> 12 us  [shifted(): lax.ppermute(value, axis, [(i, (i + shift) % size) for i in range(size)])]
    ppermute x0 -> x8, waiting for transfers between devices: none -> 4.18 us  [shifted_in_plane(): return lax.ppermute(value, ('row', 'col'), pairs)]
  transfers between devices with their start and end apart: 14 -> 15, of which waited for: 10 -> 6; matrix products, arithmetic and copies ran while one was open for 0% -> 0% of each run, Pallas kernels for 16% -> 18%
where the time goes in v3:
time: 38.8 us; the launch traced here: 38.6 us
  starting transfers between devices  18.9 us (49%)
  Pallas kernels  10.7 us (28%)
  waiting for transfers between devices  7.25 us (19%)
  between operations  1.62 us (4%)
    ppermute x7, starting transfers between devices, shifted(): lax.ppermute(value, axis, [(i, (i + shift) % size) for i in range(size)])  12 us
    ppermute x8, starting transfers between devices, shifted_in_plane(): return lax.ppermute(value, ('row', 'col'), pairs)  6.89 us
    ppermute x8, waiting for transfers between devices, shifted_in_plane(): return lax.ppermute(value, ('row', 'col'), pairs)  4.18 us
    ppermute x7, waiting for transfers between devices, shifted(): lax.ppermute(value, axis, [(i, (i + shift) % size) for i in range(size)])  3.07 us
    pallas_call x1, Pallas kernels, local(): call(functools.partial(start_kernel, 'vol', len(start_shapes), len(kept))...  2.52 us
    pallas_call x1, Pallas kernels, local(): call(late_kernel, 'late_volume', [VMEM] * 3 + [SMEM], [shape((angles, vol...  2 us
    pallas_call x1, Pallas kernels, local(): call(functools.partial(boundary_kernel, 'vol'), 'boundary', [VMEM] * 4 +...  1.81 us
    pallas_call x1, Pallas kernels, local(): call(functools.partial(early_kernel, 'vol', nv, nc), 'early_volume', [VME...  1.42 us
  transfers between devices with their start and end apart: 15, of which 6 were waited for; matrix products, arithmetic and copies ran while one was open for 0% of the time, Pallas kernels for 18%

profile of v3, /device:TPU:0, one launch (start us, length us, event | category | flops | bytes accessed | tf_op | source)
XLA Modules:
  0.0 38.6 jit_solution(14503205334346033961)
XLA Ops:
  0.6 0.0 copy-start
  0.6 0.0 copy-start.2
  0.7 0.0 copy-start.1
  1.5 2.5 %start.1 = (bf16[64,128]{1,0:T(8,128)(2,1)S(1)}, f32[64,128]{1,0:T(8,128)S(1)}, bf16[128,128]{1,0:T(8,128)(2,1)S(1)}, bf16[128,128]{1,0:T(8,128)(2,1)S(1)}, bf16...) custom-call(s32[1]{0:T(128)S(6)} %copy.14.refs_0_.refs_6_, ...), custom_call_target="tpu_custom_call" | custom-call | flops 67108864 | bytes 1048576 | tf_op jit(solution)/shard_map/start/pallas_call | solution.py:378
  4.0 3.1 %collective-permute-start = (bf16[128,128]{1,0:T(8,128)(2,1)S(1)}, bf16[128,128]{1,0:T(8,128)(2,1)S(1)}, u32[]{:S(2)}, u32[]{:S(2)}) collective-permute-start(bf16[128,128]{1,0:T(8,128)(2,1)S(1)} %get-tuple-element.42), channel_id=1, source_target_pairs={{0,8},{8,16},{16,24},{24,0},{1,9},{9,17},{17,25},{25,1},{2,10},{10... | collective-permute-start | bytes 98312 | tf_op jit(solution)/shard_map/ppermute | solution.py:333
  7.1 2.6 %collective-permute-start.1 = (bf16[128,128]{1,0:T(8,128)(2,1)S(1)}, bf16[128,128]{1,0:T(8,128)(2,1)S(1)}, u32[]{:S(2)}, u32[]{:S(2)}) collective-permute-start(bf16[128,128]{1,0:T(8,128)(2,1)S(1)} %get-tuple-element.43), channel_id=1, source_target_pairs={{0,16},{8,24},{16,0},{24,8},{1,17},{9,25},{17,1},{25,9},{2,18},{10... | collective-permute-start | bytes 98312 | tf_op jit(solution)/shard_map/ppermute | solution.py:333
  9.7 1.3 %collective-permute-start.2 = (bf16[128,128]{1,0:T(8,128)(2,1)S(1)}, bf16[128,128]{1,0:T(8,128)(2,1)S(1)}, u32[]{:S(2)}, u32[]{:S(2)}) collective-permute-start(bf16[128,128]{1,0:T(8,128)(2,1)S(1)} %get-tuple-element.44), channel_id=1, source_target_pairs={{0,24},{8,0},{16,8},{24,16},{1,25},{9,1},{17,9},{25,17},{2,26},{10... | collective-permute-start | bytes 98312 | tf_op jit(solution)/shard_map/ppermute | solution.py:333
  11.0 1.4 %dense.1 = (bf16[2048,256]{1,0:T(8,128)(2,1)S(1)}, bf16[1216,128]{1,0:T(8,128)(2,1)S(1)}, bf16[1024,128]{1,0:T(8,128)(2,1)S(1)}, bf16[1024,128]{1,0:T(8,128)(2,1)S(1)}) custom-call(bf16[2,1,4,128,128]{4,3,2,1,0:T(8,128)(2,1)S(1)} %get-tuple-element.45.refs_0_, s32[2,1,4]{2,1,0:T(1,128)S(1)} %get-tuple-element.46.refs_1_, ...), custom_call_target="tpu_custom_call" | custom-call | flops 67108864 | bytes 2097152 | tf_op jit(solution)/shard_map/dense/pallas_call | solution.py:408
  12.4 1.6 %collective-permute-start.6 = (bf16[1216,128]{1,0:T(8,128)(2,1)S(1)}, bf16[1216,128]{1,0:T(8,128)(2,1)S(1)}, u32[]{:S(2)}, u32[]{:S(2)}) collective-permute-start(bf16[1216,128]{1,0:T(8,128)(2,1)S(1)} %get-tuple-element.60), channel_id=1, source_target_pairs={{0,1},{1,0},{2,3},{3,2},{4,5},{5,4},{6,7},{7,6},{8,9},{9,8},{10,11... | collective-permute-start | bytes 933896 | tf_op jit(solution)/shard_map/ppermute | solution.py:344
  14.0 0.0 collective-permute-done.refs_6_
  14.0 0.0 collective-permute-done.1.refs_7_
  14.0 0.0 collective-permute-done.2.refs_8_
  14.0 0.1 collective-permute-start.5
  14.1 1.6 %collective-permute-start.4 = (bf16[256,128]{1,0:T(8,128)(2,1)S(1)}, bf16[256,128]{1,0:T(8,128)(2,1)S(1)}, u32[]{:S(2)}, u32[]{:S(2)}) collective-permute-start(bf16[256,128]{1,0:T(8,128)(2,1)S(1)} %pad_maximum_fusion.1.refs_0_), channel_id=1, source_target_pairs={{0,4},{1,5},{2,6},{3,7},{4,0},{5,1},{6,2},{7,3},{8,12},{9,13},{10,... | collective-permute-start | bytes 196616 | tf_op jit(solution)/shard_map/ppermute | solution.py:344
  15.7 0.3 collective-permute-start.3
  15.9 1.5 %collective-permute-start.11 = (bf16[1024,128]{1,0:T(8,128)(2,1)S(1)}, bf16[1024,128]{1,0:T(8,128)(2,1)S(1)}, u32[]{:S(2)}, u32[]{:S(2)}) collective-permute-start(bf16[1024,128]{1,0:T(8,128)(2,1)S(1)} %get-tuple-element.66), channel_id=1, source_target_pairs={{0,4},{1,5},{2,6},{3,7},{4,0},{5,1},{6,2},{7,3},{8,12},{9,13},{10,... | collective-permute-start | bytes 786440 | tf_op jit(solution)/shard_map/ppermute | solution.py:344
  17.5 0.0 copy-done
  17.5 0.0 copy-done.2
  17.5 0.0 copy-done.1
  17.5 0.0 copy-start.3
  17.5 0.0 copy-start.4
  17.5 1.8 %boundary.1.refs_9_.refs_3_ = f32[4,64,128]{2,1,0:T(8,128)S(1)} custom-call(bf16[256,128]{1,0:T(8,128)(2,1)S(1)} %pad_maximum_fusion.1.refs_0_, bf16[64,1536]{1,0:T(8,128)(2,1)S(1)} %copy-done.1, bf16[12,7,128,128]{3,2,1,0:T(8,128)(2,1)S(1)} %copy-done, bf16[4,128,128]{2,1,0:T(8,128)(2,1)S(1)} %copy-done.2, s32[7,12]{1,0:T(8,128)S(1)} %get-tuple-element.55.refs_4_.refs_3_, ...), custom_call_target="tpu_custom_call" | custom-call | flops 75497472 | bytes 1048576 | tf_op jit(solution)/shard_map/boundary/pallas_call | solution.py:428
  19.3 0.0 collective-permute-done.5.refs_3_
  19.3 0.6 %collective-permute-done.4.refs_2_ = bf16[256,128]{1,0:T(8,128)(2,1)S(1)} collective-permute-done((bf16[256,128]{1,0:T(8,128)(2,1)S(1)}, bf16[256,128]{1,0:T(8,128)(2,1)S(1)}, u32[]{:S(2)}, u32[]{:S(2)}) %collective-permute-start.4) | collective-permute-done | bytes 65568 | tf_op jit(solution)/shard_map/ppermute | solution.py:344
  19.9 0.0 collective-permute-done.3.refs_1_
  20.0 0.3 integral.1
  20.3 1.1 %collective-permute-start.7 = (bf16[128,128]{1,0:T(8,128)(2,1)S(1)}, bf16[128,128]{1,0:T(8,128)(2,1)S(1)}, u32[]{:S(2)}, u32[]{:S(2)}) collective-permute-start(bf16[128,128]{1,0:T(8,128)(2,1)S(1)} %get-tuple-element.61), channel_id=1, source_target_pairs={{0,1},{1,0},{2,3},{3,2},{4,5},{5,4},{6,7},{7,6},{8,9},{9,8},{10,11... | collective-permute-start | bytes 98312 | tf_op jit(solution)/shard_map/ppermute | solution.py:333
  21.4 1.0 %collective-permute-start.12 = (bf16[1024,128]{1,0:T(8,128)(2,1)S(1)}, bf16[1024,128]{1,0:T(8,128)(2,1)S(1)}, u32[]{:S(2)}, u32[]{:S(2)}) collective-permute-start(bf16[1024,128]{1,0:T(8,128)(2,1)S(1)} %get-tuple-element.70), channel_id=1, source_target_pairs={{0,5},{1,4},{2,7},{3,6},{4,1},{5,0},{6,3},{7,2},{8,13},{9,12},{10,... | collective-permute-start | bytes 786440 | tf_op jit(solution)/shard_map/ppermute | solution.py:344
  22.4 2.0 %collective-permute-done.7.refs_5_ = bf16[128,128]{1,0:T(8,128)(2,1)S(1)} collective-permute-done((bf16[128,128]{1,0:T(8,128)(2,1)S(1)}, bf16[128,128]{1,0:T(8,128)(2,1)S(1)}, u32[]{:S(2)}, u32[]{:S(2)}) %collective-permute-start.7) | collective-permute-done | bytes 32800 | tf_op jit(solution)/shard_map/ppermute | solution.py:333
  24.5 0.0 collective-permute-done.6.refs_4_.refs_3_
  24.5 0.0 copy-done.3
  24.5 0.0 copy-done.4
  24.5 0.2 step.1
  24.7 0.8 %collective-permute-start.8 = (bf16[192,128]{1,0:T(8,128)(2,1)S(1)}, bf16[192,128]{1,0:T(8,128)(2,1)S(1)}, u32[]{:S(2)}, u32[]{:S(2)}) collective-permute-start(bf16[192,128]{1,0:T(8,128)(2,1)S(1)} %get-tuple-element.63), channel_id=1, source_target_pairs={{0,8},{8,16},{16,24},{24,0},{1,9},{9,17},{17,25},{25,1},{2,10},{10... | collective-permute-start | bytes 147464 | tf_op jit(solution)/shard_map/ppermute | solution.py:333
  25.6 2.3 %collective-permute-start.9 = (bf16[192,128]{1,0:T(8,128)(2,1)S(1)}, bf16[192,128]{1,0:T(8,128)(2,1)S(1)}, u32[]{:S(2)}, u32[]{:S(2)}) collective-permute-start(bf16[192,128]{1,0:T(8,128)(2,1)S(1)} %get-tuple-element.64), channel_id=1, source_target_pairs={{0,16},{8,24},{16,0},{24,8},{1,17},{9,25},{17,1},{25,9},{2,18},{10... | collective-permute-start | bytes 147464 | tf_op jit(solution)/shard_map/ppermute | solution.py:333
  27.8 0.8 %collective-permute-start.10 = (bf16[192,128]{1,0:T(8,128)(2,1)S(1)}, bf16[192,128]{1,0:T(8,128)(2,1)S(1)}, u32[]{:S(2)}, u32[]{:S(2)}) collective-permute-start(bf16[192,128]{1,0:T(8,128)(2,1)S(1)} %get-tuple-element.65), channel_id=1, source_target_pairs={{0,24},{8,0},{16,8},{24,16},{1,25},{9,1},{17,9},{25,17},{2,26},{10... | collective-permute-start | bytes 147464 | tf_op jit(solution)/shard_map/ppermute | solution.py:333
  28.6 2.5 %collective-permute-done.11.refs_4_ = bf16[1024,128]{1,0:T(8,128)(2,1)S(1)} collective-permute-done((bf16[1024,128]{1,0:T(8,128)(2,1)S(1)}, bf16[1024,128]{1,0:T(8,128)(2,1)S(1)}, u32[]{:S(2)}, u32[]{:S(2)}) %collective-permute-start.11) | collective-permute-done | bytes 262176 | tf_op jit(solution)/shard_map/ppermute | solution.py:344
  31.1 0.0 collective-permute-done.8.refs_6_
  31.1 0.5 %collective-permute-done.9.refs_7_ = bf16[192,128]{1,0:T(8,128)(2,1)S(1)} collective-permute-done((bf16[192,128]{1,0:T(8,128)(2,1)S(1)}, bf16[192,128]{1,0:T(8,128)(2,1)S(1)}, u32[]{:S(2)}, u32[]{:S(2)}) %collective-permute-start.9) | collective-permute-done | bytes 49184 | tf_op jit(solution)/shard_map/ppermute | solution.py:333
  31.6 0.5 %collective-permute-done.10.refs_8_ = bf16[192,128]{1,0:T(8,128)(2,1)S(1)} collective-permute-done((bf16[192,128]{1,0:T(8,128)(2,1)S(1)}, bf16[192,128]{1,0:T(8,128)(2,1)S(1)}, u32[]{:S(2)}, u32[]{:S(2)}) %collective-permute-start.10) | collective-permute-done | bytes 49184 | tf_op jit(solution)/shard_map/ppermute | solution.py:333
  32.2 0.0 collective-permute-done.12.refs_5_
  32.2 0.1 collective-permute-start.13
  32.3 1.4 %early_volume.1 = (f32[64,768]{1,0:T(8,128)S(1)}, bf16[12,64,128]{2,1,0:T(8,128)(2,1)S(1)}) custom-call(bf16[512,128]{1,0:T(8,128)(2,1)S(1)} %pad_maximum_fusion.refs_0_, bf16[64,1536]{1,0:T(8,128)(2,1)S(1)} %copy-done.1, bf16[12,7,128,128]{3,2,1,0:T(8,128)(2,1)S(1)} %copy-done, bf16[4,128,128]{2,1,0:T(8,128)(2,1)S(1)} %copy-done.2, ...), custom_call_target="tpu_custom_call" | custom-call | flops 88080384 | bytes 1376256 | tf_op jit(solution)/shard_map/early_volume/pallas_call | solution.py:477
  33.7 0.0 collective-permute-done.13.refs_1_
  33.7 0.3 last_integral.1
  34.0 0.8 %collective-permute-start.14 = (bf16[64,128]{1,0:T(8,128)(2,1)S(1)}, bf16[64,128]{1,0:T(8,128)(2,1)S(1)}, u32[]{:S(2)}, u32[]{:S(2)}) collective-permute-start(bf16[64,128]{1,0:T(8,128)(2,1)S(1)} %get-tuple-element.79), channel_id=1, source_target_pairs={{0,4},{1,5},{2,6},{3,7},{4,0},{5,1},{6,2},{7,3},{8,12},{9,13},{10,... | collective-permute-start | bytes 49160 | tf_op jit(solution)/shard_map/ppermute | solution.py:344
  34.8 2.0 %late_volume.1 = f32[64,1536]{1,0:T(8,128)} custom-call(f32[64,768]{1,0:T(8,128)S(1)} %get-tuple-element.72.refs_0_.refs_6_, bf16[12,64,128]{2,1,0:T(8,128)(2,1)S(1)} %get-tuple-element.73.refs_1_, bf16[12,7,128,128]{3,2,1,0:T(8,128)(2,1)S(1)} %copy-done, s32[7,12]{1,0:T(8,128)S(1)} %get-tuple-element.55.refs_4_.refs_3_), custom_call_target="tpu_custom_call" | custom-call | flops 88080384 | bytes 1376256 | tf_op jit(solution)/shard_map/late_volume/pallas_call | solution.py:494
  36.8 1.0 %collective-permute-done.14.refs_5_ = bf16[64,128]{1,0:T(8,128)(2,1)S(1)} collective-permute-done((bf16[64,128]{1,0:T(8,128)(2,1)S(1)}, bf16[64,128]{1,0:T(8,128)(2,1)S(1)}, u32[]{:S(2)}, u32[]{:S(2)}) %collective-permute-start.14) | collective-permute-done | bytes 16416 | tf_op jit(solution)/shard_map/ppermute | solution.py:344
  37.8 0.8 %last.1 = f32[64,128]{1,0:T(8,128)} custom-call(f32[64,128]{1,0:T(8,128)S(1)} %get-tuple-element.74.refs_0_, bf16[64,128]{1,0:T(8,128)(2,1)S(1)} %copy-done.4, bf16[1,128,128]{2,1,0:T(8,128)(2,1)S(1)} %copy-done.3, f32[64,128]{1,0:T(8,128)S(1)} %get-tuple-element.77.refs_3_, f32[64,128]{1,0:T(8,128)S(1)} %get-tuple-element.78.refs_4_, ...), custom_call_target="tpu_custom_call" | custom-call | flops 2097152 | bytes 131072 | tf_op jit(solution)/shard_map/last/pallas_call | solution.py:502
  (8 shorter events, 0.0 us)
Async XLA Ops:
  0.6 16.8 %copy-start = (bf16[12,7,128,128]{3,2,1,0:T(8,128)(2,1)S(1)}, bf16[12,7,128,128]{3,2,1,0:T(8,128)(2,1)}, u32[]{:S(2)}) copy-start(bf16[12,7,128,128]{3,2,1,0:T(8,128)(2,1)} %refs_2_.10) | copy-start | bytes 8257540
  0.6 16.8 %copy-start.2 = (bf16[4,128,128]{2,1,0:T(8,128)(2,1)S(1)}, bf16[4,128,128]{2,1,0:T(8,128)(2,1)}, u32[]{:S(2)}) copy-start(bf16[4,128,128]{2,1,0:T(8,128)(2,1)} %refs_3_.5) | copy-start | bytes 393220
  0.7 16.8 %copy-start.1 = (bf16[64,1536]{1,0:T(8,128)(2,1)S(1)}, bf16[64,1536]{1,0:T(8,128)(2,1)}, u32[]{:S(2)}) copy-start(bf16[64,1536]{1,0:T(8,128)(2,1)} %refs_1_.8) | copy-start | bytes 589828
  4.0 10.0 %collective-permute-start = (bf16[128,128]{1,0:T(8,128)(2,1)S(1)}, bf16[128,128]{1,0:T(8,128)(2,1)S(1)}, u32[]{:S(2)}, u32[]{:S(2)}) collective-permute-start(bf16[128,128]{1,0:T(8,128)(2,1)S(1)} %get-tuple-element.42), channel_id=1, source_target_pairs={{0,8},{8,16},{16,24},{24,0},{1,9},{9,17},{17,25},{25,1},{2,10},{10... | collective-permute-start | bytes 98312 | tf_op jit(solution)/shard_map/ppermute | solution.py:333
  7.1 6.9 %collective-permute-start.1 = (bf16[128,128]{1,0:T(8,128)(2,1)S(1)}, bf16[128,128]{1,0:T(8,128)(2,1)S(1)}, u32[]{:S(2)}, u32[]{:S(2)}) collective-permute-start(bf16[128,128]{1,0:T(8,128)(2,1)S(1)} %get-tuple-element.43), channel_id=1, source_target_pairs={{0,16},{8,24},{16,0},{24,8},{1,17},{9,25},{17,1},{25,9},{2,18},{10... | collective-permute-start | bytes 98312 | tf_op jit(solution)/shard_map/ppermute | solution.py:333
  9.7 4.3 %collective-permute-start.2 = (bf16[128,128]{1,0:T(8,128)(2,1)S(1)}, bf16[128,128]{1,0:T(8,128)(2,1)S(1)}, u32[]{:S(2)}, u32[]{:S(2)}) collective-permute-start(bf16[128,128]{1,0:T(8,128)(2,1)S(1)} %get-tuple-element.44), channel_id=1, source_target_pairs={{0,24},{8,0},{16,8},{24,16},{1,25},{9,1},{17,9},{25,17},{2,26},{10... | collective-permute-start | bytes 98312 | tf_op jit(solution)/shard_map/ppermute | solution.py:333
  12.4 12.1 %collective-permute-start.6 = (bf16[1216,128]{1,0:T(8,128)(2,1)S(1)}, bf16[1216,128]{1,0:T(8,128)(2,1)S(1)}, u32[]{:S(2)}, u32[]{:S(2)}) collective-permute-start(bf16[1216,128]{1,0:T(8,128)(2,1)S(1)} %get-tuple-element.60), channel_id=1, source_target_pairs={{0,1},{1,0},{2,3},{3,2},{4,5},{5,4},{6,7},{7,6},{8,9},{9,8},{10,11... | collective-permute-start | bytes 933896 | tf_op jit(solution)/shard_map/ppermute | solution.py:344
  14.0 5.3 %collective-permute-start.5 = (bf16[256,128]{1,0:T(8,128)(2,1)S(1)}, bf16[256,128]{1,0:T(8,128)(2,1)S(1)}, u32[]{:S(2)}, u32[]{:S(2)}) collective-permute-start(bf16[256,128]{1,0:T(8,128)(2,1)S(1)} %pad_maximum_fusion.1.refs_0_), channel_id=1, source_target_pairs={{0,6},{1,7},{2,4},{3,5},{4,2},{5,3},{6,0},{7,1},{8,14},{9,15},{10,... | collective-permute-start | bytes 196616 | tf_op jit(solution)/shard_map/ppermute | solution.py:344
  14.1 5.9 %collective-permute-start.4 = (bf16[256,128]{1,0:T(8,128)(2,1)S(1)}, bf16[256,128]{1,0:T(8,128)(2,1)S(1)}, u32[]{:S(2)}, u32[]{:S(2)}) collective-permute-start(bf16[256,128]{1,0:T(8,128)(2,1)S(1)} %pad_maximum_fusion.1.refs_0_), channel_id=1, source_target_pairs={{0,4},{1,5},{2,6},{3,7},{4,0},{5,1},{6,2},{7,3},{8,12},{9,13},{10,... | collective-permute-start | bytes 196616 | tf_op jit(solution)/shard_map/ppermute | solution.py:344
  15.7 4.3 %collective-permute-start.3 = (bf16[256,128]{1,0:T(8,128)(2,1)S(1)}, bf16[256,128]{1,0:T(8,128)(2,1)S(1)}, u32[]{:S(2)}, u32[]{:S(2)}) collective-permute-start(bf16[256,128]{1,0:T(8,128)(2,1)S(1)} %pad_maximum_fusion.1.refs_0_), channel_id=1, source_target_pairs={{0,2},{1,3},{2,0},{3,1},{4,6},{5,7},{6,4},{7,5},{8,10},{9,11},{10,... | collective-permute-start | bytes 196616 | tf_op jit(solution)/shard_map/ppermute | solution.py:344
  15.9 15.2 %collective-permute-start.11 = (bf16[1024,128]{1,0:T(8,128)(2,1)S(1)}, bf16[1024,128]{1,0:T(8,128)(2,1)S(1)}, u32[]{:S(2)}, u32[]{:S(2)}) collective-permute-start(bf16[1024,128]{1,0:T(8,128)(2,1)S(1)} %get-tuple-element.66), channel_id=1, source_target_pairs={{0,4},{1,5},{2,6},{3,7},{4,0},{5,1},{6,2},{7,3},{8,12},{9,13},{10,... | collective-permute-start | bytes 786440 | tf_op jit(solution)/shard_map/ppermute | solution.py:344
  17.5 7.0 %copy-start.3 = (bf16[1,128,128]{2,1,0:T(8,128)(2,1)S(1)}, bf16[1,128,128]{2,1,0:T(8,128)(2,1)}, u32[]{:S(2)}) copy-start(bf16[1,128,128]{2,1,0:T(8,128)(2,1)} %refs_2_.11) | copy-start | bytes 98308
  17.5 7.0 %copy-start.4 = (bf16[64,128]{1,0:T(8,128)(2,1)S(1)}, bf16[64,128]{1,0:T(8,128)(2,1)}, u32[]{:S(2)}) copy-start(bf16[64,128]{1,0:T(8,128)(2,1)} %refs_1_.9) | copy-start | bytes 49156
  20.3 4.2 %collective-permute-start.7 = (bf16[128,128]{1,0:T(8,128)(2,1)S(1)}, bf16[128,128]{1,0:T(8,128)(2,1)S(1)}, u32[]{:S(2)}, u32[]{:S(2)}) collective-permute-start(bf16[128,128]{1,0:T(8,128)(2,1)S(1)} %get-tuple-element.61), channel_id=1, source_target_pairs={{0,1},{1,0},{2,3},{3,2},{4,5},{5,4},{6,7},{7,6},{8,9},{9,8},{10,11... | collective-permute-start | bytes 98312 | tf_op jit(solution)/shard_map/ppermute | solution.py:333
  21.4 10.8 %collective-permute-start.12 = (bf16[1024,128]{1,0:T(8,128)(2,1)S(1)}, bf16[1024,128]{1,0:T(8,128)(2,1)S(1)}, u32[]{:S(2)}, u32[]{:S(2)}) collective-permute-start(bf16[1024,128]{1,0:T(8,128)(2,1)S(1)} %get-tuple-element.70), channel_id=1, source_target_pairs={{0,5},{1,4},{2,7},{3,6},{4,1},{5,0},{6,3},{7,2},{8,13},{9,12},{10,... | collective-permute-start | bytes 786440 | tf_op jit(solution)/shard_map/ppermute | solution.py:344
  24.7 6.4 %collective-permute-start.8 = (bf16[192,128]{1,0:T(8,128)(2,1)S(1)}, bf16[192,128]{1,0:T(8,128)(2,1)S(1)}, u32[]{:S(2)}, u32[]{:S(2)}) collective-permute-start(bf16[192,128]{1,0:T(8,128)(2,1)S(1)} %get-tuple-element.63), channel_id=1, source_target_pairs={{0,8},{8,16},{16,24},{24,0},{1,9},{9,17},{17,25},{25,1},{2,10},{10... | collective-permute-start | bytes 147464 | tf_op jit(solution)/shard_map/ppermute | solution.py:333
  25.6 6.1 %collective-permute-start.9 = (bf16[192,128]{1,0:T(8,128)(2,1)S(1)}, bf16[192,128]{1,0:T(8,128)(2,1)S(1)}, u32[]{:S(2)}, u32[]{:S(2)}) collective-permute-start(bf16[192,128]{1,0:T(8,128)(2,1)S(1)} %get-tuple-element.64), channel_id=1, source_target_pairs={{0,16},{8,24},{16,0},{24,8},{1,17},{9,25},{17,1},{25,9},{2,18},{10... | collective-permute-start | bytes 147464 | tf_op jit(solution)/shard_map/ppermute | solution.py:333
  27.8 4.3 %collective-permute-start.10 = (bf16[192,128]{1,0:T(8,128)(2,1)S(1)}, bf16[192,128]{1,0:T(8,128)(2,1)S(1)}, u32[]{:S(2)}, u32[]{:S(2)}) collective-permute-start(bf16[192,128]{1,0:T(8,128)(2,1)S(1)} %get-tuple-element.65), channel_id=1, source_target_pairs={{0,24},{8,0},{16,8},{24,16},{1,25},{9,1},{17,9},{25,17},{2,26},{10... | collective-permute-start | bytes 147464 | tf_op jit(solution)/shard_map/ppermute | solution.py:333
  32.2 1.5 %collective-permute-start.13 = (bf16[512,128]{1,0:T(8,128)(2,1)S(1)}, bf16[512,128]{1,0:T(8,128)(2,1)S(1)}, u32[]{:S(2)}, u32[]{:S(2)}) collective-permute-start(bf16[512,128]{1,0:T(8,128)(2,1)S(1)} %pad_maximum_fusion.refs_0_), channel_id=1, source_target_pairs={{0,2},{1,3},{2,0},{3,1},{4,6},{5,7},{6,4},{7,5},{8,10},{9,11},{10,... | collective-permute-start | bytes 393224 | tf_op jit(solution)/shard_map/ppermute | solution.py:344
  34.0 3.8 %collective-permute-start.14 = (bf16[64,128]{1,0:T(8,128)(2,1)S(1)}, bf16[64,128]{1,0:T(8,128)(2,1)S(1)}, u32[]{:S(2)}, u32[]{:S(2)}) collective-permute-start(bf16[64,128]{1,0:T(8,128)(2,1)S(1)} %get-tuple-element.79), channel_id=1, source_target_pairs={{0,4},{1,5},{2,6},{3,7},{4,0},{5,1},{6,2},{7,3},{8,12},{9,13},{10,... | collective-permute-start | bytes 49160 | tf_op jit(solution)/shard_map/ppermute | solution.py:344

commit v4 on v3

--- a/solution.py
+++ b/solution.py
@@ -80,8 +80,9 @@
 def start_kernel(axis, outs, kept, refs):
     bnd_count, operands, refs = refs[0], refs[1 : 8 + kept], refs[8 + kept :]
     half_out, own_trace, *payloads = refs[:outs]
-    copied, refs = refs[outs : outs + kept + 2], refs[outs + kept + 2 :]
-    surf_rhs, surf_inverse, vol_rhs, blocks, coupling, columns, trace_map, total, sems = refs
+    loaded, copied, refs = refs[outs : outs + 5], refs[outs + 5 : outs + 7 + kept], refs[outs + 7 + kept :]
+    surf_rhs, surf_inverse, vol_rhs, blocks, coupling = loaded
+    columns, trace_map, total, sems = refs
     slots = coupling.shape[0]
     bs = coupling.shape[-1]
     count = iter(range(sems.shape[0]))
@@ -119,14 +120,17 @@
 
 
 def boundary_kernel(axis, refs):
-    (group, vol_rhs, blocks, coupling, columns, trace_map, bnd_count, total, field) = refs
+    group, vol_rhs, blocks, coupling, *tables, bnd_count, total, field, columns, trace_map, sems = refs
+    copies = to_scalars(tables, (columns, trace_map), sems)
     bs = coupling.shape[-1]
     slots = coupling.shape[0]
     count = total.shape[0]
     for b in range(slots, vol_rhs.shape[1] // bs):
         field[b] = vol_rhs[:, b * bs : (b + 1) * bs]
+    total[...] = jnp.zeros_like(total)
+    for c in copies:
+        c.wait()
     residual_blocks(field, vol_rhs, group, coupling, trace_map, bnd_count, axis, count, 1)
-    total[...] = jnp.zeros_like(total)
 
     def boundary(j):
         return block_row(lambda col: field[col], blocks, columns, j).astype(HALF)
@@ -135,26 +139,32 @@
 
 
 def early_kernel(axis, count, stride, refs):
-    (group, vol_rhs, blocks, coupling, columns, trace_map, bnd_count, early, field) = refs
+    group, vol_rhs, blocks, coupling, *tables, bnd_count, early, field, columns, trace_map, sems = refs
+    copies = to_scalars(tables, (columns, trace_map), sems)
     bs = coupling.shape[-1]
     for b in range(coupling.shape[0], vol_rhs.shape[1] // bs):
         field[b] = vol_rhs[:, b * bs : (b + 1) * bs]
+    for c in copies:
+        c.wait()
     residual_blocks(field, vol_rhs, group, coupling, trace_map, bnd_count, axis, count, stride)
     for b in range(early.shape[1] // bs):
         early[:, b * bs : (b + 1) * bs] = block_row(lambda col: field[col], blocks, columns, b)
 
 
 def late_kernel(refs):
-    early, field, blocks, columns, volume = refs
+    early, field, blocks, table, volume, columns, sems = refs
+    (copy,) = to_scalars([table], [columns], sems)
     bs = field.shape[-1]
     first = early.shape[1] // bs
     volume[:, : first * bs] = early[...]
+    copy.wait()
     for b in range(first, blocks.shape[0]):
         volume[:, b * bs : (b + 1) * bs] = block_row(lambda col: field[col], blocks, columns, b)
 
 
 def dense_kernel(vol_size, row_size, col_size, refs):
-    near_blocks, near_cols, far_u, far_v, surf_rhs, surf_inverse, dense, *messages, work = refs
+    near_blocks, table, far_u, far_v, surf_rhs, surf_inverse, dense, *messages, work, near_cols, sems = refs
+    (copy,) = to_scalars([table], [near_cols], sems)
     bs = near_blocks.shape[-1]
     rows = near_blocks.shape[0]
     subs = rows // col_size
@@ -187,6 +197,8 @@
                 return _
 
             lax.fori_loop(0, total, far, 0, unroll=min(total, UNROLL))
+            if k == 0 and sub == 0:
+                copy.wait()
             for n in range(near_blocks.shape[2]):
                 where = (block(place(near_cols[b, 0, n]), bs), slice(None))
                 work[where] = work[where] + near_blocks[b, 0, n].astype(F32).T
@@ -207,6 +219,16 @@
             message[at : at + bs, sub * bs : (sub + 1) * bs] = surf_inverse[sub]
 
 
+def to_scalars(tables, held, sems):
+    copies = [
+        pltpu.make_async_copy(table, to, sems.at[i])
+        for i, (table, to) in enumerate(zip(tables, held, strict=True))
+    ]
+    for c in copies:
+        c.start()
+    return copies
+
+
 def add_received(total, received):
     for r in received:
         total = total + r[-total.shape[0] :, :].astype(F32)
@@ -214,7 +236,7 @@
 
 
 def integral_kernel(row_size, vol_size, col_size, refs):
-    groups, refs = refs[:row_size], refs[row_size:]
+    groups, refs = refs[row_size - 1 :: -1], refs[row_size:]
     dense, own_trace, *received, _, parts, message = refs
     angles, width = own_trace.shape
     field = jnp.concatenate(
@@ -373,29 +395,26 @@
     start_shapes = [shape(piece, HALF), shape(piece, F32)] + payload_shapes
     totals = pltpu.VMEM((nv,) + piece, F32)
     field = pltpu.VMEM((vol_count, angles, bs), HALF)
-
-    kept = (near_blocks, near_cols, far_u, far_v, surf_rhs, surf_inverse)
+    scalars = [pltpu.SMEM(t.shape, jnp.int32) for t in tables] + [pltpu.SemaphoreType.DMA((2,))]
+
+    kept = (near_blocks, near_cols, far_u, far_v)
+    loaded = (surf_rhs, surf_inverse, vol_rhs, jax.ShapeDtypeStruct((slots, terms, bs, bs), HALF), coupling)
     started = call(
         functools.partial(start_kernel, "vol", len(start_shapes), len(kept)),
         "start",
         [SMEM] + [HBM] * (7 + len(kept)),
-        start_shapes + [pltpu.VMEM(a.shape, a.dtype) for a in tables + kept],
+        start_shapes + [pltpu.VMEM(a.shape, a.dtype) for a in loaded + tables + kept],
         product * slots * (terms + 1),
         2 * bs * bs * slots * (terms + 1),
         [
-            pltpu.VMEM(piece, HALF),
-            pltpu.VMEM(surf_inverse.shape, HALF),
-            pltpu.VMEM(vol_rhs.shape, HALF),
-            pltpu.VMEM((slots, terms, bs, bs), HALF),
-            pltpu.VMEM(coupling.shape, HALF),
             *(pltpu.SMEM(t.shape, jnp.int32) for t in tables),
             totals,
             pltpu.SemaphoreType.DMA((8 + slots + len(kept),)),
         ],
     )(bnd_count, *map(in_hbm, (surf_rhs, surf_inverse, vol_rhs, vol_blocks, coupling) + tables + kept))
     half, own_trace, *payloads = started[: len(start_shapes)]
-    kept = started[len(start_shapes) :]
-    tables, kept = (*kept[:2], bnd_count), kept[2:]
+    surf_rhs, surf_inverse, vol_rhs, boundary_blocks, coupling, *kept = started[len(start_shapes) :]
+    tables, kept = (*kept[:2], bnd_count), (*kept[2:], surf_rhs, surf_inverse)
 
     pair = pair_size(nr)
     chips = nr // pair
@@ -408,12 +427,16 @@
     dense, *messages = call(
         functools.partial(dense_kernel, nv, nr, nc),
         "dense",
-        [VMEM, SMEM] + [VMEM] * 4,
+        [VMEM] * 6,
         [shape((nv * nr * width, nc * width), HALF)]
         + [shape((size, width), HALF) for size in sizes[1:]],
         product * nv * nr * nc,
         4 * nv * nr * nc * bs * bs,
-        [pltpu.VMEM((nv * nr * width, bs), F32)],
+        [
+            pltpu.VMEM((nv * nr * width, bs), F32),
+            pltpu.SMEM(near_cols.shape, jnp.int32),
+            pltpu.SemaphoreType.DMA((1,)),
+        ],
     )(*kept)
 
     received = [shifted(payloads[k - 1], "vol", k) for k in range(1, nv)]
@@ -428,12 +451,12 @@
     (total,) = call(
         functools.partial(boundary_kernel, "vol"),
         "boundary",
-        [VMEM] * 4 + [SMEM] * 3,
+        [VMEM] * 6 + [SMEM],
         [shape((nv,) + piece, F32)],
         product * slots * (terms + 2),
         2 * bs * bs * slots * (terms + 1),
-        [field],
-    )(group, vol_rhs, vol_blocks, coupling, *tables)
+        [field] + scalars,
+    )(group, vol_rhs, boundary_blocks, coupling, *tables)
     ahead = [
         shifted_in_plane(messages[i - 1], chip=-(i // nc), col=0) for i in range(nc, nc * chips, nc)
     ]
@@ -444,10 +467,10 @@
         [shape((nc * angles, width), F32), shape((nc * angles, width), HALF)],
         INTEGRAL_COST,
         2 * nv * nr * nc * width * width,
-    )(*groups, dense, own_trace, *received, total)
+    )(*groups[::-1], dense, own_trace, *received, total)
     sums = [shifted(message, "col", k) for k in range(1, nc)]
-    parts, *later = lax.optimization_barrier(
-        (parts, *(messages[i - 1] for i in range(nc, nc * chips) if i % nc))
+    parts, vol_blocks, *later = lax.optimization_barrier(
+        (parts, vol_blocks, *(messages[i - 1] for i in range(nc, nc * chips) if i % nc))
     )
     later = iter(later)
     after = {
@@ -466,21 +489,23 @@
     )(parts, surf_rhs, surf_inverse, total, *blocks, *sums)
 
     received = [shifted(payloads[k - 1], "vol", k) for k in range(1, nv)]
-    received, ahead = lax.optimization_barrier((received, ahead))
+    received, ahead = lax.optimization_barrier((received[1:] + received[:1], ahead))
+    received = received[-1:] + received[:-1]
     group = jnp.concatenate([half] + [r[: nc * angles] for r in received], axis=0)
     group, after = lax.optimization_barrier((group, after))
     blocks += [
         after[i] if i % nc else ahead[i // nc - 1] for i in range(nc, nc * chips)
     ]
     groups = [group] + [shifted_in_plane(group, chip=0, core=k) for k in range(1, pair)]
-    split = vol_count // 2
+    split = vol_count // 3
     early, residual = call(
         functools.partial(early_kernel, "vol", nv, nc),
         "early_volume",
-        [VMEM] * 4 + [SMEM] * 3,
+        [VMEM] * 6 + [SMEM],
         [shape((angles, split * bs), F32), shape((vol_count, angles, bs), HALF)],
         product * split * terms,
         2 * bs * bs * split * terms,
+        scalars,
     )(group, vol_rhs, vol_blocks, coupling, *tables)
     integral, *parts = call(
         functools.partial(last_integral_kernel, pair, nv, nc, chips),
@@ -494,10 +519,11 @@
     (volume,) = call(
         late_kernel,
         "late_volume",
-        [VMEM] * 3 + [SMEM],
+        [VMEM] * 4,
         [shape((angles, vol_count * bs), F32)],
         product * (vol_count - split) * terms,
         2 * bs * bs * (vol_count - split) * terms,
+        [scalars[0], pltpu.SemaphoreType.DMA((1,))],
     )(early, residual, vol_blocks, tables[0])
     (surface,) = call(
         functools.partial(last_kernel, chips - 1),

time: 38.8 us -> 38.2 us (0.985)
  no operation moved by 1% of the time
where the time goes in v4:
time: 38.2 us; the launch traced here: 38.1 us
  starting transfers between devices  18.9 us (49%)
  Pallas kernels  10.5 us (27%)
  waiting for transfers between devices  7.21 us (19%)
  between operations  1.45 us (4%)
    ppermute x7, starting transfers between devices, shifted(): lax.ppermute(value, axis, [(i, (i + shift) % size) for i in range(size)])  12.2 us
    ppermute x8, starting transfers between devices, shifted_in_plane(): return lax.ppermute(value, ('row', 'col'), pairs)  6.69 us
    ppermute x8, waiting for transfers between devices, shifted_in_plane(): return lax.ppermute(value, ('row', 'col'), pairs)  4.27 us
    ppermute x7, waiting for transfers between devices, shifted(): lax.ppermute(value, axis, [(i, (i + shift) % size) for i in range(size)])  2.94 us
    pallas_call x1, Pallas kernels, local(): call(functools.partial(start_kernel, 'vol', len(start_shapes), len(kept))...  2.42 us
    pallas_call x1, Pallas kernels, local(): call(late_kernel, 'late_volume', [VMEM] * 4, [shape((angles, vol_count *...  2.16 us
    pallas_call x1, Pallas kernels, local(): call(functools.partial(boundary_kernel, 'vol'), 'boundary', [VMEM] * 6 +...  1.83 us
    pallas_call x1, Pallas kernels, local(): call(functools.partial(early_kernel, 'vol', nv, nc), 'early_volume', [VME...  1.27 us
  transfers between devices with their start and end apart: 15, of which 6 were waited for; matrix products, arithmetic and copies ran while one was open for 0% of the time, Pallas kernels for 18%

profile of v4, /device:TPU:0, one launch (start us, length us, event | category | flops | bytes accessed | tf_op | source)
XLA Modules:
  0.0 38.1 jit_solution(17864051079678130078)
XLA Ops:
  1.3 2.4 %start.1 = (bf16[64,128]{1,0:T(8,128)(2,1)S(1)}, f32[64,128]{1,0:T(8,128)S(1)}, bf16[128,128]{1,0:T(8,128)(2,1)S(1)}, bf16[128,128]{1,0:T(8,128)(2,1)S(1)}, bf16...) custom-call(s32[1]{0:T(128)S(6)} %copy.14.refs_0_.refs_6_, ...), custom_call_target="tpu_custom_call" | custom-call | flops 67108864 | bytes 1048576 | tf_op jit(solution)/shard_map/start/pallas_call | solution.py:402
  3.7 3.1 %collective-permute-start = (bf16[128,128]{1,0:T(8,128)(2,1)S(1)}, bf16[128,128]{1,0:T(8,128)(2,1)S(1)}, u32[]{:S(2)}, u32[]{:S(2)}) collective-permute-start(bf16[128,128]{1,0:T(8,128)(2,1)S(1)} %get-tuple-element.46), channel_id=1, source_target_pairs={{0,8},{8,16},{16,24},{24,0},{1,9},{9,17},{17,25},{25,1},{2,10},{10... | collective-permute-start | bytes 98312 | tf_op jit(solution)/shard_map/ppermute | solution.py:355
  6.8 2.6 %collective-permute-start.1 = (bf16[128,128]{1,0:T(8,128)(2,1)S(1)}, bf16[128,128]{1,0:T(8,128)(2,1)S(1)}, u32[]{:S(2)}, u32[]{:S(2)}) collective-permute-start(bf16[128,128]{1,0:T(8,128)(2,1)S(1)} %get-tuple-element.47), channel_id=1, source_target_pairs={{0,16},{8,24},{16,0},{24,8},{1,17},{9,25},{17,1},{25,9},{2,18},{10... | collective-permute-start | bytes 98312 | tf_op jit(solution)/shard_map/ppermute | solution.py:355
  9.4 1.4 %collective-permute-start.2 = (bf16[128,128]{1,0:T(8,128)(2,1)S(1)}, bf16[128,128]{1,0:T(8,128)(2,1)S(1)}, u32[]{:S(2)}, u32[]{:S(2)}) collective-permute-start(bf16[128,128]{1,0:T(8,128)(2,1)S(1)} %get-tuple-element.48), channel_id=1, source_target_pairs={{0,24},{8,0},{16,8},{24,16},{1,25},{9,1},{17,9},{25,17},{2,26},{10... | collective-permute-start | bytes 98312 | tf_op jit(solution)/shard_map/ppermute | solution.py:355
  10.7 1.2 %dense.1 = (bf16[2048,256]{1,0:T(8,128)(2,1)S(1)}, bf16[1216,128]{1,0:T(8,128)(2,1)S(1)}, bf16[1024,128]{1,0:T(8,128)(2,1)S(1)}, bf16[1024,128]{1,0:T(8,128)(2,1)S(1)}) custom-call(bf16[2,1,4,128,128]{4,3,2,1,0:T(8,128)(2,1)S(1)} %get-tuple-element.49.refs_0_, s32[2,1,4]{2,1,0:T(1,128)S(1)} %get-tuple-element.50.refs_1_, ...), custom_call_target="tpu_custom_call" | custom-call | flops 67108864 | bytes 2097152 | tf_op jit(solution)/shard_map/dense/pallas_call | solution.py:427
  12.0 1.6 %collective-permute-start.6 = (bf16[1216,128]{1,0:T(8,128)(2,1)S(1)}, bf16[1216,128]{1,0:T(8,128)(2,1)S(1)}, u32[]{:S(2)}, u32[]{:S(2)}) collective-permute-start(bf16[1216,128]{1,0:T(8,128)(2,1)S(1)} %get-tuple-element.67), channel_id=1, source_target_pairs={{0,1},{1,0},{2,3},{3,2},{4,5},{5,4},{6,7},{7,6},{8,9},{9,8},{10,11... | collective-permute-start | bytes 933896 | tf_op jit(solution)/shard_map/ppermute | solution.py:366
  13.5 0.0 collective-permute-done.refs_6_
  13.5 0.0 collective-permute-done.1.refs_7_
  13.6 0.0 collective-permute-done.2.refs_8_
  13.6 0.1 collective-permute-start.3
  13.7 1.6 %collective-permute-start.4 = (bf16[256,128]{1,0:T(8,128)(2,1)S(1)}, bf16[256,128]{1,0:T(8,128)(2,1)S(1)}, u32[]{:S(2)}, u32[]{:S(2)}) collective-permute-start(bf16[256,128]{1,0:T(8,128)(2,1)S(1)} %pad_maximum_fusion.1.refs_0_.refs_3_), channel_id=1, source_target_pairs={{0,4},{1,5},{2,6},{3,7},{4,0},{5,1},{6,2},{7,3},{8,12},{9,13},{10,... | collective-permute-start | bytes 196616 | tf_op jit(solution)/shard_map/ppermute | solution.py:366
  15.2 0.3 collective-permute-start.5
  15.5 1.5 %collective-permute-start.11 = (bf16[1024,128]{1,0:T(8,128)(2,1)S(1)}, bf16[1024,128]{1,0:T(8,128)(2,1)S(1)}, u32[]{:S(2)}, u32[]{:S(2)}) collective-permute-start(bf16[1024,128]{1,0:T(8,128)(2,1)S(1)} %get-tuple-element.73), channel_id=1, source_target_pairs={{0,4},{1,5},{2,6},{3,7},{4,0},{5,1},{6,2},{7,3},{8,12},{9,13},{10,... | collective-permute-start | bytes 786440 | tf_op jit(solution)/shard_map/ppermute | solution.py:366
  17.0 1.8 %boundary.1.refs_9_.refs_3_ = f32[4,64,128]{2,1,0:T(8,128)S(1)} custom-call(bf16[256,128]{1,0:T(8,128)(2,1)S(1)} %pad_maximum_fusion.1.refs_0_.refs_3_, bf16[64,1536]{1,0:T(8,128)(2,1)S(1)} %get-tuple-element.59.refs_1_, bf16[4,7,128,128]{3,2,1,0:T(8,128)(2,1)S(1)} %get-tuple-element.60.refs_2_, bf16[4,128,128]{2,1,0:T(8,128)(2,1)S(1)} %get-tuple-element.61.refs_3_, ...), custom_call_target="tpu_custom_call" | custom-call | flops 75497472 | bytes 1048576 | tf_op jit(solution)/shard_map/boundary/pallas_call | solution.py:451
  18.9 0.0 collective-permute-done.3.refs_0_
  18.9 0.6 %collective-permute-done.4.refs_1_ = bf16[256,128]{1,0:T(8,128)(2,1)S(1)} collective-permute-done((bf16[256,128]{1,0:T(8,128)(2,1)S(1)}, bf16[256,128]{1,0:T(8,128)(2,1)S(1)}, u32[]{:S(2)}, u32[]{:S(2)}) %collective-permute-start.4) | collective-permute-done | bytes 65568 | tf_op jit(solution)/shard_map/ppermute | solution.py:366
  19.5 0.0 collective-permute-done.5.refs_2_
  19.5 0.3 integral.1
  19.8 0.0 copy-start
  19.8 1.3 %collective-permute-start.7 = (bf16[128,128]{1,0:T(8,128)(2,1)S(1)}, bf16[128,128]{1,0:T(8,128)(2,1)S(1)}, u32[]{:S(2)}, u32[]{:S(2)}) collective-permute-start(bf16[128,128]{1,0:T(8,128)(2,1)S(1)} %get-tuple-element.68), channel_id=1, source_target_pairs={{0,1},{1,0},{2,3},{3,2},{4,5},{5,4},{6,7},{7,6},{8,9},{9,8},{10,11... | collective-permute-start | bytes 98312 | tf_op jit(solution)/shard_map/ppermute | solution.py:355
  21.1 0.9 %collective-permute-start.12 = (bf16[1024,128]{1,0:T(8,128)(2,1)S(1)}, bf16[1024,128]{1,0:T(8,128)(2,1)S(1)}, u32[]{:S(2)}, u32[]{:S(2)}) collective-permute-start(bf16[1024,128]{1,0:T(8,128)(2,1)S(1)} %get-tuple-element.77), channel_id=1, source_target_pairs={{0,5},{1,4},{2,7},{3,6},{4,1},{5,0},{6,3},{7,2},{8,13},{9,12},{10,... | collective-permute-start | bytes 786440 | tf_op jit(solution)/shard_map/ppermute | solution.py:366
  22.0 1.9 %collective-permute-done.7.refs_5_ = bf16[128,128]{1,0:T(8,128)(2,1)S(1)} collective-permute-done((bf16[128,128]{1,0:T(8,128)(2,1)S(1)}, bf16[128,128]{1,0:T(8,128)(2,1)S(1)}, u32[]{:S(2)}, u32[]{:S(2)}) %collective-permute-start.7) | collective-permute-done | bytes 32800 | tf_op jit(solution)/shard_map/ppermute | solution.py:355
  23.9 0.0 collective-permute-done.6.refs_4_.refs_3_
  23.9 0.2 step.1
  24.1 1.0 %collective-permute-start.10 = (bf16[192,128]{1,0:T(8,128)(2,1)S(1)}, bf16[192,128]{1,0:T(8,128)(2,1)S(1)}, u32[]{:S(2)}, u32[]{:S(2)}) collective-permute-start(bf16[192,128]{1,0:T(8,128)(2,1)S(1)} %get-tuple-element.72), channel_id=1, source_target_pairs={{0,8},{8,16},{16,24},{24,0},{1,9},{9,17},{17,25},{25,1},{2,10},{10... | collective-permute-start | bytes 147464 | tf_op jit(solution)/shard_map/ppermute | solution.py:355
  25.1 2.4 %collective-permute-start.8 = (bf16[192,128]{1,0:T(8,128)(2,1)S(1)}, bf16[192,128]{1,0:T(8,128)(2,1)S(1)}, u32[]{:S(2)}, u32[]{:S(2)}) collective-permute-start(bf16[192,128]{1,0:T(8,128)(2,1)S(1)} %get-tuple-element.70), channel_id=1, source_target_pairs={{0,16},{8,24},{16,0},{24,8},{1,17},{9,25},{17,1},{25,9},{2,18},{10... | collective-permute-start | bytes 147464 | tf_op jit(solution)/shard_map/ppermute | solution.py:355
  27.5 0.5 %collective-permute-start.9 = (bf16[192,128]{1,0:T(8,128)(2,1)S(1)}, bf16[192,128]{1,0:T(8,128)(2,1)S(1)}, u32[]{:S(2)}, u32[]{:S(2)}) collective-permute-start(bf16[192,128]{1,0:T(8,128)(2,1)S(1)} %get-tuple-element.71), channel_id=1, source_target_pairs={{0,24},{8,0},{16,8},{24,16},{1,25},{9,1},{17,9},{25,17},{2,26},{10... | collective-permute-start | bytes 147464 | tf_op jit(solution)/shard_map/ppermute | solution.py:355
  28.0 2.7 %collective-permute-done.11.refs_4_ = bf16[1024,128]{1,0:T(8,128)(2,1)S(1)} collective-permute-done((bf16[1024,128]{1,0:T(8,128)(2,1)S(1)}, bf16[1024,128]{1,0:T(8,128)(2,1)S(1)}, u32[]{:S(2)}, u32[]{:S(2)}) %collective-permute-start.11) | collective-permute-done | bytes 262176 | tf_op jit(solution)/shard_map/ppermute | solution.py:366
  30.7 0.0 collective-permute-done.10.refs_6_
  30.7 0.5 %collective-permute-done.8.refs_7_ = bf16[192,128]{1,0:T(8,128)(2,1)S(1)} collective-permute-done((bf16[192,128]{1,0:T(8,128)(2,1)S(1)}, bf16[192,128]{1,0:T(8,128)(2,1)S(1)}, u32[]{:S(2)}, u32[]{:S(2)}) %collective-permute-start.8) | collective-permute-done | bytes 49184 | tf_op jit(solution)/shard_map/ppermute | solution.py:355
  31.2 0.5 %collective-permute-done.9.refs_8_ = bf16[192,128]{1,0:T(8,128)(2,1)S(1)} collective-permute-done((bf16[192,128]{1,0:T(8,128)(2,1)S(1)}, bf16[192,128]{1,0:T(8,128)(2,1)S(1)}, u32[]{:S(2)}, u32[]{:S(2)}) %collective-permute-start.9) | collective-permute-done | bytes 49184 | tf_op jit(solution)/shard_map/ppermute | solution.py:355
  31.8 0.0 collective-permute-done.12.refs_5_
  31.8 0.1 collective-permute-start.13
  31.9 0.0 copy-done
  31.9 1.3 %early_volume.1 = (f32[64,512]{1,0:T(8,128)S(1)}, bf16[12,64,128]{2,1,0:T(8,128)(2,1)S(1)}) custom-call(bf16[512,128]{1,0:T(8,128)(2,1)S(1)} %pad_maximum_fusion.refs_0_, bf16[64,1536]{1,0:T(8,128)(2,1)S(1)} %get-tuple-element.59.refs_1_, bf16[12,7,128,128]{3,2,1,0:T(8,128)(2,1)S(1)} %copy-done, bf16[4,128,128]{2,1,0:T(8,128)(2,1)S(1)} %get-tuple-element.61.refs_3_, ...), custom_call_target="tpu_custom_call" | custom-call | flops 58720256 | bytes 917504 | tf_op jit(solution)/shard_map/early_volume/pallas_call | solution.py:501
  33.1 0.0 collective-permute-done.13.refs_1_
  33.2 0.3 last_integral.1
  33.5 0.7 %collective-permute-start.14 = (bf16[64,128]{1,0:T(8,128)(2,1)S(1)}, bf16[64,128]{1,0:T(8,128)(2,1)S(1)}, u32[]{:S(2)}, u32[]{:S(2)}) collective-permute-start(bf16[64,128]{1,0:T(8,128)(2,1)S(1)} %get-tuple-element.87), channel_id=1, source_target_pairs={{0,4},{1,5},{2,6},{3,7},{4,0},{5,1},{6,2},{7,3},{8,12},{9,13},{10,... | collective-permute-start | bytes 49160 | tf_op jit(solution)/shard_map/ppermute | solution.py:366
  34.2 2.2 %late_volume.1 = f32[64,1536]{1,0:T(8,128)} custom-call(f32[64,512]{1,0:T(8,128)S(1)} %get-tuple-element.80.refs_0_.refs_6_, bf16[12,64,128]{2,1,0:T(8,128)(2,1)S(1)} %get-tuple-element.81.refs_1_, bf16[12,7,128,128]{3,2,1,0:T(8,128)(2,1)S(1)} %copy-done, s32[7,12]{1,0:T(8,128)S(1)} %get-tuple-element.62.refs_4_.refs_3_), custom_call_target="tpu_custom_call" | custom-call | flops 117440512 | bytes 1835008 | tf_op jit(solution)/shard_map/late_volume/pallas_call | solution.py:519
  36.4 0.9 %collective-permute-done.14.refs_5_ = bf16[64,128]{1,0:T(8,128)(2,1)S(1)} collective-permute-done((bf16[64,128]{1,0:T(8,128)(2,1)S(1)}, bf16[64,128]{1,0:T(8,128)(2,1)S(1)}, u32[]{:S(2)}, u32[]{:S(2)}) %collective-permute-start.14) | collective-permute-done | bytes 16416 | tf_op jit(solution)/shard_map/ppermute | solution.py:366
  37.3 0.8 %last.1 = f32[64,128]{1,0:T(8,128)} custom-call(f32[64,128]{1,0:T(8,128)S(1)} %get-tuple-element.82.refs_0_, bf16[64,128]{1,0:T(8,128)(2,1)S(1)} %get-tuple-element.53.refs_4_.refs_1_, bf16[1,128,128]{2,1,0:T(8,128)(2,1)S(1)} %get-tuple-element.54.refs_5_.refs_2_, f32[64,128]{1,0:T(8,128)S(1)} %get-tuple-element.85.refs_3_, ...), custom_call_target="tpu_custom_call" | custom-call | flops 2097152 | bytes 131072 | tf_op jit(solution)/shard_map/last/pallas_call | solution.py:528
  (8 shorter events, 0.0 us)
Async XLA Ops:
  3.7 9.8 %collective-permute-start = (bf16[128,128]{1,0:T(8,128)(2,1)S(1)}, bf16[128,128]{1,0:T(8,128)(2,1)S(1)}, u32[]{:S(2)}, u32[]{:S(2)}) collective-permute-start(bf16[128,128]{1,0:T(8,128)(2,1)S(1)} %get-tuple-element.46), channel_id=1, source_target_pairs={{0,8},{8,16},{16,24},{24,0},{1,9},{9,17},{17,25},{25,1},{2,10},{10... | collective-permute-start | bytes 98312 | tf_op jit(solution)/shard_map/ppermute | solution.py:355
  6.8 6.8 %collective-permute-start.1 = (bf16[128,128]{1,0:T(8,128)(2,1)S(1)}, bf16[128,128]{1,0:T(8,128)(2,1)S(1)}, u32[]{:S(2)}, u32[]{:S(2)}) collective-permute-start(bf16[128,128]{1,0:T(8,128)(2,1)S(1)} %get-tuple-element.47), channel_id=1, source_target_pairs={{0,16},{8,24},{16,0},{24,8},{1,17},{9,25},{17,1},{25,9},{2,18},{10... | collective-permute-start | bytes 98312 | tf_op jit(solution)/shard_map/ppermute | solution.py:355
  9.4 4.2 %collective-permute-start.2 = (bf16[128,128]{1,0:T(8,128)(2,1)S(1)}, bf16[128,128]{1,0:T(8,128)(2,1)S(1)}, u32[]{:S(2)}, u32[]{:S(2)}) collective-permute-start(bf16[128,128]{1,0:T(8,128)(2,1)S(1)} %get-tuple-element.48), channel_id=1, source_target_pairs={{0,24},{8,0},{16,8},{24,16},{1,25},{9,1},{17,9},{25,17},{2,26},{10... | collective-permute-start | bytes 98312 | tf_op jit(solution)/shard_map/ppermute | solution.py:355
  12.0 11.9 %collective-permute-start.6 = (bf16[1216,128]{1,0:T(8,128)(2,1)S(1)}, bf16[1216,128]{1,0:T(8,128)(2,1)S(1)}, u32[]{:S(2)}, u32[]{:S(2)}) collective-permute-start(bf16[1216,128]{1,0:T(8,128)(2,1)S(1)} %get-tuple-element.67), channel_id=1, source_target_pairs={{0,1},{1,0},{2,3},{3,2},{4,5},{5,4},{6,7},{7,6},{8,9},{9,8},{10,11... | collective-permute-start | bytes 933896 | tf_op jit(solution)/shard_map/ppermute | solution.py:366
  13.6 5.3 %collective-permute-start.3 = (bf16[256,128]{1,0:T(8,128)(2,1)S(1)}, bf16[256,128]{1,0:T(8,128)(2,1)S(1)}, u32[]{:S(2)}, u32[]{:S(2)}) collective-permute-start(bf16[256,128]{1,0:T(8,128)(2,1)S(1)} %pad_maximum_fusion.1.refs_0_.refs_3_), channel_id=1, source_target_pairs={{0,6},{1,7},{2,4},{3,5},{4,2},{5,3},{6,0},{7,1},{8,14},{9,15},{10,... | collective-permute-start | bytes 196616 | tf_op jit(solution)/shard_map/ppermute | solution.py:366
  13.7 5.8 %collective-permute-start.4 = (bf16[256,128]{1,0:T(8,128)(2,1)S(1)}, bf16[256,128]{1,0:T(8,128)(2,1)S(1)}, u32[]{:S(2)}, u32[]{:S(2)}) collective-permute-start(bf16[256,128]{1,0:T(8,128)(2,1)S(1)} %pad_maximum_fusion.1.refs_0_.refs_3_), channel_id=1, source_target_pairs={{0,4},{1,5},{2,6},{3,7},{4,0},{5,1},{6,2},{7,3},{8,12},{9,13},{10,... | collective-permute-start | bytes 196616 | tf_op jit(solution)/shard_map/ppermute | solution.py:366
  15.2 4.3 %collective-permute-start.5 = (bf16[256,128]{1,0:T(8,128)(2,1)S(1)}, bf16[256,128]{1,0:T(8,128)(2,1)S(1)}, u32[]{:S(2)}, u32[]{:S(2)}) collective-permute-start(bf16[256,128]{1,0:T(8,128)(2,1)S(1)} %pad_maximum_fusion.1.refs_0_.refs_3_), channel_id=1, source_target_pairs={{0,2},{1,3},{2,0},{3,1},{4,6},{5,7},{6,4},{7,5},{8,10},{9,11},{10,... | collective-permute-start | bytes 196616 | tf_op jit(solution)/shard_map/ppermute | solution.py:366
  15.5 15.2 %collective-permute-start.11 = (bf16[1024,128]{1,0:T(8,128)(2,1)S(1)}, bf16[1024,128]{1,0:T(8,128)(2,1)S(1)}, u32[]{:S(2)}, u32[]{:S(2)}) collective-permute-start(bf16[1024,128]{1,0:T(8,128)(2,1)S(1)} %get-tuple-element.73), channel_id=1, source_target_pairs={{0,4},{1,5},{2,6},{3,7},{4,0},{5,1},{6,2},{7,3},{8,12},{9,13},{10,... | collective-permute-start | bytes 786440 | tf_op jit(solution)/shard_map/ppermute | solution.py:366
  19.8 12.0 %copy-start = (bf16[12,7,128,128]{3,2,1,0:T(8,128)(2,1)S(1)}, bf16[12,7,128,128]{3,2,1,0:T(8,128)(2,1)}, u32[]{:S(2)}) copy-start(bf16[12,7,128,128]{3,2,1,0:T(8,128)(2,1)} %refs_2_.3) | copy-start | bytes 8257540
  19.8 4.1 %collective-permute-start.7 = (bf16[128,128]{1,0:T(8,128)(2,1)S(1)}, bf16[128,128]{1,0:T(8,128)(2,1)S(1)}, u32[]{:S(2)}, u32[]{:S(2)}) collective-permute-start(bf16[128,128]{1,0:T(8,128)(2,1)S(1)} %get-tuple-element.68), channel_id=1, source_target_pairs={{0,1},{1,0},{2,3},{3,2},{4,5},{5,4},{6,7},{7,6},{8,9},{9,8},{10,11... | collective-permute-start | bytes 98312 | tf_op jit(solution)/shard_map/ppermute | solution.py:355
  21.1 10.7 %collective-permute-start.12 = (bf16[1024,128]{1,0:T(8,128)(2,1)S(1)}, bf16[1024,128]{1,0:T(8,128)(2,1)S(1)}, u32[]{:S(2)}, u32[]{:S(2)}) collective-permute-start(bf16[1024,128]{1,0:T(8,128)(2,1)S(1)} %get-tuple-element.77), channel_id=1, source_target_pairs={{0,5},{1,4},{2,7},{3,6},{4,1},{5,0},{6,3},{7,2},{8,13},{9,12},{10,... | collective-permute-start | bytes 786440 | tf_op jit(solution)/shard_map/ppermute | solution.py:366
  24.1 6.6 %collective-permute-start.10 = (bf16[192,128]{1,0:T(8,128)(2,1)S(1)}, bf16[192,128]{1,0:T(8,128)(2,1)S(1)}, u32[]{:S(2)}, u32[]{:S(2)}) collective-permute-start(bf16[192,128]{1,0:T(8,128)(2,1)S(1)} %get-tuple-element.72), channel_id=1, source_target_pairs={{0,8},{8,16},{16,24},{24,0},{1,9},{9,17},{17,25},{25,1},{2,10},{10... | collective-permute-start | bytes 147464 | tf_op jit(solution)/shard_map/ppermute | solution.py:355
  25.1 6.1 %collective-permute-start.8 = (bf16[192,128]{1,0:T(8,128)(2,1)S(1)}, bf16[192,128]{1,0:T(8,128)(2,1)S(1)}, u32[]{:S(2)}, u32[]{:S(2)}) collective-permute-start(bf16[192,128]{1,0:T(8,128)(2,1)S(1)} %get-tuple-element.70), channel_id=1, source_target_pairs={{0,16},{8,24},{16,0},{24,8},{1,17},{9,25},{17,1},{25,9},{2,18},{10... | collective-permute-start | bytes 147464 | tf_op jit(solution)/shard_map/ppermute | solution.py:355
  27.5 4.2 %collective-permute-start.9 = (bf16[192,128]{1,0:T(8,128)(2,1)S(1)}, bf16[192,128]{1,0:T(8,128)(2,1)S(1)}, u32[]{:S(2)}, u32[]{:S(2)}) collective-permute-start(bf16[192,128]{1,0:T(8,128)(2,1)S(1)} %get-tuple-element.71), channel_id=1, source_target_pairs={{0,24},{8,0},{16,8},{24,16},{1,25},{9,1},{17,9},{25,17},{2,26},{10... | collective-permute-start | bytes 147464 | tf_op jit(solution)/shard_map/ppermute | solution.py:355
  31.8 1.4 %collective-permute-start.13 = (bf16[512,128]{1,0:T(8,128)(2,1)S(1)}, bf16[512,128]{1,0:T(8,128)(2,1)S(1)}, u32[]{:S(2)}, u32[]{:S(2)}) collective-permute-start(bf16[512,128]{1,0:T(8,128)(2,1)S(1)} %pad_maximum_fusion.refs_0_), channel_id=1, source_target_pairs={{0,2},{1,3},{2,0},{3,1},{4,6},{5,7},{6,4},{7,5},{8,10},{9,11},{10,... | collective-permute-start | bytes 393224 | tf_op jit(solution)/shard_map/ppermute | solution.py:366
  33.5 3.8 %collective-permute-start.14 = (bf16[64,128]{1,0:T(8,128)(2,1)S(1)}, bf16[64,128]{1,0:T(8,128)(2,1)S(1)}, u32[]{:S(2)}, u32[]{:S(2)}) collective-permute-start(bf16[64,128]{1,0:T(8,128)(2,1)S(1)} %get-tuple-element.87), channel_id=1, source_target_pairs={{0,4},{1,5},{2,6},{3,7},{4,0},{5,1},{6,2},{7,3},{8,12},{9,13},{10,... | collective-permute-start | bytes 49160 | tf_op jit(solution)/shard_map/ppermute | solution.py:366

commit v5 on v4

--- a/solution.py
+++ b/solution.py
@@ -163,7 +163,7 @@
 
 
 def dense_kernel(vol_size, row_size, col_size, refs):
-    near_blocks, table, far_u, far_v, surf_rhs, surf_inverse, dense, *messages, work, near_cols, sems = refs
+    near_blocks, table, far_u, far_v, surf_rhs, surf_inverse, dense, *messages, near_cols, sems = refs
     (copy,) = to_scalars([table], [near_cols], sems)
     bs = near_blocks.shape[-1]
     rows = near_blocks.shape[0]
@@ -183,33 +183,38 @@
 
     total = vol_size * row_size * subs
     part = total * bs // chips
-    for k in range(col_size):
-        piece = lax.rem(col + k, col_size)
-        for sub in range(subs):
-            b = piece * subs + sub
-            u = far_u[0, :, block(b, bs)]
-
-            def far(number, _):
-                v = far_v[0, 0, :, block(number, bs)]
-                work[block(place(number), bs), :] = lax.dot_general(
-                    v, u, (((0,), (0,)), ((), ())), preferred_element_type=F32
-                )
-                return _
-
-            lax.fori_loop(0, total, far, 0, unroll=min(total, UNROLL))
-            if k == 0 and sub == 0:
-                copy.wait()
+    together = 2 - rows % 2
+    for first in range(0, rows, together):
+        numbers = [
+            lax.rem(col + at // subs, col_size) * subs + at % subs
+            for at in range(first, first + together)
+        ]
+        u = jnp.concatenate([far_u[0, :, block(b, bs)] for b in numbers], axis=1)
+        cols = slice(first * bs, (first + together) * bs)
+
+        def far(number, _):
+            v = far_v[0, 0, :, block(number, bs)]
+            dense[block(place(number), bs), cols] = lax.dot_general(
+                v, u, (((0,), (0,)), ((), ())), preferred_element_type=F32
+            ).astype(HALF)
+            return _
+
+        lax.fori_loop(0, total, far, 0, unroll=min(total, UNROLL))
+        if first == 0:
+            copy.wait()
+        for i, b in enumerate(numbers):
+            cols = slice((first + i) * bs, (first + i + 1) * bs)
             for n in range(near_blocks.shape[2]):
-                where = (block(place(near_cols[b, 0, n]), bs), slice(None))
-                work[where] = work[where] + near_blocks[b, 0, n].astype(F32).T
-            at = (k * subs + sub) * bs
-            dense[:, at : at + bs] = work[...].astype(HALF)
-            for a in range(chips):
-                if a or k:
-                    message = messages[a * col_size + k - 1]
-                    message[0:part, sub * bs : (sub + 1) * bs] = work[
-                        a * part : (a + 1) * part, :
-                    ].astype(HALF)
+                where = (block(place(near_cols[b, 0, n]), bs), cols)
+                near = near_blocks[b, 0, n].astype(F32).T
+                dense[where] = (dense[where].astype(F32) + near).astype(HALF)
+    width = subs * bs
+    for a in range(chips):
+        for k in range(col_size):
+            if a or k:
+                messages[a * col_size + k - 1][0:part, :] = dense[
+                    a * part : (a + 1) * part, k * width : (k + 1) * width
+                ]
     angles = surf_rhs.shape[0]
     for k in range(1, col_size):
         message = messages[k - 1]
@@ -236,7 +241,9 @@
 
 
 def integral_kernel(row_size, vol_size, col_size, refs):
-    groups, refs = refs[row_size - 1 :: -1], refs[row_size:]
+    pair = pair_size(row_size)
+    groups = refs[row_size - pair : row_size][::-1] + refs[: row_size - pair]
+    refs = refs[row_size:]
     dense, own_trace, *received, _, parts, message = refs
     angles, width = own_trace.shape
     field = jnp.concatenate(
@@ -433,7 +440,6 @@
         product * nv * nr * nc,
         4 * nv * nr * nc * bs * bs,
         [
-            pltpu.VMEM((nv * nr * width, bs), F32),
             pltpu.SMEM(near_cols.shape, jnp.int32),
             pltpu.SemaphoreType.DMA((1,)),
         ],
@@ -467,7 +473,7 @@
         [shape((nc * angles, width), F32), shape((nc * angles, width), HALF)],
         INTEGRAL_COST,
         2 * nv * nr * nc * width * width,
-    )(*groups[::-1], dense, own_trace, *received, total)
+    )(*groups[pair:], *groups[:pair][::-1], dense, own_trace, *received, total)
     sums = [shifted(message, "col", k) for k in range(1, nc)]
     parts, vol_blocks, *later = lax.optimization_barrier(
         (parts, vol_blocks, *(messages[i - 1] for i in range(nc, nc * chips) if i % nc))

time: 38.2 us -> 37.9 us (level)
  waiting for transfers between devices: 7.21 us -> 6.06 us
  starting transfers between devices: 18.9 us -> 20 us
    ppermute x8, waiting for transfers between devices: 4.27 us -> 3.22 us  [shifted_in_plane(): return lax.ppermute(value, ('row', 'col'), pairs)]
    ppermute x8, starting transfers between devices: 6.69 us -> 7.58 us  [shifted_in_plane(): return lax.ppermute(value, ('row', 'col'), pairs)]
  transfers between devices with their start and end apart: 15 -> 15, of which waited for: 6 -> 7; matrix products, arithmetic and copies ran while one was open for 0% -> 0% of each run, Pallas kernels for 18% -> 18%
where the time goes in v5:
time: 37.9 us; the launch traced here: 37.8 us
  starting transfers between devices  20 us (53%)
  Pallas kernels  10.2 us (27%)
  waiting for transfers between devices  6.06 us (16%)
  between operations  1.42 us (4%)
    ppermute x7, starting transfers between devices, shifted(): lax.ppermute(value, axis, [(i, (i + shift) % size) for i in range(size)])  12.5 us
    ppermute x8, starting transfers between devices, shifted_in_plane(): return lax.ppermute(value, ('row', 'col'), pairs)  7.58 us
    ppermute x8, waiting for transfers between devices, shifted_in_plane(): return lax.ppermute(value, ('row', 'col'), pairs)  3.22 us
    ppermute x7, waiting for transfers between devices, shifted(): lax.ppermute(value, axis, [(i, (i + shift) % size) for i in range(size)])  2.84 us
    pallas_call x1, Pallas kernels, local(): call(functools.partial(start_kernel, 'vol', len(start_shapes), len(kept))...  2.42 us
    pallas_call x1, Pallas kernels, local(): call(late_kernel, 'late_volume', [VMEM] * 4, [shape((angles, vol_count *...  2.16 us
    pallas_call x1, Pallas kernels, local(): call(functools.partial(boundary_kernel, 'vol'), 'boundary', [VMEM] * 6 +...  1.83 us
    pallas_call x1, Pallas kernels, local(): call(functools.partial(early_kernel, 'vol', nv, nc), 'early_volume', [VME...  1.26 us
  transfers between devices with their start and end apart: 15, of which 7 were waited for; matrix products, arithmetic and copies ran while one was open for 0% of the time, Pallas kernels for 18%

profile of v5, /device:TPU:0, one launch (start us, length us, event | category | flops | bytes accessed | tf_op | source)
XLA Modules:
  0.0 37.8 jit_solution(13041059127042125703)
XLA Ops:
  1.3 2.4 %start.1 = (bf16[64,128]{1,0:T(8,128)(2,1)S(1)}, f32[64,128]{1,0:T(8,128)S(1)}, bf16[128,128]{1,0:T(8,128)(2,1)S(1)}, bf16[128,128]{1,0:T(8,128)(2,1)S(1)}, bf16...) custom-call(s32[1]{0:T(128)S(6)} %copy.14.refs_0_.refs_6_, ...), custom_call_target="tpu_custom_call" | custom-call | flops 67108864 | bytes 1048576 | tf_op jit(solution)/shard_map/start/pallas_call | solution.py:409
  3.7 3.1 %collective-permute-start = (bf16[128,128]{1,0:T(8,128)(2,1)S(1)}, bf16[128,128]{1,0:T(8,128)(2,1)S(1)}, u32[]{:S(2)}, u32[]{:S(2)}) collective-permute-start(bf16[128,128]{1,0:T(8,128)(2,1)S(1)} %get-tuple-element.46), channel_id=1, source_target_pairs={{0,8},{8,16},{16,24},{24,0},{1,9},{9,17},{17,25},{25,1},{2,10},{10... | collective-permute-start | bytes 98312 | tf_op jit(solution)/shard_map/ppermute | solution.py:362
  6.8 2.6 %collective-permute-start.1 = (bf16[128,128]{1,0:T(8,128)(2,1)S(1)}, bf16[128,128]{1,0:T(8,128)(2,1)S(1)}, u32[]{:S(2)}, u32[]{:S(2)}) collective-permute-start(bf16[128,128]{1,0:T(8,128)(2,1)S(1)} %get-tuple-element.47), channel_id=1, source_target_pairs={{0,16},{8,24},{16,0},{24,8},{1,17},{9,25},{17,1},{25,9},{2,18},{10... | collective-permute-start | bytes 98312 | tf_op jit(solution)/shard_map/ppermute | solution.py:362
  9.4 1.3 %collective-permute-start.2 = (bf16[128,128]{1,0:T(8,128)(2,1)S(1)}, bf16[128,128]{1,0:T(8,128)(2,1)S(1)}, u32[]{:S(2)}, u32[]{:S(2)}) collective-permute-start(bf16[128,128]{1,0:T(8,128)(2,1)S(1)} %get-tuple-element.48), channel_id=1, source_target_pairs={{0,24},{8,0},{16,8},{24,16},{1,25},{9,1},{17,9},{25,17},{2,26},{10... | collective-permute-start | bytes 98312 | tf_op jit(solution)/shard_map/ppermute | solution.py:362
  10.7 1.0 %dense.1 = (bf16[2048,256]{1,0:T(8,128)(2,1)S(1)}, bf16[1216,128]{1,0:T(8,128)(2,1)S(1)}, bf16[1024,128]{1,0:T(8,128)(2,1)S(1)}, bf16[1024,128]{1,0:T(8,128)(2,1)S(1)}) custom-call(bf16[2,1,4,128,128]{4,3,2,1,0:T(8,128)(2,1)S(1)} %get-tuple-element.49.refs_0_, s32[2,1,4]{2,1,0:T(1,128)S(1)} %get-tuple-element.50.refs_1_, ...), custom_call_target="tpu_custom_call" | custom-call | flops 67108864 | bytes 2097152 | tf_op jit(solution)/shard_map/dense/pallas_call | solution.py:434
  11.7 1.6 %collective-permute-start.6 = (bf16[1216,128]{1,0:T(8,128)(2,1)S(1)}, bf16[1216,128]{1,0:T(8,128)(2,1)S(1)}, u32[]{:S(2)}, u32[]{:S(2)}) collective-permute-start(bf16[1216,128]{1,0:T(8,128)(2,1)S(1)} %get-tuple-element.67), channel_id=1, source_target_pairs={{0,1},{1,0},{2,3},{3,2},{4,5},{5,4},{6,7},{7,6},{8,9},{9,8},{10,11... | collective-permute-start | bytes 933896 | tf_op jit(solution)/shard_map/ppermute | solution.py:373
  13.2 0.0 collective-permute-done.refs_6_
  13.2 0.0 collective-permute-done.1.refs_7_
  13.3 0.0 collective-permute-done.2.refs_8_
  13.3 1.6 %collective-permute-start.3 = (bf16[256,128]{1,0:T(8,128)(2,1)S(1)}, bf16[256,128]{1,0:T(8,128)(2,1)S(1)}, u32[]{:S(2)}, u32[]{:S(2)}) collective-permute-start(bf16[256,128]{1,0:T(8,128)(2,1)S(1)} %pad_maximum_fusion.1.refs_0_.refs_3_), channel_id=1, source_target_pairs={{0,4},{1,5},{2,6},{3,7},{4,0},{5,1},{6,2},{7,3},{8,12},{9,13},{10,... | collective-permute-start | bytes 196616 | tf_op jit(solution)/shard_map/ppermute | solution.py:373
  14.9 0.0 collective-permute-start.4
  14.9 0.6 %collective-permute-start.5 = (bf16[256,128]{1,0:T(8,128)(2,1)S(1)}, bf16[256,128]{1,0:T(8,128)(2,1)S(1)}, u32[]{:S(2)}, u32[]{:S(2)}) collective-permute-start(bf16[256,128]{1,0:T(8,128)(2,1)S(1)} %pad_maximum_fusion.1.refs_0_.refs_3_), channel_id=1, source_target_pairs={{0,2},{1,3},{2,0},{3,1},{4,6},{5,7},{6,4},{7,5},{8,10},{9,11},{10,... | collective-permute-start | bytes 196616 | tf_op jit(solution)/shard_map/ppermute | solution.py:373
  15.5 1.5 %collective-permute-start.11 = (bf16[1024,128]{1,0:T(8,128)(2,1)S(1)}, bf16[1024,128]{1,0:T(8,128)(2,1)S(1)}, u32[]{:S(2)}, u32[]{:S(2)}) collective-permute-start(bf16[1024,128]{1,0:T(8,128)(2,1)S(1)} %get-tuple-element.73), channel_id=1, source_target_pairs={{0,4},{1,5},{2,6},{3,7},{4,0},{5,1},{6,2},{7,3},{8,12},{9,13},{10,... | collective-permute-start | bytes 786440 | tf_op jit(solution)/shard_map/ppermute | solution.py:373
  17.0 1.8 %boundary.1.refs_9_.refs_3_ = f32[4,64,128]{2,1,0:T(8,128)S(1)} custom-call(bf16[256,128]{1,0:T(8,128)(2,1)S(1)} %pad_maximum_fusion.1.refs_0_.refs_3_, bf16[64,1536]{1,0:T(8,128)(2,1)S(1)} %get-tuple-element.59.refs_1_, bf16[4,7,128,128]{3,2,1,0:T(8,128)(2,1)S(1)} %get-tuple-element.60.refs_2_, bf16[4,128,128]{2,1,0:T(8,128)(2,1)S(1)} %get-tuple-element.61.refs_3_, ...), custom_call_target="tpu_custom_call" | custom-call | flops 75497472 | bytes 1048576 | tf_op jit(solution)/shard_map/boundary/pallas_call | solution.py:457
  18.9 0.0 collective-permute-done.3.refs_0_
  18.9 0.2 collective-permute-done.4.refs_1_
  19.0 0.0 collective-permute-done.5.refs_2_
  19.0 0.3 integral.1
  19.4 0.0 copy-start
  19.4 1.6 %collective-permute-start.7 = (bf16[128,128]{1,0:T(8,128)(2,1)S(1)}, bf16[128,128]{1,0:T(8,128)(2,1)S(1)}, u32[]{:S(2)}, u32[]{:S(2)}) collective-permute-start(bf16[128,128]{1,0:T(8,128)(2,1)S(1)} %get-tuple-element.68), channel_id=1, source_target_pairs={{0,1},{1,0},{2,3},{3,2},{4,5},{5,4},{6,7},{7,6},{8,9},{9,8},{10,11... | collective-permute-start | bytes 98312 | tf_op jit(solution)/shard_map/ppermute | solution.py:362
  20.9 0.8 %collective-permute-start.12 = (bf16[1024,128]{1,0:T(8,128)(2,1)S(1)}, bf16[1024,128]{1,0:T(8,128)(2,1)S(1)}, u32[]{:S(2)}, u32[]{:S(2)}) collective-permute-start(bf16[1024,128]{1,0:T(8,128)(2,1)S(1)} %get-tuple-element.77), channel_id=1, source_target_pairs={{0,5},{1,4},{2,7},{3,6},{4,1},{5,0},{6,3},{7,2},{8,13},{9,12},{10,... | collective-permute-start | bytes 786440 | tf_op jit(solution)/shard_map/ppermute | solution.py:373
  21.7 1.6 %collective-permute-done.7.refs_5_ = bf16[128,128]{1,0:T(8,128)(2,1)S(1)} collective-permute-done((bf16[128,128]{1,0:T(8,128)(2,1)S(1)}, bf16[128,128]{1,0:T(8,128)(2,1)S(1)}, u32[]{:S(2)}, u32[]{:S(2)}) %collective-permute-start.7) | collective-permute-done | bytes 32800 | tf_op jit(solution)/shard_map/ppermute | solution.py:362
  23.3 0.0 collective-permute-done.6.refs_4_.refs_3_
  23.3 0.2 step.1
  23.6 0.7 %collective-permute-start.10 = (bf16[192,128]{1,0:T(8,128)(2,1)S(1)}, bf16[192,128]{1,0:T(8,128)(2,1)S(1)}, u32[]{:S(2)}, u32[]{:S(2)}) collective-permute-start(bf16[192,128]{1,0:T(8,128)(2,1)S(1)} %get-tuple-element.72), channel_id=1, source_target_pairs={{0,8},{8,16},{16,24},{24,0},{1,9},{9,17},{17,25},{25,1},{2,10},{10... | collective-permute-start | bytes 147464 | tf_op jit(solution)/shard_map/ppermute | solution.py:362
  24.3 3.0 %collective-permute-start.8 = (bf16[192,128]{1,0:T(8,128)(2,1)S(1)}, bf16[192,128]{1,0:T(8,128)(2,1)S(1)}, u32[]{:S(2)}, u32[]{:S(2)}) collective-permute-start(bf16[192,128]{1,0:T(8,128)(2,1)S(1)} %get-tuple-element.70), channel_id=1, source_target_pairs={{0,16},{8,24},{16,0},{24,8},{1,17},{9,25},{17,1},{25,9},{2,18},{10... | collective-permute-start | bytes 147464 | tf_op jit(solution)/shard_map/ppermute | solution.py:362
  27.3 0.1 collective-permute-start.9
  27.5 2.8 %collective-permute-done.11.refs_4_ = bf16[1024,128]{1,0:T(8,128)(2,1)S(1)} collective-permute-done((bf16[1024,128]{1,0:T(8,128)(2,1)S(1)}, bf16[1024,128]{1,0:T(8,128)(2,1)S(1)}, u32[]{:S(2)}, u32[]{:S(2)}) %collective-permute-start.11) | collective-permute-done | bytes 262176 | tf_op jit(solution)/shard_map/ppermute | solution.py:373
  30.3 0.0 collective-permute-done.10.refs_6_
  30.3 0.6 %collective-permute-done.8.refs_7_ = bf16[192,128]{1,0:T(8,128)(2,1)S(1)} collective-permute-done((bf16[192,128]{1,0:T(8,128)(2,1)S(1)}, bf16[192,128]{1,0:T(8,128)(2,1)S(1)}, u32[]{:S(2)}, u32[]{:S(2)}) %collective-permute-start.8) | collective-permute-done | bytes 49184 | tf_op jit(solution)/shard_map/ppermute | solution.py:362
  30.9 0.5 %collective-permute-done.9.refs_8_ = bf16[192,128]{1,0:T(8,128)(2,1)S(1)} collective-permute-done((bf16[192,128]{1,0:T(8,128)(2,1)S(1)}, bf16[192,128]{1,0:T(8,128)(2,1)S(1)}, u32[]{:S(2)}, u32[]{:S(2)}) %collective-permute-start.9) | collective-permute-done | bytes 49184 | tf_op jit(solution)/shard_map/ppermute | solution.py:362
  31.5 0.0 collective-permute-done.12.refs_5_
  31.5 0.1 collective-permute-start.13
  31.6 0.0 copy-done
  31.6 1.3 %early_volume.1 = (f32[64,512]{1,0:T(8,128)S(1)}, bf16[12,64,128]{2,1,0:T(8,128)(2,1)S(1)}) custom-call(bf16[512,128]{1,0:T(8,128)(2,1)S(1)} %pad_maximum_fusion.refs_0_, bf16[64,1536]{1,0:T(8,128)(2,1)S(1)} %get-tuple-element.59.refs_1_, bf16[12,7,128,128]{3,2,1,0:T(8,128)(2,1)S(1)} %copy-done, bf16[4,128,128]{2,1,0:T(8,128)(2,1)S(1)} %get-tuple-element.61.refs_3_, ...), custom_call_target="tpu_custom_call" | custom-call | flops 58720256 | bytes 917504 | tf_op jit(solution)/shard_map/early_volume/pallas_call | solution.py:507
  32.8 0.1 collective-permute-done.13.refs_1_
  32.9 0.3 last_integral.1
  33.2 1.4 %collective-permute-start.14 = (bf16[64,128]{1,0:T(8,128)(2,1)S(1)}, bf16[64,128]{1,0:T(8,128)(2,1)S(1)}, u32[]{:S(2)}, u32[]{:S(2)}) collective-permute-start(bf16[64,128]{1,0:T(8,128)(2,1)S(1)} %get-tuple-element.87), channel_id=1, source_target_pairs={{0,4},{1,5},{2,6},{3,7},{4,0},{5,1},{6,2},{7,3},{8,12},{9,13},{10,... | collective-permute-start | bytes 49160 | tf_op jit(solution)/shard_map/ppermute | solution.py:373
  34.7 2.2 %late_volume.1 = f32[64,1536]{1,0:T(8,128)} custom-call(f32[64,512]{1,0:T(8,128)S(1)} %get-tuple-element.80.refs_0_.refs_6_, bf16[12,64,128]{2,1,0:T(8,128)(2,1)S(1)} %get-tuple-element.81.refs_1_, bf16[12,7,128,128]{3,2,1,0:T(8,128)(2,1)S(1)} %copy-done, s32[7,12]{1,0:T(8,128)S(1)} %get-tuple-element.62.refs_4_.refs_3_), custom_call_target="tpu_custom_call" | custom-call | flops 117440512 | bytes 1835008 | tf_op jit(solution)/shard_map/late_volume/pallas_call | solution.py:525
  36.8 0.2 collective-permute-done.14.refs_5_
  37.0 0.8 %last.1 = f32[64,128]{1,0:T(8,128)} custom-call(f32[64,128]{1,0:T(8,128)S(1)} %get-tuple-element.82.refs_0_, bf16[64,128]{1,0:T(8,128)(2,1)S(1)} %get-tuple-element.53.refs_4_.refs_1_, bf16[1,128,128]{2,1,0:T(8,128)(2,1)S(1)} %get-tuple-element.54.refs_5_.refs_2_, f32[64,128]{1,0:T(8,128)S(1)} %get-tuple-element.85.refs_3_, ...), custom_call_target="tpu_custom_call" | custom-call | flops 2097152 | bytes 131072 | tf_op jit(solution)/shard_map/last/pallas_call | solution.py:534
  (8 shorter events, 0.0 us)
Async XLA Ops:
  3.7 9.5 %collective-permute-start = (bf16[128,128]{1,0:T(8,128)(2,1)S(1)}, bf16[128,128]{1,0:T(8,128)(2,1)S(1)}, u32[]{:S(2)}, u32[]{:S(2)}) collective-permute-start(bf16[128,128]{1,0:T(8,128)(2,1)S(1)} %get-tuple-element.46), channel_id=1, source_target_pairs={{0,8},{8,16},{16,24},{24,0},{1,9},{9,17},{17,25},{25,1},{2,10},{10... | collective-permute-start | bytes 98312 | tf_op jit(solution)/shard_map/ppermute | solution.py:362
  6.8 6.5 %collective-permute-start.1 = (bf16[128,128]{1,0:T(8,128)(2,1)S(1)}, bf16[128,128]{1,0:T(8,128)(2,1)S(1)}, u32[]{:S(2)}, u32[]{:S(2)}) collective-permute-start(bf16[128,128]{1,0:T(8,128)(2,1)S(1)} %get-tuple-element.47), channel_id=1, source_target_pairs={{0,16},{8,24},{16,0},{24,8},{1,17},{9,25},{17,1},{25,9},{2,18},{10... | collective-permute-start | bytes 98312 | tf_op jit(solution)/shard_map/ppermute | solution.py:362
  9.4 3.9 %collective-permute-start.2 = (bf16[128,128]{1,0:T(8,128)(2,1)S(1)}, bf16[128,128]{1,0:T(8,128)(2,1)S(1)}, u32[]{:S(2)}, u32[]{:S(2)}) collective-permute-start(bf16[128,128]{1,0:T(8,128)(2,1)S(1)} %get-tuple-element.48), channel_id=1, source_target_pairs={{0,24},{8,0},{16,8},{24,16},{1,25},{9,1},{17,9},{25,17},{2,26},{10... | collective-permute-start | bytes 98312 | tf_op jit(solution)/shard_map/ppermute | solution.py:362
  11.7 11.7 %collective-permute-start.6 = (bf16[1216,128]{1,0:T(8,128)(2,1)S(1)}, bf16[1216,128]{1,0:T(8,128)(2,1)S(1)}, u32[]{:S(2)}, u32[]{:S(2)}) collective-permute-start(bf16[1216,128]{1,0:T(8,128)(2,1)S(1)} %get-tuple-element.67), channel_id=1, source_target_pairs={{0,1},{1,0},{2,3},{3,2},{4,5},{5,4},{6,7},{7,6},{8,9},{9,8},{10,11... | collective-permute-start | bytes 933896 | tf_op jit(solution)/shard_map/ppermute | solution.py:373
  13.3 5.6 %collective-permute-start.3 = (bf16[256,128]{1,0:T(8,128)(2,1)S(1)}, bf16[256,128]{1,0:T(8,128)(2,1)S(1)}, u32[]{:S(2)}, u32[]{:S(2)}) collective-permute-start(bf16[256,128]{1,0:T(8,128)(2,1)S(1)} %pad_maximum_fusion.1.refs_0_.refs_3_), channel_id=1, source_target_pairs={{0,4},{1,5},{2,6},{3,7},{4,0},{5,1},{6,2},{7,3},{8,12},{9,13},{10,... | collective-permute-start | bytes 196616 | tf_op jit(solution)/shard_map/ppermute | solution.py:373
  14.9 4.1 %collective-permute-start.4 = (bf16[256,128]{1,0:T(8,128)(2,1)S(1)}, bf16[256,128]{1,0:T(8,128)(2,1)S(1)}, u32[]{:S(2)}, u32[]{:S(2)}) collective-permute-start(bf16[256,128]{1,0:T(8,128)(2,1)S(1)} %pad_maximum_fusion.1.refs_0_.refs_3_), channel_id=1, source_target_pairs={{0,6},{1,7},{2,4},{3,5},{4,2},{5,3},{6,0},{7,1},{8,14},{9,15},{10,... | collective-permute-start | bytes 196616 | tf_op jit(solution)/shard_map/ppermute | solution.py:373
  14.9 4.1 %collective-permute-start.5 = (bf16[256,128]{1,0:T(8,128)(2,1)S(1)}, bf16[256,128]{1,0:T(8,128)(2,1)S(1)}, u32[]{:S(2)}, u32[]{:S(2)}) collective-permute-start(bf16[256,128]{1,0:T(8,128)(2,1)S(1)} %pad_maximum_fusion.1.refs_0_.refs_3_), channel_id=1, source_target_pairs={{0,2},{1,3},{2,0},{3,1},{4,6},{5,7},{6,4},{7,5},{8,10},{9,11},{10,... | collective-permute-start | bytes 196616 | tf_op jit(solution)/shard_map/ppermute | solution.py:373
  15.5 14.8 %collective-permute-start.11 = (bf16[1024,128]{1,0:T(8,128)(2,1)S(1)}, bf16[1024,128]{1,0:T(8,128)(2,1)S(1)}, u32[]{:S(2)}, u32[]{:S(2)}) collective-permute-start(bf16[1024,128]{1,0:T(8,128)(2,1)S(1)} %get-tuple-element.73), channel_id=1, source_target_pairs={{0,4},{1,5},{2,6},{3,7},{4,0},{5,1},{6,2},{7,3},{8,12},{9,13},{10,... | collective-permute-start | bytes 786440 | tf_op jit(solution)/shard_map/ppermute | solution.py:373
  19.4 12.2 %copy-start = (bf16[12,7,128,128]{3,2,1,0:T(8,128)(2,1)S(1)}, bf16[12,7,128,128]{3,2,1,0:T(8,128)(2,1)}, u32[]{:S(2)}) copy-start(bf16[12,7,128,128]{3,2,1,0:T(8,128)(2,1)} %refs_2_.3) | copy-start | bytes 8257540
  19.4 4.0 %collective-permute-start.7 = (bf16[128,128]{1,0:T(8,128)(2,1)S(1)}, bf16[128,128]{1,0:T(8,128)(2,1)S(1)}, u32[]{:S(2)}, u32[]{:S(2)}) collective-permute-start(bf16[128,128]{1,0:T(8,128)(2,1)S(1)} %get-tuple-element.68), channel_id=1, source_target_pairs={{0,1},{1,0},{2,3},{3,2},{4,5},{5,4},{6,7},{7,6},{8,9},{9,8},{10,11... | collective-permute-start | bytes 98312 | tf_op jit(solution)/shard_map/ppermute | solution.py:362
  20.9 10.6 %collective-permute-start.12 = (bf16[1024,128]{1,0:T(8,128)(2,1)S(1)}, bf16[1024,128]{1,0:T(8,128)(2,1)S(1)}, u32[]{:S(2)}, u32[]{:S(2)}) collective-permute-start(bf16[1024,128]{1,0:T(8,128)(2,1)S(1)} %get-tuple-element.77), channel_id=1, source_target_pairs={{0,5},{1,4},{2,7},{3,6},{4,1},{5,0},{6,3},{7,2},{8,13},{9,12},{10,... | collective-permute-start | bytes 786440 | tf_op jit(solution)/shard_map/ppermute | solution.py:373
  23.6 6.7 %collective-permute-start.10 = (bf16[192,128]{1,0:T(8,128)(2,1)S(1)}, bf16[192,128]{1,0:T(8,128)(2,1)S(1)}, u32[]{:S(2)}, u32[]{:S(2)}) collective-permute-start(bf16[192,128]{1,0:T(8,128)(2,1)S(1)} %get-tuple-element.72), channel_id=1, source_target_pairs={{0,8},{8,16},{16,24},{24,0},{1,9},{9,17},{17,25},{25,1},{2,10},{10... | collective-permute-start | bytes 147464 | tf_op jit(solution)/shard_map/ppermute | solution.py:362
  24.3 6.6 %collective-permute-start.8 = (bf16[192,128]{1,0:T(8,128)(2,1)S(1)}, bf16[192,128]{1,0:T(8,128)(2,1)S(1)}, u32[]{:S(2)}, u32[]{:S(2)}) collective-permute-start(bf16[192,128]{1,0:T(8,128)(2,1)S(1)} %get-tuple-element.70), channel_id=1, source_target_pairs={{0,16},{8,24},{16,0},{24,8},{1,17},{9,25},{17,1},{25,9},{2,18},{10... | collective-permute-start | bytes 147464 | tf_op jit(solution)/shard_map/ppermute | solution.py:362
  27.3 4.1 %collective-permute-start.9 = (bf16[192,128]{1,0:T(8,128)(2,1)S(1)}, bf16[192,128]{1,0:T(8,128)(2,1)S(1)}, u32[]{:S(2)}, u32[]{:S(2)}) collective-permute-start(bf16[192,128]{1,0:T(8,128)(2,1)S(1)} %get-tuple-element.71), channel_id=1, source_target_pairs={{0,24},{8,0},{16,8},{24,16},{1,25},{9,1},{17,9},{25,17},{2,26},{10... | collective-permute-start | bytes 147464 | tf_op jit(solution)/shard_map/ppermute | solution.py:362
  31.5 1.4 %collective-permute-start.13 = (bf16[512,128]{1,0:T(8,128)(2,1)S(1)}, bf16[512,128]{1,0:T(8,128)(2,1)S(1)}, u32[]{:S(2)}, u32[]{:S(2)}) collective-permute-start(bf16[512,128]{1,0:T(8,128)(2,1)S(1)} %pad_maximum_fusion.refs_0_), channel_id=1, source_target_pairs={{0,2},{1,3},{2,0},{3,1},{4,6},{5,7},{6,4},{7,5},{8,10},{9,11},{10,... | collective-permute-start | bytes 393224 | tf_op jit(solution)/shard_map/ppermute | solution.py:373
  33.2 3.8 %collective-permute-start.14 = (bf16[64,128]{1,0:T(8,128)(2,1)S(1)}, bf16[64,128]{1,0:T(8,128)(2,1)S(1)}, u32[]{:S(2)}, u32[]{:S(2)}) collective-permute-start(bf16[64,128]{1,0:T(8,128)(2,1)S(1)} %get-tuple-element.87), channel_id=1, source_target_pairs={{0,4},{1,5},{2,6},{3,7},{4,0},{5,1},{6,2},{7,3},{8,12},{9,13},{10,... | collective-permute-start | bytes 49160 | tf_op jit(solution)/shard_map/ppermute | solution.py:373

commit v6 on v5

--- a/solution.py
+++ b/solution.py
@@ -138,28 +138,41 @@
     add_traces(total, boundary, coupling, trace_map, bnd_count, axis)
 
 
-def early_kernel(axis, count, stride, refs):
-    group, vol_rhs, blocks, coupling, *tables, bnd_count, early, field, columns, trace_map, sems = refs
-    copies = to_scalars(tables, (columns, trace_map), sems)
-    bs = coupling.shape[-1]
-    for b in range(coupling.shape[0], vol_rhs.shape[1] // bs):
-        field[b] = vol_rhs[:, b * bs : (b + 1) * bs]
+def base_kernel(refs):
+    vol_rhs, blocks, table, base, matrix, columns, sems = refs
+    (copy,) = to_scalars([table], [columns], sems)
+    bs = blocks.shape[-1]
+    slots = matrix.shape[1] // bs - 1
+    matrix[...] = jnp.zeros_like(matrix)
+    copy.wait()
+    for b in range(blocks.shape[0]):
+        rows = slice(b * bs, (b + 1) * bs)
+        for n in range(blocks.shape[1]):
+            matrix[rows, block(lax.min(columns[n, b], slots), bs)] = blocks[b, n]
+        read = lambda col: vol_rhs[:, block(col, bs)]
+        base[:, rows] = block_row(read, blocks, columns, b)
+
+
+def volume_kernel(axis, count, stride, refs):
+    group, coupling, table, bnd_count, base, matrix, volume, trace_map, sems = refs
+    copies = to_scalars([table], [trace_map], sems)
+    slots, bs, _ = coupling.shape
+    angles = volume.shape[0]
+    subs = group.shape[1] // bs
+    here = lax.axis_index(axis)
     for c in copies:
         c.wait()
-    residual_blocks(field, vol_rhs, group, coupling, trace_map, bnd_count, axis, count, stride)
-    for b in range(early.shape[1] // bs):
-        early[:, b * bs : (b + 1) * bs] = block_row(lambda col: field[col], blocks, columns, b)
-
-
-def late_kernel(refs):
-    early, field, blocks, table, volume, columns, sems = refs
-    (copy,) = to_scalars([table], [columns], sems)
-    bs = field.shape[-1]
-    first = early.shape[1] // bs
-    volume[:, : first * bs] = early[...]
-    copy.wait()
-    for b in range(first, blocks.shape[0]):
-        volume[:, b * bs : (b + 1) * bs] = block_row(lambda col: field[col], blocks, columns, b)
+    currents = []
+    for j in range(slots):
+        alive = (j < bnd_count[0]).astype(F32)
+        target = trace_map[j]
+        slot = slot_of(here, target // subs, count)
+        picked = group[block(slot * stride, angles), block(lax.rem(target, subs), bs)]
+        currents.append((by_rows(picked, coupling[j]) * alive).astype(HALF))
+    current = jnp.concatenate(currents, axis=1)
+    for first in range(0, volume.shape[1], 2 * bs):
+        part = slice(first, min(first + 2 * bs, volume.shape[1]))
+        volume[:, part] = base[:, part] - by_rows(current, matrix[part, 0 : slots * bs])
 
 
 def dense_kernel(vol_size, row_size, col_size, refs):
@@ -497,40 +510,44 @@
     received = [shifted(payloads[k - 1], "vol", k) for k in range(1, nv)]
     received, ahead = lax.optimization_barrier((received[1:] + received[:1], ahead))
     received = received[-1:] + received[:-1]
+    half, vol_blocks = lax.optimization_barrier((half, vol_blocks))
+    base, matrix = call(
+        base_kernel,
+        "base_volume",
+        [VMEM] * 3,
+        [
+            shape((angles, vol_count * bs), F32),
+            shape((vol_count * bs, (slots + 1) * bs), HALF),
+        ],
+        product * vol_count * terms,
+        2 * bs * bs * vol_count * terms,
+        [scalars[0], pltpu.SemaphoreType.DMA((1,))],
+    )(vol_rhs, vol_blocks, tables[0])
     group = jnp.concatenate([half] + [r[: nc * angles] for r in received], axis=0)
     group, after = lax.optimization_barrier((group, after))
     blocks += [
         after[i] if i % nc else ahead[i // nc - 1] for i in range(nc, nc * chips)
     ]
+    group, base = lax.optimization_barrier((group, base))
     groups = [group] + [shifted_in_plane(group, chip=0, core=k) for k in range(1, pair)]
-    split = vol_count // 3
-    early, residual = call(
-        functools.partial(early_kernel, "vol", nv, nc),
-        "early_volume",
-        [VMEM] * 6 + [SMEM],
-        [shape((angles, split * bs), F32), shape((vol_count, angles, bs), HALF)],
-        product * split * terms,
-        2 * bs * bs * split * terms,
-        scalars,
-    )(group, vol_rhs, vol_blocks, coupling, *tables)
     integral, *parts = call(
         functools.partial(last_integral_kernel, pair, nv, nc, chips),
         "last_integral",
-        [VMEM] * (pair + chips * nc) + [ANY],
+        [VMEM] * (pair + chips * nc),
         [shape(piece, F32)] + [shape(piece, HALF)] * (chips - 1),
         product * nv * nr * nc,
         2 * nv * nr * nc * width * width,
-    )(*groups, dense, *blocks, early)
+    )(*groups, dense, *blocks)
     sums = [shifted_in_plane(parts[a - 1], chip=a) for a in range(1, chips)]
     (volume,) = call(
-        late_kernel,
-        "late_volume",
-        [VMEM] * 4,
+        functools.partial(volume_kernel, "vol", nv, nc),
+        "volume",
+        [VMEM] * 3 + [SMEM] + [VMEM] * 2,
         [shape((angles, vol_count * bs), F32)],
-        product * (vol_count - split) * terms,
-        2 * bs * bs * (vol_count - split) * terms,
-        [scalars[0], pltpu.SemaphoreType.DMA((1,))],
-    )(early, residual, vol_blocks, tables[0])
+        product * slots * (vol_count + 1),
+        2 * bs * bs * slots * (vol_count + 1),
+        [scalars[1], pltpu.SemaphoreType.DMA((1,))],
+    )(group, coupling, tables[1], tables[2], base, matrix)
     (surface,) = call(
         functools.partial(last_kernel, chips - 1),
         "last",

time: 37.9 us -> 37.9 us (level)
  Pallas kernels: 10.2 us -> 10.6 us
    pallas_call x2, Pallas kernels: 3.43 us -> 3.82 us  [the longest x1 1.99 us: local(): call(functools.partial(volume_kernel, 'vol', nv, nc), 'volume', [VMEM] *...]
  transfers between devices with their start and end apart: 15 -> 15, of which waited for: 7 -> 7; matrix products, arithmetic and copies ran while one was open for 0% -> 0% of each run, Pallas kernels for 18% -> 19%
where the time goes in v6:
time: 37.9 us; the launch traced here: 37.8 us
  starting transfers between devices  20 us (53%)
  Pallas kernels  10.6 us (28%)
  waiting for transfers between devices  5.7 us (15%)
  between operations  1.42 us (4%)
    ppermute x7, starting transfers between devices, shifted(): lax.ppermute(value, axis, [(i, (i + shift) % size) for i in range(size)])  12.5 us
    ppermute x8, starting transfers between devices, shifted_in_plane(): return lax.ppermute(value, ('row', 'col'), pairs)  7.57 us
    ppermute x8, waiting for transfers between devices, shifted_in_plane(): return lax.ppermute(value, ('row', 'col'), pairs)  2.86 us
    ppermute x7, waiting for transfers between devices, shifted(): lax.ppermute(value, axis, [(i, (i + shift) % size) for i in range(size)])  2.83 us
    pallas_call x1, Pallas kernels, local(): call(functools.partial(start_kernel, 'vol', len(start_shapes), len(kept))...  2.41 us
    pallas_call x1, Pallas kernels, local(): call(functools.partial(volume_kernel, 'vol', nv, nc), 'volume', [VMEM] *...  1.99 us
    pallas_call x1, Pallas kernels, local(): call(functools.partial(boundary_kernel, 'vol'), 'boundary', [VMEM] * 6 +...  1.83 us
    pallas_call x1, Pallas kernels, local(): call(base_kernel, 'base_volume', [VMEM] * 3, [shape((angles, vol_count *...  1.83 us
  transfers between devices with their start and end apart: 15, of which 7 were waited for; matrix products, arithmetic and copies ran while one was open for 0% of the time, Pallas kernels for 19%

profile of v6, /device:TPU:0, one launch (start us, length us, event | category | flops | bytes accessed | tf_op | source)
XLA Modules:
  0.0 37.8 jit_solution(724587678800821294)
XLA Ops:
  1.3 2.4 %start.1 = (bf16[64,128]{1,0:T(8,128)(2,1)S(1)}, f32[64,128]{1,0:T(8,128)S(1)}, bf16[128,128]{1,0:T(8,128)(2,1)S(1)}, bf16[128,128]{1,0:T(8,128)(2,1)S(1)}, bf16...) custom-call(s32[1]{0:T(128)S(6)} %copy.14.refs_0_.refs_6_.refs_3_, ...), custom_call_target="tpu_custom_call" | custom-call | flops 67108864 | bytes 1048576 | tf_op jit(solution)/shard_map/start/pallas_call | solution.py:422
  3.7 3.1 %collective-permute-start = (bf16[128,128]{1,0:T(8,128)(2,1)S(1)}, bf16[128,128]{1,0:T(8,128)(2,1)S(1)}, u32[]{:S(2)}, u32[]{:S(2)}) collective-permute-start(bf16[128,128]{1,0:T(8,128)(2,1)S(1)} %get-tuple-element.50), channel_id=1, source_target_pairs={{0,8},{8,16},{16,24},{24,0},{1,9},{9,17},{17,25},{25,1},{2,10},{10... | collective-permute-start | bytes 98312 | tf_op jit(solution)/shard_map/ppermute | solution.py:375
  6.8 2.6 %collective-permute-start.1 = (bf16[128,128]{1,0:T(8,128)(2,1)S(1)}, bf16[128,128]{1,0:T(8,128)(2,1)S(1)}, u32[]{:S(2)}, u32[]{:S(2)}) collective-permute-start(bf16[128,128]{1,0:T(8,128)(2,1)S(1)} %get-tuple-element.51), channel_id=1, source_target_pairs={{0,16},{8,24},{16,0},{24,8},{1,17},{9,25},{17,1},{25,9},{2,18},{10... | collective-permute-start | bytes 98312 | tf_op jit(solution)/shard_map/ppermute | solution.py:375
  9.4 1.3 %collective-permute-start.2 = (bf16[128,128]{1,0:T(8,128)(2,1)S(1)}, bf16[128,128]{1,0:T(8,128)(2,1)S(1)}, u32[]{:S(2)}, u32[]{:S(2)}) collective-permute-start(bf16[128,128]{1,0:T(8,128)(2,1)S(1)} %get-tuple-element.52), channel_id=1, source_target_pairs={{0,24},{8,0},{16,8},{24,16},{1,25},{9,1},{17,9},{25,17},{2,26},{10... | collective-permute-start | bytes 98312 | tf_op jit(solution)/shard_map/ppermute | solution.py:375
  10.7 0.9 %dense.1 = (bf16[2048,256]{1,0:T(8,128)(2,1)S(1)}, bf16[1216,128]{1,0:T(8,128)(2,1)S(1)}, bf16[1024,128]{1,0:T(8,128)(2,1)S(1)}, bf16[1024,128]{1,0:T(8,128)(2,1)S(1)}) custom-call(bf16[2,1,4,128,128]{4,3,2,1,0:T(8,128)(2,1)S(1)} %get-tuple-element.53.refs_0_, s32[2,1,4]{2,1,0:T(1,128)S(1)} %get-tuple-element.54.refs_1_, ...), custom_call_target="tpu_custom_call" | custom-call | flops 67108864 | bytes 2097152 | tf_op jit(solution)/shard_map/dense/pallas_call | solution.py:447
  11.7 1.6 %collective-permute-start.6 = (bf16[1216,128]{1,0:T(8,128)(2,1)S(1)}, bf16[1216,128]{1,0:T(8,128)(2,1)S(1)}, u32[]{:S(2)}, u32[]{:S(2)}) collective-permute-start(bf16[1216,128]{1,0:T(8,128)(2,1)S(1)} %get-tuple-element.71), channel_id=1, source_target_pairs={{0,1},{1,0},{2,3},{3,2},{4,5},{5,4},{6,7},{7,6},{8,9},{9,8},{10,11... | collective-permute-start | bytes 933896 | tf_op jit(solution)/shard_map/ppermute | solution.py:386
  13.2 0.0 collective-permute-done.refs_6_
  13.2 0.0 collective-permute-done.1.refs_7_
  13.3 0.0 collective-permute-done.2.refs_8_
  13.3 1.6 %collective-permute-start.3 = (bf16[256,128]{1,0:T(8,128)(2,1)S(1)}, bf16[256,128]{1,0:T(8,128)(2,1)S(1)}, u32[]{:S(2)}, u32[]{:S(2)}) collective-permute-start(bf16[256,128]{1,0:T(8,128)(2,1)S(1)} %pad_maximum_fusion.1.refs_0_.refs_3_), channel_id=1, source_target_pairs={{0,4},{1,5},{2,6},{3,7},{4,0},{5,1},{6,2},{7,3},{8,12},{9,13},{10,... | collective-permute-start | bytes 196616 | tf_op jit(solution)/shard_map/ppermute | solution.py:386
  14.9 0.0 collective-permute-start.4
  14.9 0.6 %collective-permute-start.5 = (bf16[256,128]{1,0:T(8,128)(2,1)S(1)}, bf16[256,128]{1,0:T(8,128)(2,1)S(1)}, u32[]{:S(2)}, u32[]{:S(2)}) collective-permute-start(bf16[256,128]{1,0:T(8,128)(2,1)S(1)} %pad_maximum_fusion.1.refs_0_.refs_3_), channel_id=1, source_target_pairs={{0,2},{1,3},{2,0},{3,1},{4,6},{5,7},{6,4},{7,5},{8,10},{9,11},{10,... | collective-permute-start | bytes 196616 | tf_op jit(solution)/shard_map/ppermute | solution.py:386
  15.5 1.5 %collective-permute-start.11 = (bf16[1024,128]{1,0:T(8,128)(2,1)S(1)}, bf16[1024,128]{1,0:T(8,128)(2,1)S(1)}, u32[]{:S(2)}, u32[]{:S(2)}) collective-permute-start(bf16[1024,128]{1,0:T(8,128)(2,1)S(1)} %get-tuple-element.79), channel_id=1, source_target_pairs={{0,4},{1,5},{2,6},{3,7},{4,0},{5,1},{6,2},{7,3},{8,12},{9,13},{10,... | collective-permute-start | bytes 786440 | tf_op jit(solution)/shard_map/ppermute | solution.py:386
  17.0 1.8 %boundary.1.refs_9_.refs_3_ = f32[4,64,128]{2,1,0:T(8,128)S(1)} custom-call(bf16[256,128]{1,0:T(8,128)(2,1)S(1)} %pad_maximum_fusion.1.refs_0_.refs_3_, bf16[64,1536]{1,0:T(8,128)(2,1)S(1)} %get-tuple-element.63.refs_1_.refs_0_, bf16[4,7,128,128]{3,2,1,0:T(8,128)(2,1)S(1)} %get-tuple-element.64.refs_2_, ...), custom_call_target="tpu_custom_call" | custom-call | flops 75497472 | bytes 1048576 | tf_op jit(solution)/shard_map/boundary/pallas_call | solution.py:470
  18.9 0.0 collective-permute-done.3.refs_0_
  18.9 0.2 collective-permute-done.4.refs_1_
  19.0 0.0 collective-permute-done.5.refs_2_
  19.0 0.3 integral.1
  19.3 0.0 copy-start
  19.4 1.6 %collective-permute-start.7 = (bf16[128,128]{1,0:T(8,128)(2,1)S(1)}, bf16[128,128]{1,0:T(8,128)(2,1)S(1)}, u32[]{:S(2)}, u32[]{:S(2)}) collective-permute-start(bf16[128,128]{1,0:T(8,128)(2,1)S(1)} %get-tuple-element.72), channel_id=1, source_target_pairs={{0,1},{1,0},{2,3},{3,2},{4,5},{5,4},{6,7},{7,6},{8,9},{9,8},{10,11... | collective-permute-start | bytes 98312 | tf_op jit(solution)/shard_map/ppermute | solution.py:375
  20.9 0.8 %collective-permute-start.12 = (bf16[1024,128]{1,0:T(8,128)(2,1)S(1)}, bf16[1024,128]{1,0:T(8,128)(2,1)S(1)}, u32[]{:S(2)}, u32[]{:S(2)}) collective-permute-start(bf16[1024,128]{1,0:T(8,128)(2,1)S(1)} %get-tuple-element.83), channel_id=1, source_target_pairs={{0,5},{1,4},{2,7},{3,6},{4,1},{5,0},{6,3},{7,2},{8,13},{9,12},{10,... | collective-permute-start | bytes 786440 | tf_op jit(solution)/shard_map/ppermute | solution.py:386
  21.7 1.6 %collective-permute-done.7.refs_5_ = bf16[128,128]{1,0:T(8,128)(2,1)S(1)} collective-permute-done((bf16[128,128]{1,0:T(8,128)(2,1)S(1)}, bf16[128,128]{1,0:T(8,128)(2,1)S(1)}, u32[]{:S(2)}, u32[]{:S(2)}) %collective-permute-start.7) | collective-permute-done | bytes 32800 | tf_op jit(solution)/shard_map/ppermute | solution.py:375
  23.3 0.0 collective-permute-done.6.refs_4_.refs_3_
  23.3 0.2 step.1
  23.6 0.7 %collective-permute-start.10 = (bf16[192,128]{1,0:T(8,128)(2,1)S(1)}, bf16[192,128]{1,0:T(8,128)(2,1)S(1)}, u32[]{:S(2)}, u32[]{:S(2)}) collective-permute-start(bf16[192,128]{1,0:T(8,128)(2,1)S(1)} %get-tuple-element.78), channel_id=1, source_target_pairs={{0,8},{8,16},{16,24},{24,0},{1,9},{9,17},{17,25},{25,1},{2,10},{10... | collective-permute-start | bytes 147464 | tf_op jit(solution)/shard_map/ppermute | solution.py:375
  24.3 3.0 %collective-permute-start.8 = (bf16[192,128]{1,0:T(8,128)(2,1)S(1)}, bf16[192,128]{1,0:T(8,128)(2,1)S(1)}, u32[]{:S(2)}, u32[]{:S(2)}) collective-permute-start(bf16[192,128]{1,0:T(8,128)(2,1)S(1)} %get-tuple-element.76), channel_id=1, source_target_pairs={{0,16},{8,24},{16,0},{24,8},{1,17},{9,25},{17,1},{25,9},{2,18},{10... | collective-permute-start | bytes 147464 | tf_op jit(solution)/shard_map/ppermute | solution.py:375
  27.3 0.1 collective-permute-start.9
  27.5 0.0 copy-done
  27.5 1.8 %base_volume.1 = (f32[64,1536]{1,0:T(8,128)S(1)}, bf16[1536,640]{1,0:T(8,128)(2,1)S(1)}) custom-call(bf16[64,1536]{1,0:T(8,128)(2,1)S(1)} %get-tuple-element.63.refs_1_.refs_0_, bf16[12,7,128,128]{3,2,1,0:T(8,128)(2,1)S(1)} %copy-done, s32[7,12]{1,0:T(8,128)S(1)} %get-tuple-element.66.refs_4_.refs_2_), custom_call_target="tpu_custom_call" | custom-call | flops 176160768 | bytes 2752512 | tf_op jit(solution)/shard_map/base_volume/pallas_call | solution.py:514
  29.3 1.0 %collective-permute-done.11.refs_4_ = bf16[1024,128]{1,0:T(8,128)(2,1)S(1)} collective-permute-done((bf16[1024,128]{1,0:T(8,128)(2,1)S(1)}, bf16[1024,128]{1,0:T(8,128)(2,1)S(1)}, u32[]{:S(2)}, u32[]{:S(2)}) %collective-permute-start.11) | collective-permute-done | bytes 262176 | tf_op jit(solution)/shard_map/ppermute | solution.py:386
  30.3 0.0 collective-permute-done.10.refs_6_
  30.3 0.6 %collective-permute-done.8.refs_7_ = bf16[192,128]{1,0:T(8,128)(2,1)S(1)} collective-permute-done((bf16[192,128]{1,0:T(8,128)(2,1)S(1)}, bf16[192,128]{1,0:T(8,128)(2,1)S(1)}, u32[]{:S(2)}, u32[]{:S(2)}) %collective-permute-start.8) | collective-permute-done | bytes 49184 | tf_op jit(solution)/shard_map/ppermute | solution.py:375
  30.9 0.5 %collective-permute-done.9.refs_8_ = bf16[192,128]{1,0:T(8,128)(2,1)S(1)} collective-permute-done((bf16[192,128]{1,0:T(8,128)(2,1)S(1)}, bf16[192,128]{1,0:T(8,128)(2,1)S(1)}, u32[]{:S(2)}, u32[]{:S(2)}) %collective-permute-start.9) | collective-permute-done | bytes 49184 | tf_op jit(solution)/shard_map/ppermute | solution.py:375
  31.5 0.0 collective-permute-done.12.refs_5_
  31.5 0.1 collective-permute-start.13
  31.6 1.3 %collective-permute-done.13.refs_1_ = bf16[512,128]{1,0:T(8,128)(2,1)S(1)} collective-permute-done((bf16[512,128]{1,0:T(8,128)(2,1)S(1)}, bf16[512,128]{1,0:T(8,128)(2,1)S(1)}, u32[]{:S(2)}, u32[]{:S(2)}) %collective-permute-start.13) | collective-permute-done | bytes 131104 | tf_op jit(solution)/shard_map/ppermute | solution.py:386
  32.9 0.3 last_integral.1
  33.2 1.4 %collective-permute-start.14 = (bf16[64,128]{1,0:T(8,128)(2,1)S(1)}, bf16[64,128]{1,0:T(8,128)(2,1)S(1)}, u32[]{:S(2)}, u32[]{:S(2)}) collective-permute-start(bf16[64,128]{1,0:T(8,128)(2,1)S(1)} %get-tuple-element.95), channel_id=1, source_target_pairs={{0,4},{1,5},{2,6},{3,7},{4,0},{5,1},{6,2},{7,3},{8,12},{9,13},{10,... | collective-permute-start | bytes 49160 | tf_op jit(solution)/shard_map/ppermute | solution.py:386
  34.6 2.0 %volume.1 = f32[64,1536]{1,0:T(8,128)} custom-call(bf16[512,128]{1,0:T(8,128)(2,1)S(1)} %pad_maximum_fusion.refs_0_, bf16[4,128,128]{2,1,0:T(8,128)(2,1)S(1)} %get-tuple-element.65.refs_3_.refs_1_, s32[4]{0:T(128)S(1)} %get-tuple-element.67.refs_5_.refs_2_, s32[1]{0:T(128)S(6)} %copy.14.refs_0_.refs_6_.refs_3_, f32[64,1536]{1,0:T(8,128)S(1)} %get-tuple-element.88.refs_4_, ...), custom_call_target="tpu_custom_call" | custom-call | flops 109051904 | bytes 1703936 | tf_op jit(solution)/shard_map/volume/pallas_call | solution.py:542
  36.6 0.4 %collective-permute-done.14.refs_5_ = bf16[64,128]{1,0:T(8,128)(2,1)S(1)} collective-permute-done((bf16[64,128]{1,0:T(8,128)(2,1)S(1)}, bf16[64,128]{1,0:T(8,128)(2,1)S(1)}, u32[]{:S(2)}, u32[]{:S(2)}) %collective-permute-start.14) | collective-permute-done | bytes 16416 | tf_op jit(solution)/shard_map/ppermute | solution.py:386
  37.0 0.8 %last.1 = f32[64,128]{1,0:T(8,128)} custom-call(f32[64,128]{1,0:T(8,128)S(1)} %get-tuple-element.90.refs_0_, bf16[64,128]{1,0:T(8,128)(2,1)S(1)} %get-tuple-element.57.refs_4_.refs_1_, bf16[1,128,128]{2,1,0:T(8,128)(2,1)S(1)} %get-tuple-element.58.refs_5_.refs_2_, f32[64,128]{1,0:T(8,128)S(1)} %get-tuple-element.93.refs_3_, ...), custom_call_target="tpu_custom_call" | custom-call | flops 2097152 | bytes 131072 | tf_op jit(solution)/shard_map/last/pallas_call | solution.py:551
  (8 shorter events, 0.0 us)
Async XLA Ops:
  3.7 9.5 %collective-permute-start = (bf16[128,128]{1,0:T(8,128)(2,1)S(1)}, bf16[128,128]{1,0:T(8,128)(2,1)S(1)}, u32[]{:S(2)}, u32[]{:S(2)}) collective-permute-start(bf16[128,128]{1,0:T(8,128)(2,1)S(1)} %get-tuple-element.50), channel_id=1, source_target_pairs={{0,8},{8,16},{16,24},{24,0},{1,9},{9,17},{17,25},{25,1},{2,10},{10... | collective-permute-start | bytes 98312 | tf_op jit(solution)/shard_map/ppermute | solution.py:375
  6.8 6.5 %collective-permute-start.1 = (bf16[128,128]{1,0:T(8,128)(2,1)S(1)}, bf16[128,128]{1,0:T(8,128)(2,1)S(1)}, u32[]{:S(2)}, u32[]{:S(2)}) collective-permute-start(bf16[128,128]{1,0:T(8,128)(2,1)S(1)} %get-tuple-element.51), channel_id=1, source_target_pairs={{0,16},{8,24},{16,0},{24,8},{1,17},{9,25},{17,1},{25,9},{2,18},{10... | collective-permute-start | bytes 98312 | tf_op jit(solution)/shard_map/ppermute | solution.py:375
  9.4 3.9 %collective-permute-start.2 = (bf16[128,128]{1,0:T(8,128)(2,1)S(1)}, bf16[128,128]{1,0:T(8,128)(2,1)S(1)}, u32[]{:S(2)}, u32[]{:S(2)}) collective-permute-start(bf16[128,128]{1,0:T(8,128)(2,1)S(1)} %get-tuple-element.52), channel_id=1, source_target_pairs={{0,24},{8,0},{16,8},{24,16},{1,25},{9,1},{17,9},{25,17},{2,26},{10... | collective-permute-start | bytes 98312 | tf_op jit(solution)/shard_map/ppermute | solution.py:375
  11.7 11.7 %collective-permute-start.6 = (bf16[1216,128]{1,0:T(8,128)(2,1)S(1)}, bf16[1216,128]{1,0:T(8,128)(2,1)S(1)}, u32[]{:S(2)}, u32[]{:S(2)}) collective-permute-start(bf16[1216,128]{1,0:T(8,128)(2,1)S(1)} %get-tuple-element.71), channel_id=1, source_target_pairs={{0,1},{1,0},{2,3},{3,2},{4,5},{5,4},{6,7},{7,6},{8,9},{9,8},{10,11... | collective-permute-start | bytes 933896 | tf_op jit(solution)/shard_map/ppermute | solution.py:386
  13.3 5.6 %collective-permute-start.3 = (bf16[256,128]{1,0:T(8,128)(2,1)S(1)}, bf16[256,128]{1,0:T(8,128)(2,1)S(1)}, u32[]{:S(2)}, u32[]{:S(2)}) collective-permute-start(bf16[256,128]{1,0:T(8,128)(2,1)S(1)} %pad_maximum_fusion.1.refs_0_.refs_3_), channel_id=1, source_target_pairs={{0,4},{1,5},{2,6},{3,7},{4,0},{5,1},{6,2},{7,3},{8,12},{9,13},{10,... | collective-permute-start | bytes 196616 | tf_op jit(solution)/shard_map/ppermute | solution.py:386
  14.9 4.1 %collective-permute-start.4 = (bf16[256,128]{1,0:T(8,128)(2,1)S(1)}, bf16[256,128]{1,0:T(8,128)(2,1)S(1)}, u32[]{:S(2)}, u32[]{:S(2)}) collective-permute-start(bf16[256,128]{1,0:T(8,128)(2,1)S(1)} %pad_maximum_fusion.1.refs_0_.refs_3_), channel_id=1, source_target_pairs={{0,6},{1,7},{2,4},{3,5},{4,2},{5,3},{6,0},{7,1},{8,14},{9,15},{10,... | collective-permute-start | bytes 196616 | tf_op jit(solution)/shard_map/ppermute | solution.py:386
  14.9 4.1 %collective-permute-start.5 = (bf16[256,128]{1,0:T(8,128)(2,1)S(1)}, bf16[256,128]{1,0:T(8,128)(2,1)S(1)}, u32[]{:S(2)}, u32[]{:S(2)}) collective-permute-start(bf16[256,128]{1,0:T(8,128)(2,1)S(1)} %pad_maximum_fusion.1.refs_0_.refs_3_), channel_id=1, source_target_pairs={{0,2},{1,3},{2,0},{3,1},{4,6},{5,7},{6,4},{7,5},{8,10},{9,11},{10,... | collective-permute-start | bytes 196616 | tf_op jit(solution)/shard_map/ppermute | solution.py:386
  15.5 14.8 %collective-permute-start.11 = (bf16[1024,128]{1,0:T(8,128)(2,1)S(1)}, bf16[1024,128]{1,0:T(8,128)(2,1)S(1)}, u32[]{:S(2)}, u32[]{:S(2)}) collective-permute-start(bf16[1024,128]{1,0:T(8,128)(2,1)S(1)} %get-tuple-element.79), channel_id=1, source_target_pairs={{0,4},{1,5},{2,6},{3,7},{4,0},{5,1},{6,2},{7,3},{8,12},{9,13},{10,... | collective-permute-start | bytes 786440 | tf_op jit(solution)/shard_map/ppermute | solution.py:386
  19.3 8.1 %copy-start = (bf16[12,7,128,128]{3,2,1,0:T(8,128)(2,1)S(1)}, bf16[12,7,128,128]{3,2,1,0:T(8,128)(2,1)}, u32[]{:S(2)}) copy-start(bf16[12,7,128,128]{3,2,1,0:T(8,128)(2,1)} %refs_1_.2) | copy-start | bytes 8257540
  19.4 4.0 %collective-permute-start.7 = (bf16[128,128]{1,0:T(8,128)(2,1)S(1)}, bf16[128,128]{1,0:T(8,128)(2,1)S(1)}, u32[]{:S(2)}, u32[]{:S(2)}) collective-permute-start(bf16[128,128]{1,0:T(8,128)(2,1)S(1)} %get-tuple-element.72), channel_id=1, source_target_pairs={{0,1},{1,0},{2,3},{3,2},{4,5},{5,4},{6,7},{7,6},{8,9},{9,8},{10,11... | collective-permute-start | bytes 98312 | tf_op jit(solution)/shard_map/ppermute | solution.py:375
  20.9 10.6 %collective-permute-start.12 = (bf16[1024,128]{1,0:T(8,128)(2,1)S(1)}, bf16[1024,128]{1,0:T(8,128)(2,1)S(1)}, u32[]{:S(2)}, u32[]{:S(2)}) collective-permute-start(bf16[1024,128]{1,0:T(8,128)(2,1)S(1)} %get-tuple-element.83), channel_id=1, source_target_pairs={{0,5},{1,4},{2,7},{3,6},{4,1},{5,0},{6,3},{7,2},{8,13},{9,12},{10,... | collective-permute-start | bytes 786440 | tf_op jit(solution)/shard_map/ppermute | solution.py:386
  23.6 6.7 %collective-permute-start.10 = (bf16[192,128]{1,0:T(8,128)(2,1)S(1)}, bf16[192,128]{1,0:T(8,128)(2,1)S(1)}, u32[]{:S(2)}, u32[]{:S(2)}) collective-permute-start(bf16[192,128]{1,0:T(8,128)(2,1)S(1)} %get-tuple-element.78), channel_id=1, source_target_pairs={{0,8},{8,16},{16,24},{24,0},{1,9},{9,17},{17,25},{25,1},{2,10},{10... | collective-permute-start | bytes 147464 | tf_op jit(solution)/shard_map/ppermute | solution.py:375
  24.3 6.6 %collective-permute-start.8 = (bf16[192,128]{1,0:T(8,128)(2,1)S(1)}, bf16[192,128]{1,0:T(8,128)(2,1)S(1)}, u32[]{:S(2)}, u32[]{:S(2)}) collective-permute-start(bf16[192,128]{1,0:T(8,128)(2,1)S(1)} %get-tuple-element.76), channel_id=1, source_target_pairs={{0,16},{8,24},{16,0},{24,8},{1,17},{9,25},{17,1},{25,9},{2,18},{10... | collective-permute-start | bytes 147464 | tf_op jit(solution)/shard_map/ppermute | solution.py:375
  27.3 4.1 %collective-permute-start.9 = (bf16[192,128]{1,0:T(8,128)(2,1)S(1)}, bf16[192,128]{1,0:T(8,128)(2,1)S(1)}, u32[]{:S(2)}, u32[]{:S(2)}) collective-permute-start(bf16[192,128]{1,0:T(8,128)(2,1)S(1)} %get-tuple-element.77), channel_id=1, source_target_pairs={{0,24},{8,0},{16,8},{24,16},{1,25},{9,1},{17,9},{25,17},{2,26},{10... | collective-permute-start | bytes 147464 | tf_op jit(solution)/shard_map/ppermute | solution.py:375
  31.5 1.4 %collective-permute-start.13 = (bf16[512,128]{1,0:T(8,128)(2,1)S(1)}, bf16[512,128]{1,0:T(8,128)(2,1)S(1)}, u32[]{:S(2)}, u32[]{:S(2)}) collective-permute-start(bf16[512,128]{1,0:T(8,128)(2,1)S(1)} %pad_maximum_fusion.refs_0_), channel_id=1, source_target_pairs={{0,2},{1,3},{2,0},{3,1},{4,6},{5,7},{6,4},{7,5},{8,10},{9,11},{10,... | collective-permute-start | bytes 393224 | tf_op jit(solution)/shard_map/ppermute | solution.py:386
  33.2 3.8 %collective-permute-start.14 = (bf16[64,128]{1,0:T(8,128)(2,1)S(1)}, bf16[64,128]{1,0:T(8,128)(2,1)S(1)}, u32[]{:S(2)}, u32[]{:S(2)}) collective-permute-start(bf16[64,128]{1,0:T(8,128)(2,1)S(1)} %get-tuple-element.95), channel_id=1, source_target_pairs={{0,4},{1,5},{2,6},{3,7},{4,0},{5,1},{6,2},{7,3},{8,12},{9,13},{10,... | collective-permute-start | bytes 49160 | tf_op jit(solution)/shard_map/ppermute | solution.py:386

commit v7 on v6

--- a/solution.py
+++ b/solution.py
@@ -222,12 +222,8 @@
                 near = near_blocks[b, 0, n].astype(F32).T
                 dense[where] = (dense[where].astype(F32) + near).astype(HALF)
     width = subs * bs
-    for a in range(chips):
-        for k in range(col_size):
-            if a or k:
-                messages[a * col_size + k - 1][0:part, :] = dense[
-                    a * part : (a + 1) * part, k * width : (k + 1) * width
-                ]
+    for k in range(1, col_size):
+        messages[k - 1][0:part, :] = dense[0:part, k * width : (k + 1) * width]
     angles = surf_rhs.shape[0]
     for k in range(1, col_size):
         message = messages[k - 1]
@@ -449,7 +445,7 @@
         "dense",
         [VMEM] * 6,
         [shape((nv * nr * width, nc * width), HALF)]
-        + [shape((size, width), HALF) for size in sizes[1:]],
+        + [shape((size, width), HALF) for size in sizes[1:nc]],
         product * nv * nr * nc,
         4 * nv * nr * nc * bs * bs,
         [
@@ -457,6 +453,11 @@
             pltpu.SemaphoreType.DMA((1,)),
         ],
     )(*kept)
+
+    messages += [
+        dense[i // nc * part : (i // nc + 1) * part, i % nc * width : (i % nc + 1) * width]
+        for i in range(nc, nc * chips)
+    ]
 
     received = [shifted(payloads[k - 1], "vol", k) for k in range(1, nv)]
     blocks = [
@@ -508,8 +509,8 @@
     )(parts, surf_rhs, surf_inverse, total, *blocks, *sums)
 
     received = [shifted(payloads[k - 1], "vol", k) for k in range(1, nv)]
-    received, ahead = lax.optimization_barrier((received[1:] + received[:1], ahead))
-    received = received[-1:] + received[:-1]
+    received, ahead = lax.optimization_barrier((received[:1] + received[:0:-1], ahead))
+    received = received[:1] + received[:0:-1]
     half, vol_blocks = lax.optimization_barrier((half, vol_blocks))
     base, matrix = call(
         base_kernel,

time: 37.9 us -> 37.9 us (level)
  starting transfers between devices: 20 us -> 20.9 us
  waiting for transfers between devices: 5.7 us -> 4.85 us
    ppermute x8, waiting for transfers between devices: 2.86 us -> 1.86 us  [shifted_in_plane(): return lax.ppermute(value, ('row', 'col'), pairs)]
    ppermute x7, starting transfers between devices: 12.5 us -> 13.4 us  [shifted(): lax.ppermute(value, axis, [(i, (i + shift) % size) for i in range(size)])]
  transfers between devices with their start and end apart: 15 -> 15, of which waited for: 7 -> 6; matrix products, arithmetic and copies ran while one was open for 0% -> 0% of each run, Pallas kernels for 19% -> 19%
where the time goes in v7:
time: 37.9 us; the launch traced here: 37.8 us
  starting transfers between devices  20.9 us (55%)
  Pallas kernels  10.5 us (28%)
  waiting for transfers between devices  4.85 us (13%)
  between operations  1.42 us (4%)
    ppermute x7, starting transfers between devices, shifted(): lax.ppermute(value, axis, [(i, (i + shift) % size) for i in range(size)])  13.4 us
    ppermute x8, starting transfers between devices, shifted_in_plane(): return lax.ppermute(value, ('row', 'col'), pairs)  7.53 us
    ppermute x7, waiting for transfers between devices, shifted(): lax.ppermute(value, axis, [(i, (i + shift) % size) for i in range(size)])  2.99 us
    pallas_call x1, Pallas kernels, local(): call(functools.partial(start_kernel, 'vol', len(start_shapes), len(kept))...  2.42 us
    pallas_call x1, Pallas kernels, local(): call(functools.partial(volume_kernel, 'vol', nv, nc), 'volume', [VMEM] *...  1.98 us
    ppermute x8, waiting for transfers between devices, shifted_in_plane(): return lax.ppermute(value, ('row', 'col'), pairs)  1.86 us
    pallas_call x1, Pallas kernels, local(): call(base_kernel, 'base_volume', [VMEM] * 3, [shape((angles, vol_count *...  1.83 us
    pallas_call x1, Pallas kernels, local(): call(functools.partial(boundary_kernel, 'vol'), 'boundary', [VMEM] * 6 +...  1.83 us
  transfers between devices with their start and end apart: 15, of which 6 were waited for; matrix products, arithmetic and copies ran while one was open for 0% of the time, Pallas kernels for 19%

profile of v7, /device:TPU:0, one launch (start us, length us, event | category | flops | bytes accessed | tf_op | source)
XLA Modules:
  0.0 37.8 jit_solution(17094961237202130443)
XLA Ops:
  1.3 2.4 %start.1 = (bf16[64,128]{1,0:T(8,128)(2,1)S(1)}, f32[64,128]{1,0:T(8,128)S(1)}, bf16[128,128]{1,0:T(8,128)(2,1)S(1)}, bf16[128,128]{1,0:T(8,128)(2,1)S(1)}, bf16...) custom-call(s32[1]{0:T(128)S(6)} %copy.14.refs_0_.refs_6_.refs_3_, ...), custom_call_target="tpu_custom_call" | custom-call | flops 67108864 | bytes 1048576 | tf_op jit(solution)/shard_map/start/pallas_call | solution.py:418
  3.7 3.1 %collective-permute-start = (bf16[128,128]{1,0:T(8,128)(2,1)S(1)}, bf16[128,128]{1,0:T(8,128)(2,1)S(1)}, u32[]{:S(2)}, u32[]{:S(2)}) collective-permute-start(bf16[128,128]{1,0:T(8,128)(2,1)S(1)} %get-tuple-element.48), channel_id=1, source_target_pairs={{0,8},{8,16},{16,24},{24,0},{1,9},{9,17},{17,25},{25,1},{2,10},{10... | collective-permute-start | bytes 98312 | tf_op jit(solution)/shard_map/ppermute | solution.py:371
  6.8 2.6 %collective-permute-start.1 = (bf16[128,128]{1,0:T(8,128)(2,1)S(1)}, bf16[128,128]{1,0:T(8,128)(2,1)S(1)}, u32[]{:S(2)}, u32[]{:S(2)}) collective-permute-start(bf16[128,128]{1,0:T(8,128)(2,1)S(1)} %get-tuple-element.49), channel_id=1, source_target_pairs={{0,16},{8,24},{16,0},{24,8},{1,17},{9,25},{17,1},{25,9},{2,18},{10... | collective-permute-start | bytes 98312 | tf_op jit(solution)/shard_map/ppermute | solution.py:371
  9.4 1.4 %collective-permute-start.2 = (bf16[128,128]{1,0:T(8,128)(2,1)S(1)}, bf16[128,128]{1,0:T(8,128)(2,1)S(1)}, u32[]{:S(2)}, u32[]{:S(2)}) collective-permute-start(bf16[128,128]{1,0:T(8,128)(2,1)S(1)} %get-tuple-element.50), channel_id=1, source_target_pairs={{0,24},{8,0},{16,8},{24,16},{1,25},{9,1},{17,9},{25,17},{2,26},{10... | collective-permute-start | bytes 98312 | tf_op jit(solution)/shard_map/ppermute | solution.py:371
  10.7 0.9 %dense.1 = (bf16[2048,256]{1,0:T(8,128)(2,1)S(1)}, bf16[1216,128]{1,0:T(8,128)(2,1)S(1)}) custom-call(bf16[2,1,4,128,128]{4,3,2,1,0:T(8,128)(2,1)S(1)} %get-tuple-element.51.refs_0_, s32[2,1,4]{2,1,0:T(1,128)S(1)} %get-tuple-element.52.refs_1_, bf16[1,32,256]{2,1,0:T(8,128)(2,1)S(1)} %get-tuple-element.53.refs_2_, ...), custom_call_target="tpu_custom_call" | custom-call | flops 67108864 | bytes 2097152 | tf_op jit(solution)/shard_map/dense/pallas_call | solution.py:443
  11.6 1.6 %collective-permute-start.6 = (bf16[1216,128]{1,0:T(8,128)(2,1)S(1)}, bf16[1216,128]{1,0:T(8,128)(2,1)S(1)}, u32[]{:S(2)}, u32[]{:S(2)}) collective-permute-start(bf16[1216,128]{1,0:T(8,128)(2,1)S(1)} %get-tuple-element.68), channel_id=1, source_target_pairs={{0,1},{1,0},{2,3},{3,2},{4,5},{5,4},{6,7},{7,6},{8,9},{9,8},{10,11... | collective-permute-start | bytes 933896 | tf_op jit(solution)/shard_map/ppermute | solution.py:382
  13.1 0.0 collective-permute-done.refs_6_
  13.1 0.0 collective-permute-done.1.refs_7_
  13.2 0.1 collective-permute-done.2.refs_8_
  13.3 1.6 %collective-permute-start.3 = (bf16[256,128]{1,0:T(8,128)(2,1)S(1)}, bf16[256,128]{1,0:T(8,128)(2,1)S(1)}, u32[]{:S(2)}, u32[]{:S(2)}) collective-permute-start(bf16[256,128]{1,0:T(8,128)(2,1)S(1)} %pad_maximum_fusion.1.refs_0_.refs_3_), channel_id=1, source_target_pairs={{0,4},{1,5},{2,6},{3,7},{4,0},{5,1},{6,2},{7,3},{8,12},{9,13},{10,... | collective-permute-start | bytes 196616 | tf_op jit(solution)/shard_map/ppermute | solution.py:382
  14.9 0.0 collective-permute-start.4
  14.9 0.6 %collective-permute-start.5 = (bf16[256,128]{1,0:T(8,128)(2,1)S(1)}, bf16[256,128]{1,0:T(8,128)(2,1)S(1)}, u32[]{:S(2)}, u32[]{:S(2)}) collective-permute-start(bf16[256,128]{1,0:T(8,128)(2,1)S(1)} %pad_maximum_fusion.1.refs_0_.refs_3_), channel_id=1, source_target_pairs={{0,2},{1,3},{2,0},{3,1},{4,6},{5,7},{6,4},{7,5},{8,10},{9,11},{10,... | collective-permute-start | bytes 196616 | tf_op jit(solution)/shard_map/ppermute | solution.py:382
  15.5 1.6 %collective-permute-start.11 = (bf16[1024,128]{1,0:T(8,128)(2,1)S(1)}, bf16[1024,128]{1,0:T(8,128)(2,1)S(1)}, u32[]{:S(2)}, u32[]{:S(2)}) collective-permute-start(bf16[1024,128]{1,0:T(8,128)(2,1)S(1)} %get-tuple-element.92), channel_id=1, source_target_pairs={{0,4},{1,5},{2,6},{3,7},{4,0},{5,1},{6,2},{7,3},{8,12},{9,13},{10,... | collective-permute-start | bytes 786440 | tf_op jit(solution)/shard_map/ppermute | solution.py:382
  17.1 1.8 %boundary.1.refs_9_.refs_3_ = f32[4,64,128]{2,1,0:T(8,128)S(1)} custom-call(bf16[256,128]{1,0:T(8,128)(2,1)S(1)} %pad_maximum_fusion.1.refs_0_.refs_3_, bf16[64,1536]{1,0:T(8,128)(2,1)S(1)} %get-tuple-element.61.refs_1_.refs_0_, bf16[4,7,128,128]{3,2,1,0:T(8,128)(2,1)S(1)} %get-tuple-element.62.refs_2_, ...), custom_call_target="tpu_custom_call" | custom-call | flops 75497472 | bytes 1048576 | tf_op jit(solution)/shard_map/boundary/pallas_call | solution.py:471
  19.0 0.0 collective-permute-done.3.refs_0_
  19.0 0.0 collective-permute-done.4.refs_1_
  19.0 0.0 collective-permute-done.5.refs_2_
  19.0 0.3 integral.1
  19.3 0.0 copy-start
  19.4 1.6 %collective-permute-start.7 = (bf16[128,128]{1,0:T(8,128)(2,1)S(1)}, bf16[128,128]{1,0:T(8,128)(2,1)S(1)}, u32[]{:S(2)}, u32[]{:S(2)}) collective-permute-start(bf16[128,128]{1,0:T(8,128)(2,1)S(1)} %get-tuple-element.69), channel_id=1, source_target_pairs={{0,1},{1,0},{2,3},{3,2},{4,5},{5,4},{6,7},{7,6},{8,9},{9,8},{10,11... | collective-permute-start | bytes 98312 | tf_op jit(solution)/shard_map/ppermute | solution.py:371
  20.9 0.7 %collective-permute-start.12 = (bf16[1024,128]{1,0:T(8,128)(2,1)S(1)}, bf16[1024,128]{1,0:T(8,128)(2,1)S(1)}, u32[]{:S(2)}, u32[]{:S(2)}) collective-permute-start(bf16[1024,128]{1,0:T(8,128)(2,1)S(1)} %get-tuple-element.79), channel_id=1, source_target_pairs={{0,5},{1,4},{2,7},{3,6},{4,1},{5,0},{6,3},{7,2},{8,13},{9,12},{10,... | collective-permute-start | bytes 786440 | tf_op jit(solution)/shard_map/ppermute | solution.py:382
  21.6 1.7 %collective-permute-done.7.refs_5_ = bf16[128,128]{1,0:T(8,128)(2,1)S(1)} collective-permute-done((bf16[128,128]{1,0:T(8,128)(2,1)S(1)}, bf16[128,128]{1,0:T(8,128)(2,1)S(1)}, u32[]{:S(2)}, u32[]{:S(2)}) %collective-permute-start.7) | collective-permute-done | bytes 32800 | tf_op jit(solution)/shard_map/ppermute | solution.py:371
  23.3 0.0 collective-permute-done.6.refs_4_.refs_3_
  23.3 0.2 step.1
  23.6 1.0 %collective-permute-start.10 = (bf16[192,128]{1,0:T(8,128)(2,1)S(1)}, bf16[192,128]{1,0:T(8,128)(2,1)S(1)}, u32[]{:S(2)}, u32[]{:S(2)}) collective-permute-start(bf16[192,128]{1,0:T(8,128)(2,1)S(1)} %get-tuple-element.75), channel_id=1, source_target_pairs={{0,16},{8,24},{16,0},{24,8},{1,17},{9,25},{17,1},{25,9},{2,18},{10... | collective-permute-start | bytes 147464 | tf_op jit(solution)/shard_map/ppermute | solution.py:371
  24.6 2.8 %collective-permute-start.8 = (bf16[192,128]{1,0:T(8,128)(2,1)S(1)}, bf16[192,128]{1,0:T(8,128)(2,1)S(1)}, u32[]{:S(2)}, u32[]{:S(2)}) collective-permute-start(bf16[192,128]{1,0:T(8,128)(2,1)S(1)} %get-tuple-element.73), channel_id=1, source_target_pairs={{0,8},{8,16},{16,24},{24,0},{1,9},{9,17},{17,25},{25,1},{2,10},{10... | collective-permute-start | bytes 147464 | tf_op jit(solution)/shard_map/ppermute | solution.py:371
  27.3 1.0 %collective-permute-start.9 = (bf16[192,128]{1,0:T(8,128)(2,1)S(1)}, bf16[192,128]{1,0:T(8,128)(2,1)S(1)}, u32[]{:S(2)}, u32[]{:S(2)}) collective-permute-start(bf16[192,128]{1,0:T(8,128)(2,1)S(1)} %get-tuple-element.74), channel_id=1, source_target_pairs={{0,24},{8,0},{16,8},{24,16},{1,25},{9,1},{17,9},{25,17},{2,26},{10... | collective-permute-start | bytes 147464 | tf_op jit(solution)/shard_map/ppermute | solution.py:371
  28.4 0.0 copy-done
  28.4 1.8 %base_volume.1 = (f32[64,1536]{1,0:T(8,128)S(1)}, bf16[1536,640]{1,0:T(8,128)(2,1)S(1)}) custom-call(bf16[64,1536]{1,0:T(8,128)(2,1)S(1)} %get-tuple-element.61.refs_1_.refs_0_, bf16[12,7,128,128]{3,2,1,0:T(8,128)(2,1)S(1)} %copy-done, s32[7,12]{1,0:T(8,128)S(1)} %get-tuple-element.64.refs_4_.refs_2_), custom_call_target="tpu_custom_call" | custom-call | flops 176160768 | bytes 2752512 | tf_op jit(solution)/shard_map/base_volume/pallas_call | solution.py:515
  30.2 0.0 collective-permute-done.11.refs_4_
  30.3 0.0 collective-permute-done.10.refs_7_
  30.3 0.2 collective-permute-done.8.refs_6_
  30.4 1.0 %collective-permute-done.9.refs_8_ = bf16[192,128]{1,0:T(8,128)(2,1)S(1)} collective-permute-done((bf16[192,128]{1,0:T(8,128)(2,1)S(1)}, bf16[192,128]{1,0:T(8,128)(2,1)S(1)}, u32[]{:S(2)}, u32[]{:S(2)}) %collective-permute-start.9) | collective-permute-done | bytes 49184 | tf_op jit(solution)/shard_map/ppermute | solution.py:371
  31.5 0.0 collective-permute-done.12.refs_5_
  31.5 0.1 collective-permute-start.13
  31.6 1.3 %collective-permute-done.13.refs_1_ = bf16[512,128]{1,0:T(8,128)(2,1)S(1)} collective-permute-done((bf16[512,128]{1,0:T(8,128)(2,1)S(1)}, bf16[512,128]{1,0:T(8,128)(2,1)S(1)}, u32[]{:S(2)}, u32[]{:S(2)}) %collective-permute-start.13) | collective-permute-done | bytes 131104 | tf_op jit(solution)/shard_map/ppermute | solution.py:382
  32.9 0.3 last_integral.1
  33.2 1.4 %collective-permute-start.14 = (bf16[64,128]{1,0:T(8,128)(2,1)S(1)}, bf16[64,128]{1,0:T(8,128)(2,1)S(1)}, u32[]{:S(2)}, u32[]{:S(2)}) collective-permute-start(bf16[64,128]{1,0:T(8,128)(2,1)S(1)} %get-tuple-element.91), channel_id=1, source_target_pairs={{0,4},{1,5},{2,6},{3,7},{4,0},{5,1},{6,2},{7,3},{8,12},{9,13},{10,... | collective-permute-start | bytes 49160 | tf_op jit(solution)/shard_map/ppermute | solution.py:382
  34.6 2.0 %volume.1 = f32[64,1536]{1,0:T(8,128)} custom-call(bf16[512,128]{1,0:T(8,128)(2,1)S(1)} %pad_maximum_fusion.refs_0_, bf16[4,128,128]{2,1,0:T(8,128)(2,1)S(1)} %get-tuple-element.63.refs_3_.refs_1_, s32[4]{0:T(128)S(1)} %get-tuple-element.65.refs_5_.refs_2_, s32[1]{0:T(128)S(6)} %copy.14.refs_0_.refs_6_.refs_3_, f32[64,1536]{1,0:T(8,128)S(1)} %get-tuple-element.84.refs_4_, ...), custom_call_target="tpu_custom_call" | custom-call | flops 109051904 | bytes 1703936 | tf_op jit(solution)/shard_map/volume/pallas_call | solution.py:543
  36.6 0.4 %collective-permute-done.14.refs_5_ = bf16[64,128]{1,0:T(8,128)(2,1)S(1)} collective-permute-done((bf16[64,128]{1,0:T(8,128)(2,1)S(1)}, bf16[64,128]{1,0:T(8,128)(2,1)S(1)}, u32[]{:S(2)}, u32[]{:S(2)}) %collective-permute-start.14) | collective-permute-done | bytes 16416 | tf_op jit(solution)/shard_map/ppermute | solution.py:382
  37.0 0.8 %last.1 = f32[64,128]{1,0:T(8,128)} custom-call(f32[64,128]{1,0:T(8,128)S(1)} %get-tuple-element.86.refs_0_, bf16[64,128]{1,0:T(8,128)(2,1)S(1)} %get-tuple-element.55.refs_4_.refs_1_, bf16[1,128,128]{2,1,0:T(8,128)(2,1)S(1)} %get-tuple-element.56.refs_5_.refs_2_, f32[64,128]{1,0:T(8,128)S(1)} %get-tuple-element.89.refs_3_, ...), custom_call_target="tpu_custom_call" | custom-call | flops 2097152 | bytes 131072 | tf_op jit(solution)/shard_map/last/pallas_call | solution.py:552
  (9 shorter events, 0.1 us)
Async XLA Ops:
  3.7 9.4 %collective-permute-start = (bf16[128,128]{1,0:T(8,128)(2,1)S(1)}, bf16[128,128]{1,0:T(8,128)(2,1)S(1)}, u32[]{:S(2)}, u32[]{:S(2)}) collective-permute-start(bf16[128,128]{1,0:T(8,128)(2,1)S(1)} %get-tuple-element.48), channel_id=1, source_target_pairs={{0,8},{8,16},{16,24},{24,0},{1,9},{9,17},{17,25},{25,1},{2,10},{10... | collective-permute-start | bytes 98312 | tf_op jit(solution)/shard_map/ppermute | solution.py:371
  6.8 6.4 %collective-permute-start.1 = (bf16[128,128]{1,0:T(8,128)(2,1)S(1)}, bf16[128,128]{1,0:T(8,128)(2,1)S(1)}, u32[]{:S(2)}, u32[]{:S(2)}) collective-permute-start(bf16[128,128]{1,0:T(8,128)(2,1)S(1)} %get-tuple-element.49), channel_id=1, source_target_pairs={{0,16},{8,24},{16,0},{24,8},{1,17},{9,25},{17,1},{25,9},{2,18},{10... | collective-permute-start | bytes 98312 | tf_op jit(solution)/shard_map/ppermute | solution.py:371
  9.4 3.9 %collective-permute-start.2 = (bf16[128,128]{1,0:T(8,128)(2,1)S(1)}, bf16[128,128]{1,0:T(8,128)(2,1)S(1)}, u32[]{:S(2)}, u32[]{:S(2)}) collective-permute-start(bf16[128,128]{1,0:T(8,128)(2,1)S(1)} %get-tuple-element.50), channel_id=1, source_target_pairs={{0,24},{8,0},{16,8},{24,16},{1,25},{9,1},{17,9},{25,17},{2,26},{10... | collective-permute-start | bytes 98312 | tf_op jit(solution)/shard_map/ppermute | solution.py:371
  11.6 11.8 %collective-permute-start.6 = (bf16[1216,128]{1,0:T(8,128)(2,1)S(1)}, bf16[1216,128]{1,0:T(8,128)(2,1)S(1)}, u32[]{:S(2)}, u32[]{:S(2)}) collective-permute-start(bf16[1216,128]{1,0:T(8,128)(2,1)S(1)} %get-tuple-element.68), channel_id=1, source_target_pairs={{0,1},{1,0},{2,3},{3,2},{4,5},{5,4},{6,7},{7,6},{8,9},{9,8},{10,11... | collective-permute-start | bytes 933896 | tf_op jit(solution)/shard_map/ppermute | solution.py:382
  13.3 5.7 %collective-permute-start.3 = (bf16[256,128]{1,0:T(8,128)(2,1)S(1)}, bf16[256,128]{1,0:T(8,128)(2,1)S(1)}, u32[]{:S(2)}, u32[]{:S(2)}) collective-permute-start(bf16[256,128]{1,0:T(8,128)(2,1)S(1)} %pad_maximum_fusion.1.refs_0_.refs_3_), channel_id=1, source_target_pairs={{0,4},{1,5},{2,6},{3,7},{4,0},{5,1},{6,2},{7,3},{8,12},{9,13},{10,... | collective-permute-start | bytes 196616 | tf_op jit(solution)/shard_map/ppermute | solution.py:382
  14.9 4.1 %collective-permute-start.4 = (bf16[256,128]{1,0:T(8,128)(2,1)S(1)}, bf16[256,128]{1,0:T(8,128)(2,1)S(1)}, u32[]{:S(2)}, u32[]{:S(2)}) collective-permute-start(bf16[256,128]{1,0:T(8,128)(2,1)S(1)} %pad_maximum_fusion.1.refs_0_.refs_3_), channel_id=1, source_target_pairs={{0,6},{1,7},{2,4},{3,5},{4,2},{5,3},{6,0},{7,1},{8,14},{9,15},{10,... | collective-permute-start | bytes 196616 | tf_op jit(solution)/shard_map/ppermute | solution.py:382
  14.9 4.1 %collective-permute-start.5 = (bf16[256,128]{1,0:T(8,128)(2,1)S(1)}, bf16[256,128]{1,0:T(8,128)(2,1)S(1)}, u32[]{:S(2)}, u32[]{:S(2)}) collective-permute-start(bf16[256,128]{1,0:T(8,128)(2,1)S(1)} %pad_maximum_fusion.1.refs_0_.refs_3_), channel_id=1, source_target_pairs={{0,2},{1,3},{2,0},{3,1},{4,6},{5,7},{6,4},{7,5},{8,10},{9,11},{10,... | collective-permute-start | bytes 196616 | tf_op jit(solution)/shard_map/ppermute | solution.py:382
  15.5 14.7 %collective-permute-start.11 = (bf16[1024,128]{1,0:T(8,128)(2,1)S(1)}, bf16[1024,128]{1,0:T(8,128)(2,1)S(1)}, u32[]{:S(2)}, u32[]{:S(2)}) collective-permute-start(bf16[1024,128]{1,0:T(8,128)(2,1)S(1)} %get-tuple-element.92), channel_id=1, source_target_pairs={{0,4},{1,5},{2,6},{3,7},{4,0},{5,1},{6,2},{7,3},{8,12},{9,13},{10,... | collective-permute-start | bytes 786440 | tf_op jit(solution)/shard_map/ppermute | solution.py:382
  19.3 9.0 %copy-start = (bf16[12,7,128,128]{3,2,1,0:T(8,128)(2,1)S(1)}, bf16[12,7,128,128]{3,2,1,0:T(8,128)(2,1)}, u32[]{:S(2)}) copy-start(bf16[12,7,128,128]{3,2,1,0:T(8,128)(2,1)} %refs_1_.2) | copy-start | bytes 8257540
  19.4 4.0 %collective-permute-start.7 = (bf16[128,128]{1,0:T(8,128)(2,1)S(1)}, bf16[128,128]{1,0:T(8,128)(2,1)S(1)}, u32[]{:S(2)}, u32[]{:S(2)}) collective-permute-start(bf16[128,128]{1,0:T(8,128)(2,1)S(1)} %get-tuple-element.69), channel_id=1, source_target_pairs={{0,1},{1,0},{2,3},{3,2},{4,5},{5,4},{6,7},{7,6},{8,9},{9,8},{10,11... | collective-permute-start | bytes 98312 | tf_op jit(solution)/shard_map/ppermute | solution.py:371
  20.9 10.6 %collective-permute-start.12 = (bf16[1024,128]{1,0:T(8,128)(2,1)S(1)}, bf16[1024,128]{1,0:T(8,128)(2,1)S(1)}, u32[]{:S(2)}, u32[]{:S(2)}) collective-permute-start(bf16[1024,128]{1,0:T(8,128)(2,1)S(1)} %get-tuple-element.79), channel_id=1, source_target_pairs={{0,5},{1,4},{2,7},{3,6},{4,1},{5,0},{6,3},{7,2},{8,13},{9,12},{10,... | collective-permute-start | bytes 786440 | tf_op jit(solution)/shard_map/ppermute | solution.py:382
  23.6 6.7 %collective-permute-start.10 = (bf16[192,128]{1,0:T(8,128)(2,1)S(1)}, bf16[192,128]{1,0:T(8,128)(2,1)S(1)}, u32[]{:S(2)}, u32[]{:S(2)}) collective-permute-start(bf16[192,128]{1,0:T(8,128)(2,1)S(1)} %get-tuple-element.75), channel_id=1, source_target_pairs={{0,16},{8,24},{16,0},{24,8},{1,17},{9,25},{17,1},{25,9},{2,18},{10... | collective-permute-start | bytes 147464 | tf_op jit(solution)/shard_map/ppermute | solution.py:371
  24.6 5.9 %collective-permute-start.8 = (bf16[192,128]{1,0:T(8,128)(2,1)S(1)}, bf16[192,128]{1,0:T(8,128)(2,1)S(1)}, u32[]{:S(2)}, u32[]{:S(2)}) collective-permute-start(bf16[192,128]{1,0:T(8,128)(2,1)S(1)} %get-tuple-element.73), channel_id=1, source_target_pairs={{0,8},{8,16},{16,24},{24,0},{1,9},{9,17},{17,25},{25,1},{2,10},{10... | collective-permute-start | bytes 147464 | tf_op jit(solution)/shard_map/ppermute | solution.py:371
  27.3 4.1 %collective-permute-start.9 = (bf16[192,128]{1,0:T(8,128)(2,1)S(1)}, bf16[192,128]{1,0:T(8,128)(2,1)S(1)}, u32[]{:S(2)}, u32[]{:S(2)}) collective-permute-start(bf16[192,128]{1,0:T(8,128)(2,1)S(1)} %get-tuple-element.74), channel_id=1, source_target_pairs={{0,24},{8,0},{16,8},{24,16},{1,25},{9,1},{17,9},{25,17},{2,26},{10... | collective-permute-start | bytes 147464 | tf_op jit(solution)/shard_map/ppermute | solution.py:371
  31.5 1.4 %collective-permute-start.13 = (bf16[512,128]{1,0:T(8,128)(2,1)S(1)}, bf16[512,128]{1,0:T(8,128)(2,1)S(1)}, u32[]{:S(2)}, u32[]{:S(2)}) collective-permute-start(bf16[512,128]{1,0:T(8,128)(2,1)S(1)} %pad_maximum_fusion.refs_0_), channel_id=1, source_target_pairs={{0,2},{1,3},{2,0},{3,1},{4,6},{5,7},{6,4},{7,5},{8,10},{9,11},{10,... | collective-permute-start | bytes 393224 | tf_op jit(solution)/shard_map/ppermute | solution.py:382
  33.2 3.8 %collective-permute-start.14 = (bf16[64,128]{1,0:T(8,128)(2,1)S(1)}, bf16[64,128]{1,0:T(8,128)(2,1)S(1)}, u32[]{:S(2)}, u32[]{:S(2)}) collective-permute-start(bf16[64,128]{1,0:T(8,128)(2,1)S(1)} %get-tuple-element.91), channel_id=1, source_target_pairs={{0,4},{1,5},{2,6},{3,7},{4,0},{5,1},{6,2},{7,3},{8,12},{9,13},{10,... | collective-permute-start | bytes 49160 | tf_op jit(solution)/shard_map/ppermute | solution.py:382

commit v8 on v5

--- a/solution.py
+++ b/solution.py
@@ -209,12 +209,8 @@
                 near = near_blocks[b, 0, n].astype(F32).T
                 dense[where] = (dense[where].astype(F32) + near).astype(HALF)
     width = subs * bs
-    for a in range(chips):
-        for k in range(col_size):
-            if a or k:
-                messages[a * col_size + k - 1][0:part, :] = dense[
-                    a * part : (a + 1) * part, k * width : (k + 1) * width
-                ]
+    for k in range(1, col_size):
+        messages[k - 1][0:part, :] = dense[0:part, k * width : (k + 1) * width]
     angles = surf_rhs.shape[0]
     for k in range(1, col_size):
         message = messages[k - 1]
@@ -436,7 +432,7 @@
         "dense",
         [VMEM] * 6,
         [shape((nv * nr * width, nc * width), HALF)]
-        + [shape((size, width), HALF) for size in sizes[1:]],
+        + [shape((size, width), HALF) for size in sizes[1:nc]],
         product * nv * nr * nc,
         4 * nv * nr * nc * bs * bs,
         [
@@ -444,6 +440,11 @@
             pltpu.SemaphoreType.DMA((1,)),
         ],
     )(*kept)
+
+    messages += [
+        dense[i // nc * part : (i // nc + 1) * part, i % nc * width : (i % nc + 1) * width]
+        for i in range(nc, nc * chips)
+    ]
 
     received = [shifted(payloads[k - 1], "vol", k) for k in range(1, nv)]
     blocks = [

time: 37.9 us -> 37.9 us (level)
  transfers between devices with their start and end apart: 15 -> 15, of which waited for: 7 -> 8; matrix products, arithmetic and copies ran while one was open for 0% -> 0% of each run, Pallas kernels for 18% -> 17%
where the time goes in v8:
time: 37.9 us; the launch traced here: 37.8 us
  starting transfers between devices  20 us (53%)
  Pallas kernels  10.1 us (27%)
  waiting for transfers between devices  6.14 us (16%)
  between operations  1.43 us (4%)
    ppermute x7, starting transfers between devices, shifted(): lax.ppermute(value, axis, [(i, (i + shift) % size) for i in range(size)])  12.5 us
    ppermute x8, starting transfers between devices, shifted_in_plane(): return lax.ppermute(value, ('row', 'col'), pairs)  7.56 us
    ppermute x8, waiting for transfers between devices, shifted_in_plane(): return lax.ppermute(value, ('row', 'col'), pairs)  3.19 us
    ppermute x7, waiting for transfers between devices, shifted(): lax.ppermute(value, axis, [(i, (i + shift) % size) for i in range(size)])  2.95 us
    pallas_call x1, Pallas kernels, local(): call(functools.partial(start_kernel, 'vol', len(start_shapes), len(kept))...  2.41 us
    pallas_call x1, Pallas kernels, local(): call(late_kernel, 'late_volume', [VMEM] * 4, [shape((angles, vol_count *...  2.15 us
    pallas_call x1, Pallas kernels, local(): call(functools.partial(boundary_kernel, 'vol'), 'boundary', [VMEM] * 6 +...  1.83 us
    pallas_call x1, Pallas kernels, local(): call(functools.partial(early_kernel, 'vol', nv, nc), 'early_volume', [VME...  1.26 us
  transfers between devices with their start and end apart: 15, of which 8 were waited for; matrix products, arithmetic and copies ran while one was open for 0% of the time, Pallas kernels for 17%

profile of v8, /device:TPU:0, one launch (start us, length us, event | category | flops | bytes accessed | tf_op | source)
XLA Modules:
  0.0 37.8 jit_solution(12308368683452400867)
XLA Ops:
  1.3 2.4 %start.1 = (bf16[64,128]{1,0:T(8,128)(2,1)S(1)}, f32[64,128]{1,0:T(8,128)S(1)}, bf16[128,128]{1,0:T(8,128)(2,1)S(1)}, bf16[128,128]{1,0:T(8,128)(2,1)S(1)}, bf16...) custom-call(s32[1]{0:T(128)S(6)} %copy.14.refs_0_.refs_6_, ...), custom_call_target="tpu_custom_call" | custom-call | flops 67108864 | bytes 1048576 | tf_op jit(solution)/shard_map/start/pallas_call | solution.py:405
  3.7 3.1 %collective-permute-start = (bf16[128,128]{1,0:T(8,128)(2,1)S(1)}, bf16[128,128]{1,0:T(8,128)(2,1)S(1)}, u32[]{:S(2)}, u32[]{:S(2)}) collective-permute-start(bf16[128,128]{1,0:T(8,128)(2,1)S(1)} %get-tuple-element.44), channel_id=1, source_target_pairs={{0,8},{8,16},{16,24},{24,0},{1,9},{9,17},{17,25},{25,1},{2,10},{10... | collective-permute-start | bytes 98312 | tf_op jit(solution)/shard_map/ppermute | solution.py:358
  6.8 2.6 %collective-permute-start.1 = (bf16[128,128]{1,0:T(8,128)(2,1)S(1)}, bf16[128,128]{1,0:T(8,128)(2,1)S(1)}, u32[]{:S(2)}, u32[]{:S(2)}) collective-permute-start(bf16[128,128]{1,0:T(8,128)(2,1)S(1)} %get-tuple-element.45), channel_id=1, source_target_pairs={{0,16},{8,24},{16,0},{24,8},{1,17},{9,25},{17,1},{25,9},{2,18},{10... | collective-permute-start | bytes 98312 | tf_op jit(solution)/shard_map/ppermute | solution.py:358
  9.4 1.3 %collective-permute-start.2 = (bf16[128,128]{1,0:T(8,128)(2,1)S(1)}, bf16[128,128]{1,0:T(8,128)(2,1)S(1)}, u32[]{:S(2)}, u32[]{:S(2)}) collective-permute-start(bf16[128,128]{1,0:T(8,128)(2,1)S(1)} %get-tuple-element.46), channel_id=1, source_target_pairs={{0,24},{8,0},{16,8},{24,16},{1,25},{9,1},{17,9},{25,17},{2,26},{10... | collective-permute-start | bytes 98312 | tf_op jit(solution)/shard_map/ppermute | solution.py:358
  10.7 0.9 %dense.1 = (bf16[2048,256]{1,0:T(8,128)(2,1)S(1)}, bf16[1216,128]{1,0:T(8,128)(2,1)S(1)}) custom-call(bf16[2,1,4,128,128]{4,3,2,1,0:T(8,128)(2,1)S(1)} %get-tuple-element.47.refs_0_, s32[2,1,4]{2,1,0:T(1,128)S(1)} %get-tuple-element.48.refs_1_, bf16[1,32,256]{2,1,0:T(8,128)(2,1)S(1)} %get-tuple-element.49.refs_2_, ...), custom_call_target="tpu_custom_call" | custom-call | flops 67108864 | bytes 2097152 | tf_op jit(solution)/shard_map/dense/pallas_call | solution.py:430
  11.6 1.6 %collective-permute-start.6 = (bf16[1216,128]{1,0:T(8,128)(2,1)S(1)}, bf16[1216,128]{1,0:T(8,128)(2,1)S(1)}, u32[]{:S(2)}, u32[]{:S(2)}) collective-permute-start(bf16[1216,128]{1,0:T(8,128)(2,1)S(1)} %get-tuple-element.64), channel_id=1, source_target_pairs={{0,1},{1,0},{2,3},{3,2},{4,5},{5,4},{6,7},{7,6},{8,9},{9,8},{10,11... | collective-permute-start | bytes 933896 | tf_op jit(solution)/shard_map/ppermute | solution.py:369
  13.1 0.0 collective-permute-done.refs_6_
  13.1 0.0 collective-permute-done.1.refs_7_
  13.2 0.1 collective-permute-done.2.refs_8_
  13.3 1.6 %collective-permute-start.3 = (bf16[256,128]{1,0:T(8,128)(2,1)S(1)}, bf16[256,128]{1,0:T(8,128)(2,1)S(1)}, u32[]{:S(2)}, u32[]{:S(2)}) collective-permute-start(bf16[256,128]{1,0:T(8,128)(2,1)S(1)} %pad_maximum_fusion.1.refs_0_.refs_3_), channel_id=1, source_target_pairs={{0,4},{1,5},{2,6},{3,7},{4,0},{5,1},{6,2},{7,3},{8,12},{9,13},{10,... | collective-permute-start | bytes 196616 | tf_op jit(solution)/shard_map/ppermute | solution.py:369
  14.9 0.0 collective-permute-start.4
  14.9 0.6 %collective-permute-start.5 = (bf16[256,128]{1,0:T(8,128)(2,1)S(1)}, bf16[256,128]{1,0:T(8,128)(2,1)S(1)}, u32[]{:S(2)}, u32[]{:S(2)}) collective-permute-start(bf16[256,128]{1,0:T(8,128)(2,1)S(1)} %pad_maximum_fusion.1.refs_0_.refs_3_), channel_id=1, source_target_pairs={{0,2},{1,3},{2,0},{3,1},{4,6},{5,7},{6,4},{7,5},{8,10},{9,11},{10,... | collective-permute-start | bytes 196616 | tf_op jit(solution)/shard_map/ppermute | solution.py:369
  15.5 1.6 %collective-permute-start.11 = (bf16[1024,128]{1,0:T(8,128)(2,1)S(1)}, bf16[1024,128]{1,0:T(8,128)(2,1)S(1)}, u32[]{:S(2)}, u32[]{:S(2)}) collective-permute-start(bf16[1024,128]{1,0:T(8,128)(2,1)S(1)} %get-tuple-element.84), channel_id=1, source_target_pairs={{0,4},{1,5},{2,6},{3,7},{4,0},{5,1},{6,2},{7,3},{8,12},{9,13},{10,... | collective-permute-start | bytes 786440 | tf_op jit(solution)/shard_map/ppermute | solution.py:369
  17.1 1.8 %boundary.1.refs_9_.refs_3_ = f32[4,64,128]{2,1,0:T(8,128)S(1)} custom-call(bf16[256,128]{1,0:T(8,128)(2,1)S(1)} %pad_maximum_fusion.1.refs_0_.refs_3_, bf16[64,1536]{1,0:T(8,128)(2,1)S(1)} %get-tuple-element.57.refs_1_, bf16[4,7,128,128]{3,2,1,0:T(8,128)(2,1)S(1)} %get-tuple-element.58.refs_2_, bf16[4,128,128]{2,1,0:T(8,128)(2,1)S(1)} %get-tuple-element.59.refs_3_, ...), custom_call_target="tpu_custom_call" | custom-call | flops 75497472 | bytes 1048576 | tf_op jit(solution)/shard_map/boundary/pallas_call | solution.py:458
  19.0 0.0 collective-permute-done.3.refs_0_
  19.0 0.1 collective-permute-done.4.refs_1_
  19.0 0.0 collective-permute-done.5.refs_2_
  19.0 0.3 integral.1
  19.3 0.0 copy-start
  19.4 1.6 %collective-permute-start.7 = (bf16[128,128]{1,0:T(8,128)(2,1)S(1)}, bf16[128,128]{1,0:T(8,128)(2,1)S(1)}, u32[]{:S(2)}, u32[]{:S(2)}) collective-permute-start(bf16[128,128]{1,0:T(8,128)(2,1)S(1)} %get-tuple-element.65), channel_id=1, source_target_pairs={{0,1},{1,0},{2,3},{3,2},{4,5},{5,4},{6,7},{7,6},{8,9},{9,8},{10,11... | collective-permute-start | bytes 98312 | tf_op jit(solution)/shard_map/ppermute | solution.py:358
  20.9 0.8 %collective-permute-start.12 = (bf16[1024,128]{1,0:T(8,128)(2,1)S(1)}, bf16[1024,128]{1,0:T(8,128)(2,1)S(1)}, u32[]{:S(2)}, u32[]{:S(2)}) collective-permute-start(bf16[1024,128]{1,0:T(8,128)(2,1)S(1)} %get-tuple-element.73), channel_id=1, source_target_pairs={{0,5},{1,4},{2,7},{3,6},{4,1},{5,0},{6,3},{7,2},{8,13},{9,12},{10,... | collective-permute-start | bytes 786440 | tf_op jit(solution)/shard_map/ppermute | solution.py:369
  21.7 1.7 %collective-permute-done.7.refs_5_ = bf16[128,128]{1,0:T(8,128)(2,1)S(1)} collective-permute-done((bf16[128,128]{1,0:T(8,128)(2,1)S(1)}, bf16[128,128]{1,0:T(8,128)(2,1)S(1)}, u32[]{:S(2)}, u32[]{:S(2)}) %collective-permute-start.7) | collective-permute-done | bytes 32800 | tf_op jit(solution)/shard_map/ppermute | solution.py:358
  23.3 0.0 collective-permute-done.6.refs_4_.refs_3_
  23.3 0.2 step.1
  23.6 0.6 %collective-permute-start.10 = (bf16[192,128]{1,0:T(8,128)(2,1)S(1)}, bf16[192,128]{1,0:T(8,128)(2,1)S(1)}, u32[]{:S(2)}, u32[]{:S(2)}) collective-permute-start(bf16[192,128]{1,0:T(8,128)(2,1)S(1)} %get-tuple-element.69), channel_id=1, source_target_pairs={{0,8},{8,16},{16,24},{24,0},{1,9},{9,17},{17,25},{25,1},{2,10},{10... | collective-permute-start | bytes 147464 | tf_op jit(solution)/shard_map/ppermute | solution.py:358
  24.2 3.1 %collective-permute-start.8 = (bf16[192,128]{1,0:T(8,128)(2,1)S(1)}, bf16[192,128]{1,0:T(8,128)(2,1)S(1)}, u32[]{:S(2)}, u32[]{:S(2)}) collective-permute-start(bf16[192,128]{1,0:T(8,128)(2,1)S(1)} %get-tuple-element.67), channel_id=1, source_target_pairs={{0,16},{8,24},{16,0},{24,8},{1,17},{9,25},{17,1},{25,9},{2,18},{10... | collective-permute-start | bytes 147464 | tf_op jit(solution)/shard_map/ppermute | solution.py:358
  27.3 0.1 collective-permute-start.9
  27.5 2.8 %collective-permute-done.11.refs_4_ = bf16[1024,128]{1,0:T(8,128)(2,1)S(1)} collective-permute-done((bf16[1024,128]{1,0:T(8,128)(2,1)S(1)}, bf16[1024,128]{1,0:T(8,128)(2,1)S(1)}, u32[]{:S(2)}, u32[]{:S(2)}) %collective-permute-start.11) | collective-permute-done | bytes 262176 | tf_op jit(solution)/shard_map/ppermute | solution.py:369
  30.3 0.0 collective-permute-done.10.refs_6_
  30.3 0.6 %collective-permute-done.8.refs_7_ = bf16[192,128]{1,0:T(8,128)(2,1)S(1)} collective-permute-done((bf16[192,128]{1,0:T(8,128)(2,1)S(1)}, bf16[192,128]{1,0:T(8,128)(2,1)S(1)}, u32[]{:S(2)}, u32[]{:S(2)}) %collective-permute-start.8) | collective-permute-done | bytes 49184 | tf_op jit(solution)/shard_map/ppermute | solution.py:358
  30.9 0.5 %collective-permute-done.9.refs_8_ = bf16[192,128]{1,0:T(8,128)(2,1)S(1)} collective-permute-done((bf16[192,128]{1,0:T(8,128)(2,1)S(1)}, bf16[192,128]{1,0:T(8,128)(2,1)S(1)}, u32[]{:S(2)}, u32[]{:S(2)}) %collective-permute-start.9) | collective-permute-done | bytes 49184 | tf_op jit(solution)/shard_map/ppermute | solution.py:358
  31.4 0.0 collective-permute-done.12.refs_5_
  31.5 0.1 collective-permute-start.13
  31.5 0.0 copy-done
  31.5 1.3 %early_volume.1 = (f32[64,512]{1,0:T(8,128)S(1)}, bf16[12,64,128]{2,1,0:T(8,128)(2,1)S(1)}) custom-call(bf16[512,128]{1,0:T(8,128)(2,1)S(1)} %pad_maximum_fusion.refs_0_, bf16[64,1536]{1,0:T(8,128)(2,1)S(1)} %get-tuple-element.57.refs_1_, bf16[12,7,128,128]{3,2,1,0:T(8,128)(2,1)S(1)} %copy-done, bf16[4,128,128]{2,1,0:T(8,128)(2,1)S(1)} %get-tuple-element.59.refs_3_, ...), custom_call_target="tpu_custom_call" | custom-call | flops 58720256 | bytes 917504 | tf_op jit(solution)/shard_map/early_volume/pallas_call | solution.py:508
  32.8 0.1 collective-permute-done.13.refs_1_
  32.9 0.3 last_integral.1
  33.2 1.4 %collective-permute-start.14 = (bf16[64,128]{1,0:T(8,128)(2,1)S(1)}, bf16[64,128]{1,0:T(8,128)(2,1)S(1)}, u32[]{:S(2)}, u32[]{:S(2)}) collective-permute-start(bf16[64,128]{1,0:T(8,128)(2,1)S(1)} %get-tuple-element.83), channel_id=1, source_target_pairs={{0,4},{1,5},{2,6},{3,7},{4,0},{5,1},{6,2},{7,3},{8,12},{9,13},{10,... | collective-permute-start | bytes 49160 | tf_op jit(solution)/shard_map/ppermute | solution.py:369
  34.6 2.1 %late_volume.1 = f32[64,1536]{1,0:T(8,128)} custom-call(f32[64,512]{1,0:T(8,128)S(1)} %get-tuple-element.76.refs_0_.refs_6_, bf16[12,64,128]{2,1,0:T(8,128)(2,1)S(1)} %get-tuple-element.77.refs_1_, bf16[12,7,128,128]{3,2,1,0:T(8,128)(2,1)S(1)} %copy-done, s32[7,12]{1,0:T(8,128)S(1)} %get-tuple-element.60.refs_4_.refs_3_), custom_call_target="tpu_custom_call" | custom-call | flops 117440512 | bytes 1835008 | tf_op jit(solution)/shard_map/late_volume/pallas_call | solution.py:526
  36.7 0.3 collective-permute-done.14.refs_5_
  37.0 0.8 %last.1 = f32[64,128]{1,0:T(8,128)} custom-call(f32[64,128]{1,0:T(8,128)S(1)} %get-tuple-element.78.refs_0_, bf16[64,128]{1,0:T(8,128)(2,1)S(1)} %get-tuple-element.51.refs_4_.refs_1_, bf16[1,128,128]{2,1,0:T(8,128)(2,1)S(1)} %get-tuple-element.52.refs_5_.refs_2_, f32[64,128]{1,0:T(8,128)S(1)} %get-tuple-element.81.refs_3_, ...), custom_call_target="tpu_custom_call" | custom-call | flops 2097152 | bytes 131072 | tf_op jit(solution)/shard_map/last/pallas_call | solution.py:535
  (9 shorter events, 0.1 us)
Async XLA Ops:
  3.7 9.4 %collective-permute-start = (bf16[128,128]{1,0:T(8,128)(2,1)S(1)}, bf16[128,128]{1,0:T(8,128)(2,1)S(1)}, u32[]{:S(2)}, u32[]{:S(2)}) collective-permute-start(bf16[128,128]{1,0:T(8,128)(2,1)S(1)} %get-tuple-element.44), channel_id=1, source_target_pairs={{0,8},{8,16},{16,24},{24,0},{1,9},{9,17},{17,25},{25,1},{2,10},{10... | collective-permute-start | bytes 98312 | tf_op jit(solution)/shard_map/ppermute | solution.py:358
  6.8 6.4 %collective-permute-start.1 = (bf16[128,128]{1,0:T(8,128)(2,1)S(1)}, bf16[128,128]{1,0:T(8,128)(2,1)S(1)}, u32[]{:S(2)}, u32[]{:S(2)}) collective-permute-start(bf16[128,128]{1,0:T(8,128)(2,1)S(1)} %get-tuple-element.45), channel_id=1, source_target_pairs={{0,16},{8,24},{16,0},{24,8},{1,17},{9,25},{17,1},{25,9},{2,18},{10... | collective-permute-start | bytes 98312 | tf_op jit(solution)/shard_map/ppermute | solution.py:358
  9.4 3.9 %collective-permute-start.2 = (bf16[128,128]{1,0:T(8,128)(2,1)S(1)}, bf16[128,128]{1,0:T(8,128)(2,1)S(1)}, u32[]{:S(2)}, u32[]{:S(2)}) collective-permute-start(bf16[128,128]{1,0:T(8,128)(2,1)S(1)} %get-tuple-element.46), channel_id=1, source_target_pairs={{0,24},{8,0},{16,8},{24,16},{1,25},{9,1},{17,9},{25,17},{2,26},{10... | collective-permute-start | bytes 98312 | tf_op jit(solution)/shard_map/ppermute | solution.py:358
  11.6 11.8 %collective-permute-start.6 = (bf16[1216,128]{1,0:T(8,128)(2,1)S(1)}, bf16[1216,128]{1,0:T(8,128)(2,1)S(1)}, u32[]{:S(2)}, u32[]{:S(2)}) collective-permute-start(bf16[1216,128]{1,0:T(8,128)(2,1)S(1)} %get-tuple-element.64), channel_id=1, source_target_pairs={{0,1},{1,0},{2,3},{3,2},{4,5},{5,4},{6,7},{7,6},{8,9},{9,8},{10,11... | collective-permute-start | bytes 933896 | tf_op jit(solution)/shard_map/ppermute | solution.py:369
  13.3 5.7 %collective-permute-start.3 = (bf16[256,128]{1,0:T(8,128)(2,1)S(1)}, bf16[256,128]{1,0:T(8,128)(2,1)S(1)}, u32[]{:S(2)}, u32[]{:S(2)}) collective-permute-start(bf16[256,128]{1,0:T(8,128)(2,1)S(1)} %pad_maximum_fusion.1.refs_0_.refs_3_), channel_id=1, source_target_pairs={{0,4},{1,5},{2,6},{3,7},{4,0},{5,1},{6,2},{7,3},{8,12},{9,13},{10,... | collective-permute-start | bytes 196616 | tf_op jit(solution)/shard_map/ppermute | solution.py:369
  14.9 4.2 %collective-permute-start.4 = (bf16[256,128]{1,0:T(8,128)(2,1)S(1)}, bf16[256,128]{1,0:T(8,128)(2,1)S(1)}, u32[]{:S(2)}, u32[]{:S(2)}) collective-permute-start(bf16[256,128]{1,0:T(8,128)(2,1)S(1)} %pad_maximum_fusion.1.refs_0_.refs_3_), channel_id=1, source_target_pairs={{0,6},{1,7},{2,4},{3,5},{4,2},{5,3},{6,0},{7,1},{8,14},{9,15},{10,... | collective-permute-start | bytes 196616 | tf_op jit(solution)/shard_map/ppermute | solution.py:369
  14.9 4.2 %collective-permute-start.5 = (bf16[256,128]{1,0:T(8,128)(2,1)S(1)}, bf16[256,128]{1,0:T(8,128)(2,1)S(1)}, u32[]{:S(2)}, u32[]{:S(2)}) collective-permute-start(bf16[256,128]{1,0:T(8,128)(2,1)S(1)} %pad_maximum_fusion.1.refs_0_.refs_3_), channel_id=1, source_target_pairs={{0,2},{1,3},{2,0},{3,1},{4,6},{5,7},{6,4},{7,5},{8,10},{9,11},{10,... | collective-permute-start | bytes 196616 | tf_op jit(solution)/shard_map/ppermute | solution.py:369
  15.5 14.7 %collective-permute-start.11 = (bf16[1024,128]{1,0:T(8,128)(2,1)S(1)}, bf16[1024,128]{1,0:T(8,128)(2,1)S(1)}, u32[]{:S(2)}, u32[]{:S(2)}) collective-permute-start(bf16[1024,128]{1,0:T(8,128)(2,1)S(1)} %get-tuple-element.84), channel_id=1, source_target_pairs={{0,4},{1,5},{2,6},{3,7},{4,0},{5,1},{6,2},{7,3},{8,12},{9,13},{10,... | collective-permute-start | bytes 786440 | tf_op jit(solution)/shard_map/ppermute | solution.py:369
  19.3 12.2 %copy-start = (bf16[12,7,128,128]{3,2,1,0:T(8,128)(2,1)S(1)}, bf16[12,7,128,128]{3,2,1,0:T(8,128)(2,1)}, u32[]{:S(2)}) copy-start(bf16[12,7,128,128]{3,2,1,0:T(8,128)(2,1)} %refs_2_.3) | copy-start | bytes 8257540
  19.4 4.0 %collective-permute-start.7 = (bf16[128,128]{1,0:T(8,128)(2,1)S(1)}, bf16[128,128]{1,0:T(8,128)(2,1)S(1)}, u32[]{:S(2)}, u32[]{:S(2)}) collective-permute-start(bf16[128,128]{1,0:T(8,128)(2,1)S(1)} %get-tuple-element.65), channel_id=1, source_target_pairs={{0,1},{1,0},{2,3},{3,2},{4,5},{5,4},{6,7},{7,6},{8,9},{9,8},{10,11... | collective-permute-start | bytes 98312 | tf_op jit(solution)/shard_map/ppermute | solution.py:358
  20.9 10.5 %collective-permute-start.12 = (bf16[1024,128]{1,0:T(8,128)(2,1)S(1)}, bf16[1024,128]{1,0:T(8,128)(2,1)S(1)}, u32[]{:S(2)}, u32[]{:S(2)}) collective-permute-start(bf16[1024,128]{1,0:T(8,128)(2,1)S(1)} %get-tuple-element.73), channel_id=1, source_target_pairs={{0,5},{1,4},{2,7},{3,6},{4,1},{5,0},{6,3},{7,2},{8,13},{9,12},{10,... | collective-permute-start | bytes 786440 | tf_op jit(solution)/shard_map/ppermute | solution.py:369
  23.6 6.7 %collective-permute-start.10 = (bf16[192,128]{1,0:T(8,128)(2,1)S(1)}, bf16[192,128]{1,0:T(8,128)(2,1)S(1)}, u32[]{:S(2)}, u32[]{:S(2)}) collective-permute-start(bf16[192,128]{1,0:T(8,128)(2,1)S(1)} %get-tuple-element.69), channel_id=1, source_target_pairs={{0,8},{8,16},{16,24},{24,0},{1,9},{9,17},{17,25},{25,1},{2,10},{10... | collective-permute-start | bytes 147464 | tf_op jit(solution)/shard_map/ppermute | solution.py:358
  24.2 6.7 %collective-permute-start.8 = (bf16[192,128]{1,0:T(8,128)(2,1)S(1)}, bf16[192,128]{1,0:T(8,128)(2,1)S(1)}, u32[]{:S(2)}, u32[]{:S(2)}) collective-permute-start(bf16[192,128]{1,0:T(8,128)(2,1)S(1)} %get-tuple-element.67), channel_id=1, source_target_pairs={{0,16},{8,24},{16,0},{24,8},{1,17},{9,25},{17,1},{25,9},{2,18},{10... | collective-permute-start | bytes 147464 | tf_op jit(solution)/shard_map/ppermute | solution.py:358
  27.3 4.1 %collective-permute-start.9 = (bf16[192,128]{1,0:T(8,128)(2,1)S(1)}, bf16[192,128]{1,0:T(8,128)(2,1)S(1)}, u32[]{:S(2)}, u32[]{:S(2)}) collective-permute-start(bf16[192,128]{1,0:T(8,128)(2,1)S(1)} %get-tuple-element.68), channel_id=1, source_target_pairs={{0,24},{8,0},{16,8},{24,16},{1,25},{9,1},{17,9},{25,17},{2,26},{10... | collective-permute-start | bytes 147464 | tf_op jit(solution)/shard_map/ppermute | solution.py:358
  31.5 1.4 %collective-permute-start.13 = (bf16[512,128]{1,0:T(8,128)(2,1)S(1)}, bf16[512,128]{1,0:T(8,128)(2,1)S(1)}, u32[]{:S(2)}, u32[]{:S(2)}) collective-permute-start(bf16[512,128]{1,0:T(8,128)(2,1)S(1)} %pad_maximum_fusion.refs_0_), channel_id=1, source_target_pairs={{0,2},{1,3},{2,0},{3,1},{4,6},{5,7},{6,4},{7,5},{8,10},{9,11},{10,... | collective-permute-start | bytes 393224 | tf_op jit(solution)/shard_map/ppermute | solution.py:369
  33.2 3.8 %collective-permute-start.14 = (bf16[64,128]{1,0:T(8,128)(2,1)S(1)}, bf16[64,128]{1,0:T(8,128)(2,1)S(1)}, u32[]{:S(2)}, u32[]{:S(2)}) collective-permute-start(bf16[64,128]{1,0:T(8,128)(2,1)S(1)} %get-tuple-element.83), channel_id=1, source_target_pairs={{0,4},{1,5},{2,6},{3,7},{4,0},{5,1},{6,2},{7,3},{8,12},{9,13},{10,... | collective-permute-start | bytes 49160 | tf_op jit(solution)/shard_map/ppermute | solution.py:369
